TPU v7x, 32 devices: a whole 2x2x4 slice. The times are simulated.
32 devices in a mesh: fsdp: 16 (over z, y, core), tensor: 2 (over x).
Axes of the slice: x: 2, y: 2, z: 4, core: 2. Of those that a mesh axis runs over, the one named last changes fastest.
Arguments:
- tokens: bfloat16 [4096, 2048], P('fsdp'), may hold values from -6 to 6
- head_bucket: int32 [4096], P('fsdp'), may hold values from 0 to 3
- ffn_bucket: int32 [4096], P('fsdp'), may hold values from 0 to 3
- lengths: int32 [16, 2], P('fsdp'), may hold values from 64 to 192, as said below
- norm_gains: float32 [2, 2048], replicated, may hold values from 0.5 to 1.5
- qkv_weight: bfloat16 [2048, 3, 2048], P('fsdp', None, 'tensor'), may hold values from -0.125 to 0.125
- out_weight: bfloat16 [2048, 2048], P('tensor', 'fsdp'), may hold values from -1 to 1
- up_weight: bfloat16 [2048, 8192], P('fsdp', 'tensor'), may hold values from -0.125 to 0.125
- down_weight: bfloat16 [8192, 2048], P('tensor', 'fsdp'), may hold values from -0.0625 to 0.0625
- router_first: float32 [2, 2048, 256], replicated, may hold values from -0.125 to 0.125
- router_second: float32 [2, 256, 4], replicated, may hold values from -0.375 to 0.375
- cotangent: bfloat16 [4096, 2048], P('fsdp'), may hold values from -6 to 6
Outputs:
- block_out: bfloat16 [4096, 2048], P('fsdp')
- input_grad: bfloat16 [4096, 2048], P('fsdp')
- grad_gains: float32 [2, 2048], replicated
- grad_qkv: float32 [2048, 3, 2048], P('fsdp', None, 'tensor')
- grad_out: float32 [2048, 2048], P('tensor', 'fsdp')
- grad_up: float32 [2048, 8192], P('fsdp', 'tensor')
- grad_down: float32 [8192, 2048], P('tensor', 'fsdp')
- grad_router_first: float32 [2, 2048, 256], replicated
- grad_router_second: float32 [2, 256, 4], replicated
- usage: float32 [2, 4], replicated
Inputs may be any that keep to these rules, and one draw needn't show every extreme that they name: Each row holds the lengths of the 2 sequences of one index of fsdp; a row sums to between 128 and 256, and some row to exactly 256.
All inputs are finite; a program needn't handle non-finite values.
Results may differ from a plain program's by a relative error of at most 0.014.
Values may be sent and summed in bfloat16 or wider, within the bound.
A program may use at most 320 MiB of HBM per device.

v0:
```python
from functools import partial

import jax
import jax.numpy as jnp
from jax import lax
from jax.sharding import PartitionSpec as P

HEADS = 16
HD = 128
FF = 8192
NB = 4


epsilon = 1e-05
theta_base = 10000.0
highest = lax.Precision.HIGHEST


def layout(length_row, row_count):
    slot_ids = jnp.arange(row_count, dtype=jnp.int32)
    seq_ends = jnp.cumsum(length_row)
    seq_starts = seq_ends - length_row
    member = (slot_ids[:, None] >= seq_starts[None, :]) & (slot_ids[:, None] < seq_ends[None, :])
    seq_count = length_row.shape[0]
    seq_of = jnp.sum(jnp.where(member, jnp.arange(seq_count, dtype=jnp.int32)[None, :], 0), axis=1)
    live_rows = jnp.any(member, axis=1)
    seq_begin = jnp.sum(jnp.where(member, seq_starts[None, :], 0), axis=1)
    segment = jnp.where(live_rows, seq_of, seq_count + slot_ids)
    position = slot_ids - seq_begin
    return (segment, position, live_rows)


def rotary_tables(position):
    half_dim = HD // 2
    frequency = theta_base ** (-2.0 * jnp.arange(half_dim, dtype=jnp.float32) / HD)
    angles = position.astype(jnp.float32)[:, None] * frequency[None, :]
    return (jnp.cos(angles)[:, None, :], jnp.sin(angles)[:, None, :])


def rotate(operand, cosine, sine_table):
    half_dim = operand.shape[-1] // 2
    lead_half = operand[..., :half_dim]
    tail_half = operand[..., half_dim:]
    return jnp.concatenate(
        [lead_half * cosine - tail_half * sine_table, tail_half * cosine + lead_half * sine_table],
        axis=-1,
    )


def norm_piece(values_in, gain_row):
    return (
        values_in
        * lax.rsqrt(jnp.mean(values_in * values_in, axis=-1, keepdims=True) + epsilon)
        * gain_row
    )


def route_piece(hidden_in, router_in, router_out, bucket):
    inner = jax.nn.silu(jnp.dot(hidden_in, router_in, precision=highest))
    logits = jnp.dot(inner, router_out, precision=highest)
    probs_all = jax.nn.softmax(logits, axis=-1)
    onehot = (bucket[:, None] == jnp.arange(NB, dtype=jnp.int32)[None, :]).astype(jnp.float32)
    return NB * jnp.sum(probs_all * onehot, axis=-1)


def tensor_total(local_term):
    return lax.psum(local_term, "tensor")


def contract_rows(left_in, right_in):
    return lax.dot_general(
        left_in, right_in, (((0,), (0,)), ((), ())), preferred_element_type=jnp.float32
    )


def times_transposed(left_in, matrix):
    return lax.dot_general(
        left_in, matrix, (((1,), (1,)), ((), ())), preferred_element_type=jnp.float32
    )


def block_mask(first_row, block_rows, segment, key_used):
    row_count = segment.shape[0]
    slot_ids = jnp.arange(row_count, dtype=jnp.int32)
    query_ids = first_row + jnp.arange(block_rows, dtype=jnp.int32)
    same_seq = segment[:, None] == segment[None, :]
    causal = slot_ids[None, :] <= query_ids[:, None]
    diagonal = slot_ids[None, :] == query_ids[:, None]
    return (same_seq & causal)[None] & (key_used[:, None, :] | diagonal[None])


def attend(query, keyed, value, head_used, segment):
    row_count = query.shape[0]
    block_rows = min(row_count, 512)
    scale = HD ** (-0.5)
    key_used = head_used.T

    def one_block(block_index):
        first_row = block_index * block_rows
        allowed = block_mask(first_row, block_rows, segment, key_used)
        scores = (
            jnp.einsum("qhe,khe->hqk", query, keyed, preferred_element_type=jnp.float32) * scale
        )
        scores = jnp.where(allowed, scores, -1e30)
        row_top = jnp.max(scores, axis=-1, keepdims=True)
        weights = jnp.exp(scores - row_top)
        row_total = jnp.sum(weights, axis=-1, keepdims=True)
        probs_low = (weights / row_total).astype(jnp.bfloat16)
        mixed_part = jnp.einsum(
            "hqk,khe->qhe", probs_low, value, preferred_element_type=jnp.float32
        )
        mixed_part = jnp.where(head_used[:, :, None], mixed_part, 0.0).astype(jnp.bfloat16)
        return (mixed_part, (row_top + jnp.log(row_total))[..., 0])

    mixed_all, log_totals = lax.map(one_block, jnp.arange(row_count // block_rows, dtype=jnp.int32))
    return (mixed_all.reshape(query.shape), log_totals)


def attend_back(query, keyed, value, head_used, segment, log_totals, grad_attended):
    row_count = query.shape[0]
    block_rows = min(row_count, 512)
    scale = HD ** (-0.5)
    key_used = head_used.T

    def one_block(running, block_index):
        grad_keyed, grad_value = running
        first_row = block_index * block_rows
        log_part = lax.dynamic_index_in_dim(log_totals, block_index, 0, keepdims=False)
        allowed = block_mask(first_row, block_rows, segment, key_used)
        scores = (
            jnp.einsum("qhe,khe->hqk", query, keyed, preferred_element_type=jnp.float32) * scale
        )
        scores = jnp.where(allowed, scores, -1e30)
        weights = jnp.exp(scores - log_part[:, :, None])
        grad_value = grad_value + jnp.einsum(
            "hqk,qhe->khe",
            weights.astype(jnp.bfloat16),
            grad_attended,
            preferred_element_type=jnp.float32,
        )
        grad_weights = jnp.einsum(
            "qhe,khe->hqk", grad_attended, value, preferred_element_type=jnp.float32
        )
        row_dot = jnp.sum(weights * grad_weights, axis=-1, keepdims=True)
        grad_scores = (weights * (grad_weights - row_dot)).astype(jnp.bfloat16)
        grad_query = (
            jnp.einsum("hqk,khe->qhe", grad_scores, keyed, preferred_element_type=jnp.float32)
            * scale
        )
        grad_keyed = (
            grad_keyed
            + jnp.einsum("hqk,qhe->khe", grad_scores, query, preferred_element_type=jnp.float32)
            * scale
        )
        return ((grad_keyed, grad_value), grad_query)

    zero_start = jnp.zeros(keyed.shape, jnp.float32)
    (grad_keyed, grad_value), grad_query = lax.scan(
        one_block, (zero_start, zero_start), jnp.arange(row_count // block_rows, dtype=jnp.int32)
    )
    return (grad_query.reshape(query.shape), grad_keyed, grad_value)


def shards(
    tokens,
    head_bucket,
    ffn_bucket,
    lengths,
    norm_gains,
    qkv_weight,
    out_weight,
    up_weight,
    down_weight,
    router_first,
    router_second,
    cotangent,
):
    row_count = tokens.shape[0]
    model_width = tokens.shape[1]
    local_width = out_weight.shape[0]
    local_heads = local_width // HD
    local_units = up_weight.shape[1]
    tensor_rank = lax.axis_index("tensor")
    segment, position, live_rows = layout(lengths[0], row_count)
    cosine, sine_table = rotary_tables(position)
    head_ids = tensor_rank * local_heads + jnp.arange(local_heads, dtype=jnp.int32)
    head_used = head_ids[None, :] < HEADS // NB * (head_bucket[:, None] + 1)
    unit_ids = tensor_rank * local_units + jnp.arange(local_units, dtype=jnp.int32)
    unit_used = unit_ids[None, :] < FF // NB * (ffn_bucket[:, None] + 1)
    block_in = tokens.astype(jnp.float32)
    qkv_whole, up_whole = (
        lax.all_gather(qkv_weight, "fsdp", axis=0, tiled=True),
        lax.all_gather(up_weight, "fsdp", axis=0, tiled=True),
    )
    normed_heads, norm_heads_back = jax.vjp(norm_piece, block_in, norm_gains[0])
    hidden_heads = normed_heads.astype(jnp.bfloat16)
    gate_heads, route_heads_back = jax.vjp(
        partial(route_piece, bucket=head_bucket),
        hidden_heads.astype(jnp.float32),
        router_first[0],
        router_second[0],
    )
    qkv_all = jnp.dot(
        hidden_heads,
        qkv_whole.reshape(model_width, 3 * local_width),
        preferred_element_type=jnp.float32,
    )
    qkv_all = qkv_all.reshape(row_count, 3, local_heads, HD)
    query = rotate(qkv_all[:, 0], cosine, sine_table).astype(jnp.bfloat16)
    keyed = rotate(qkv_all[:, 1], cosine, sine_table).astype(jnp.bfloat16)
    value = qkv_all[:, 2].astype(jnp.bfloat16)
    attended, log_totals = attend(query, keyed, value, head_used, segment)
    attended_flat = attended.reshape(row_count, local_width)
    out_whole, down_whole = (
        lax.all_gather(out_weight, "fsdp", axis=1, tiled=True),
        lax.all_gather(down_weight, "fsdp", axis=1, tiled=True),
    )
    projected = tensor_total(jnp.dot(attended_flat, out_whole, preferred_element_type=jnp.float32))
    middle = block_in + gate_heads[:, None] * projected
    normed_units, norm_units_back = jax.vjp(norm_piece, middle, norm_gains[1])
    hidden_units = normed_units.astype(jnp.bfloat16)
    gate_units, route_units_back = jax.vjp(
        partial(route_piece, bucket=ffn_bucket),
        hidden_units.astype(jnp.float32),
        router_first[1],
        router_second[1],
    )
    upward = jnp.dot(hidden_units, up_whole, preferred_element_type=jnp.float32)
    activated = jnp.where(unit_used, jnp.square(jax.nn.relu(upward)), 0.0).astype(jnp.bfloat16)
    downward = tensor_total(jnp.dot(activated, down_whole, preferred_element_type=jnp.float32))
    block_out = jnp.where(live_rows[:, None], middle + gate_units[:, None] * downward, 0.0).astype(
        jnp.bfloat16
    )
    grad_top = jnp.where(live_rows[:, None], cotangent.astype(jnp.float32), 0.0)
    out_back, down_back = (
        lax.all_gather(out_weight, "fsdp", axis=1, tiled=True),
        lax.all_gather(down_weight, "fsdp", axis=1, tiled=True),
    )
    qkv_back, up_back = (
        lax.all_gather(qkv_weight, "fsdp", axis=0, tiled=True),
        lax.all_gather(up_weight, "fsdp", axis=0, tiled=True),
    )
    grad_gate_units = jnp.sum(grad_top * downward, axis=1)
    grad_down_in = (gate_units[:, None] * grad_top).astype(jnp.bfloat16)
    grad_down_local = contract_rows(activated, grad_down_in)
    grad_act = times_transposed(grad_down_in, down_back)
    grad_up_in = jnp.where(unit_used, 2.0 * jax.nn.relu(upward) * grad_act, 0.0).astype(
        jnp.bfloat16
    )
    grad_up_local = contract_rows(hidden_units, grad_up_in)
    route_units_grads = route_units_back(grad_gate_units)
    grad_hidden_units = tensor_total(times_transposed(grad_up_in, up_back)) + route_units_grads[0]
    norm_units_grads = norm_units_back(grad_hidden_units)
    grad_middle = grad_top + norm_units_grads[0]
    grad_gate_heads = jnp.sum(grad_middle * projected, axis=1)
    grad_projected = (gate_heads[:, None] * grad_middle).astype(jnp.bfloat16)
    grad_out_local = contract_rows(attended_flat, grad_projected)
    grad_out_shard, grad_down_shard = (
        lax.psum_scatter(grad_out_local, "fsdp", scatter_dimension=1, tiled=True),
        lax.psum_scatter(grad_down_local, "fsdp", scatter_dimension=1, tiled=True),
    )
    grad_attended = (
        times_transposed(grad_projected, out_back)
        .astype(jnp.bfloat16)
        .reshape(row_count, local_heads, HD)
    )
    grad_attended = jnp.where(head_used[:, :, None], grad_attended, jnp.zeros((), jnp.bfloat16))
    grad_query, grad_keyed, grad_value = attend_back(
        query, keyed, value, head_used, segment, log_totals, grad_attended
    )
    grad_qkv_in = jnp.stack(
        [
            rotate(grad_query, cosine, -sine_table),
            rotate(grad_keyed, cosine, -sine_table),
            grad_value,
        ],
        axis=1,
    )
    grad_qkv_in = grad_qkv_in.astype(jnp.bfloat16).reshape(row_count, 3 * local_width)
    grad_qkv_local = contract_rows(hidden_heads, grad_qkv_in).reshape(model_width, 3, local_width)
    route_heads_grads = route_heads_back(grad_gate_heads)
    grad_hidden_heads = (
        tensor_total(times_transposed(grad_qkv_in, qkv_back.reshape(model_width, 3 * local_width)))
        + route_heads_grads[0]
    )
    norm_heads_grads = norm_heads_back(grad_hidden_heads)
    input_grad = (grad_middle + norm_heads_grads[0]).astype(jnp.bfloat16)
    grad_qkv_shard, grad_up_shard = (
        lax.psum_scatter(grad_qkv_local, "fsdp", scatter_dimension=0, tiled=True),
        lax.psum_scatter(grad_up_local, "fsdp", scatter_dimension=0, tiled=True),
    )
    bucket_ids = jnp.arange(NB, dtype=jnp.int32)[None, :]
    head_counts = jnp.sum(
        jnp.where(live_rows[:, None] & (head_bucket[:, None] == bucket_ids), 1.0, 0.0), axis=0
    )
    width_counts = jnp.sum(
        jnp.where(live_rows[:, None] & (ffn_bucket[:, None] == bucket_ids), 1.0, 0.0), axis=0
    )
    usage_local = jnp.stack([head_counts, width_counts]).astype(jnp.float32)
    gain_local = jnp.stack([norm_heads_grads[1], norm_units_grads[1]])
    first_local = jnp.stack([route_heads_grads[1], route_units_grads[1]])
    second_local = jnp.stack([route_heads_grads[2], route_units_grads[2]])
    grad_gains, grad_router_first, grad_router_second, usage = lax.psum(
        (gain_local, first_local, second_local, usage_local), "fsdp"
    )
    return (
        block_out,
        input_grad,
        grad_gains,
        grad_qkv_shard,
        grad_out_shard,
        grad_up_shard,
        grad_down_shard,
        grad_router_first,
        grad_router_second,
        usage,
    )


def solution(mesh):
    in_specs = (
        P("fsdp", None),
        P("fsdp"),
        P("fsdp"),
        P("fsdp", None),
        P(),
        P("fsdp", None, "tensor"),
        P("tensor", "fsdp"),
        P("fsdp", "tensor"),
        P("tensor", "fsdp"),
        P(),
        P(),
        P("fsdp", None),
    )
    out_specs = (
        P("fsdp", None),
        P("fsdp", None),
        P(),
        P("fsdp", None, "tensor"),
        P("tensor", "fsdp"),
        P("fsdp", "tensor"),
        P("tensor", "fsdp"),
        P(),
        P(),
        P(),
    )
    return jax.shard_map(shards, mesh=mesh, in_specs=in_specs, out_specs=out_specs, check_vma=False)
```

profile of v0, /device:TPU:0, one launch (start us, length us, event | category | flops | bytes accessed | tf_op | source)
XLA Modules:
  0.0 1910.2 jit_solution(13988335224111586730)
XLA Ops:
  7.3 2.4 copy.43
  12.2 105.3 %all-gather.5.cloned.1.call-done = bf16[2048,3,1024]{0,2,1:T(8,128)(2,1)} async-done(((bf16[128,3,1024]{0,2,1:T(8,128)(2,1)}), bf16[2048,3,1024]{0,2,1:T(8,128)(2,1)}) %all-gather.5.cloned.1.call-update) | async-done | bytes 12582928 | tf_op jit(solution)/shard_map/all_gather | solution.py:192
  117.5 6.8 fusion.28
  127.8 43.2 %all-gather.7.cloned.1.call-done = bf16[1024,2048]{1,0:T(8,128)(2,1)} async-done(((bf16[1024,128]{1,0:T(8,128)(2,1)}), bf16[1024,2048]{1,0:T(8,128)(2,1)}) %all-gather.7.cloned.1.call-update) | async-done | bytes 4194320 | tf_op jit(solution)/shard_map/all_gather | solution.py:215
  171.0 4.8 fusion.106
  177.4 2.9 fusion.15
  183.2 53.9 %all-reduce.7.cloned.1.call-done = f32[256,2048]{1,0:T(8,128)} async-done(((f32[256,2048]{1,0:T(8,128)}), f32[256,2048]{1,0:T(8,128)}) %all-reduce.7.cloned.1.call-update) | async-done | bytes 2097168 | tf_op jit(solution)/shard_map/psum | solution.py:67
  237.1 2.1 multiply_reduce_fusion.5
  239.8 1.2 multiply_convert_fusion.3
  241.0 125.3 %all-gather.9.cloned.1.call-done = bf16[2048,4096]{1,0:T(8,128)(2,1)} async-done(((bf16[128,4096]{1,0:T(8,128)(2,1)}), bf16[2048,4096]{1,0:T(8,128)(2,1)}) %all-gather.9.cloned.1.call-update) | async-done | bytes 16777232 | tf_op jit(solution)/shard_map/all_gather | solution.py:193
  366.3 12.6 convolution_maximum_fusion
  378.9 118.1 %all-gather.11.cloned.1.call-done = bf16[4096,2048]{1,0:T(8,128)(2,1)} async-done(((bf16[4096,128]{1,0:T(8,128)(2,1)}), bf16[4096,2048]{1,0:T(8,128)(2,1)}) %all-gather.11.cloned.1.call-update) | async-done | bytes 16777232 | tf_op jit(solution)/shard_map/all_gather | solution.py:216
  497.1 12.9 fusion.95
  510.6 3.1 fusion.12
  516.6 54.6 %all-reduce.9.cloned.1.call-done = f32[256,2048]{1,0:T(8,128)} async-done(((f32[256,2048]{1,0:T(8,128)}), f32[256,2048]{1,0:T(8,128)}) %all-reduce.9.cloned.1.call-update) | async-done | bytes 2097168 | tf_op jit(solution)/shard_map/psum | solution.py:67
  571.3 2.4 multiply_reduce_fusion.4
  573.7 1.4 fusion.58
  575.7 10.4 fusion
  586.1 12.2 fusion.107
  600.6 2.1 fusion.36
  602.8 58.7 %all-reduce.11.cloned.1.call-done = f32[256,2048]{1,0:T(8,128)} async-done(((f32[256,2048]{1,0:T(8,128)}), f32[256,2048]{1,0:T(8,128)}) %all-reduce.11.cloned.1.call-update) | async-done | bytes 2097168 | tf_op jit(solution)/shard_map/psum | solution.py:67
  661.5 5.5 multiply_reduce_fusion
  667.2 2.7 multiply_reduce_fusion.1
  669.9 1.3 copy-done.3
  671.2 2.1 convolution_convert_fusion
  673.3 2.0 copy.47
  675.4 2.1 multiply_reduce_fusion.2
  681.3 1.1 copy-done.6
  683.1 4.8 fusion.108
  689.1 1.2 convolution_bitcast_fusion
  691.0 1.3 convolution_bitcast_fusion.1
  692.4 2.3 pad_maximum_fusion
  694.8 1.5 copy-done.4
  696.3 5.7 fusion.92
  702.1 12.0 fusion.30
  714.8 19.4 %fusion.93 = f32[4096,2048]{1,0:T(8,128)} fusion(bf16[256,2048]{1,0:T(8,128)(2,1)} %param.23, f32[256]{0:T(256)S(1)} %copy-done.66, pred[256]{0:T(512)(128)(4,1)S(1)} %copy-done.40, f32[256,4096]{1,0:T(8,128)} %convolution_maximum_fusion, s32[4096]{0:T(1024)S(1)} %copy-done.25, s32[256]{0:T(256)S(1)} %copy-done.42), kind=kOutput, calls=%fused_computation.185 | convolution fusion | flops 4301258752 | bytes 38816000 | tf_op jit(solution)/shard_map/dot_general | solution.py:71
  734.4 17.6 fusion.109
  752.7 1.2 convolution_bitcast_fusion.4
  754.0 1.2 convolution_bitcast_fusion.5
  755.3 6.0 fusion.5
  761.3 62.3 %all-reduce = (f32[2,2048]{1,0:T(2,128)}, f32[2,256,4]{1,2,0:T(4,128)}, f32[2,4]{1,0:T(2,128)}) all-reduce(f32[2,2048]{1,0:T(2,128)S(1)} %pad_maximum_fusion.7, f32[2,256,4]{1,2,0:T(4,128)S(1)} %pad_maximum_fusion.8, f32[2,4]{1,0:T(2,128)S(1)} %pad_maximum_fusion.9), channel_id=1, replica_groups=mesh['fsdp'=16,'tensor'=2] {'fsdp'}, use_global_device_ids=true, to_apply=%region_27.28 | all-reduce | flops 6152 | bytes 49216 | tf_op jit(solution)/shard_map/psum | solution.py:303
  823.6 3.2 fusion.8
  826.8 39.9 %all-reduce.15.cloned.1.call-done = f32[2,2048,256]{2,1,0:T(8,128)} async-done(((f32[2,2048,256]{2,1,0:T(8,128)}), f32[2,2048,256]{2,1,0:T(8,128)}) %all-reduce.15.cloned.1.call-update) | async-done | bytes 4194320 | tf_op jit(solution)/shard_map/psum | solution.py:303
  866.7 108.8 %reduce-scatter.7.cloned.1.call-done = f32[1024,128]{1,0:T(8,128)} async-done(((f32[1024,2048]{1,0:T(8,128)}), f32[1024,128]{1,0:T(8,128)}) %reduce-scatter.7.cloned.1.call-update) | async-done | bytes 524304 | tf_op jit(solution)/shard_map/reduce_scatter | solution.py:259
  975.5 249.0 %reduce-scatter.5.cloned.1.call-done = f32[128,3,1024]{2,0,1:T(8,128)} async-done(((f32[2048,3,1024]{2,0,1:T(8,128)}), f32[128,3,1024]{2,0,1:T(8,128)}) %reduce-scatter.5.cloned.1.call-update) | async-done | bytes 1572880 | tf_op jit(solution)/shard_map/reduce_scatter | solution.py:289
  1224.5 337.1 %reduce-scatter.11.cloned.1.call-done = f32[4096,128]{1,0:T(8,128)} async-done(((f32[4096,2048]{1,0:T(8,128)}), f32[4096,128]{1,0:T(8,128)}) %reduce-scatter.11.cloned.1.call-update) | async-done | bytes 2097168 | tf_op jit(solution)/shard_map/reduce_scatter | solution.py:260
  1561.6 337.1 %reduce-scatter.9.cloned.1.call-done = f32[128,4096]{1,0:T(8,128)} async-done(((f32[2048,4096]{1,0:T(8,128)}), f32[128,4096]{1,0:T(8,128)}) %reduce-scatter.9.cloned.1.call-update) | async-done | bytes 2097168 | tf_op jit(solution)/shard_map/reduce_scatter | solution.py:290
  1898.8 4.5 copy.70
  (252 shorter events, 25.3 us)
Async XLA Ops:
  7.2 3.3 copy-start.83
  7.2 3.7 copy-start
  7.2 4.0 copy-start.56
  7.2 4.9 copy-start.46
  7.2 110.2 %all-gather.5.cloned.1.call-start = ((), (), s32[]{:S(2)}) async-start(), calls=%async_computation.4 | async-start | bytes 13369344 | tf_op jit(solution)/shard_map/all_gather | solution.py:192
  9.7 161.4 %all-gather.7.cloned.1.call-start = ((), (), s32[]{:S(2)}) async-start(), calls=%async_computation.5 | async-start | bytes 4456448 | tf_op jit(solution)/shard_map/all_gather | solution.py:215
  10.4 226.7 %all-reduce.7.cloned.1.call-start = ((), (), s32[]{:S(2)}) async-start(), calls=%async_computation.6 | async-start | bytes 4194304 | tf_op jit(solution)/shard_map/psum | solution.py:67
  10.8 113.5 %copy-start.37 = (pred[256]{0:T(512)(128)(4,1)}, pred[256]{0:T(512)(128)(4,1)S(1)}, u32[]{:S(2)}) copy-start(pred[256]{0:T(512)(128)(4,1)S(1)} %fusion.91) | copy-start | bytes 772
  11.2 166.1 %copy-start.28 = (f32[256]{0:T(256)}, f32[256]{0:T(256)S(1)}, u32[]{:S(2)}) copy-start(f32[256]{0:T(256)S(1)} %fusion.73) | copy-start | bytes 3076
  11.3 115.0 %copy-start.35 = (pred[256,8]{0,1:T(8,128)(4,1)}, pred[256,8]{0,1:T(8,128)(4,1)S(1)}, u32[]{:S(2)}) copy-start(pred[256,8]{0,1:T(8,128)(4,1)S(1)} %broadcast_compare_fusion.1) | copy-start | bytes 6148
  12.2 227.0 %copy-start.26 = (f32[1,2048]{1,0:T(1,128)}, f32[1,2048]{1,0:T(1,128)S(1)}, u32[]{:S(2)}) copy-start(f32[1,2048]{1,0:T(1,128)S(1)} %get-tuple-element.103) | copy-start | bytes 24580
  127.8 48.0 %copy-start.20 = (bf16[256,8,128]{0,2,1:T(8,128)(2,1)}, bf16[256,8,128]{0,2,1:T(8,128)(2,1)S(1)}, u32[]{:S(2)}) copy-start(bf16[256,8,128]{0,2,1:T(8,128)(2,1)S(1)} %fusion.26) | copy-start | bytes 1572868
  175.8 190.4 %all-gather.9.cloned.1.call-start = ((), (), s32[]{:S(2)}) async-start(), calls=%async_computation.7 | async-start | bytes 17825792 | tf_op jit(solution)/shard_map/all_gather | solution.py:193
  176.4 4.6 copy-start.80
  176.4 320.6 %all-gather.11.cloned.1.call-start = ((), (), s32[]{:S(2)}) async-start(), calls=%async_computation.8 | async-start | bytes 17825792 | tf_op jit(solution)/shard_map/all_gather | solution.py:216
  177.0 394.2 %all-reduce.9.cloned.1.call-start = ((), (), s32[]{:S(2)}) async-start(), calls=%async_computation.9 | async-start | bytes 4194304 | tf_op jit(solution)/shard_map/psum | solution.py:67
  177.4 4.7 copy-start.67
  241.0 256.1 %copy-start.41 = (s32[256]{0:T(256)S(1)}, s32[256]{0:T(256)}, u32[]{:S(2)}) copy-start(s32[256]{0:T(256)} %add_multiply_fusion) | copy-start | bytes 3076
  510.0 61.2 %copy-start.38 = (pred[256]{0:T(512)(128)(4,1)S(1)}, pred[256]{0:T(512)(128)(4,1)}, u32[]{:S(2)}) copy-start(pred[256]{0:T(512)(128)(4,1)} %copy-done.37) | copy-start | bytes 772
  510.0 151.5 %all-reduce.11.cloned.1.call-start = ((), (), s32[]{:S(2)}) async-start(), calls=%async_computation.10 | async-start | bytes 4194304 | tf_op jit(solution)/shard_map/psum | solution.py:67
  510.6 3.8 copy-start.81
  571.3 4.4 copy-start.7
  571.3 4.4 copy-start.24
  598.4 156.9 %all-reduce.13.cloned.1.call-start = ((), (), s32[]{:S(2)}) async-start(), calls=%async_computation.11 | async-start | bytes 4194304 | tf_op jit(solution)/shard_map/psum | solution.py:67
  661.5 5.6 copy-start.52
  661.5 5.6 copy-start.8
  661.5 5.6 copy-start.9
  661.5 5.6 copy-start.10
  661.5 5.6 copy-start.27
  661.5 5.6 copy-start.39
  661.5 5.6 copy-start.48
  661.5 5.6 copy-start.65
  667.2 4.0 copy-start.62
  667.2 4.0 copy-start.79
  671.2 4.2 copy-start.2
  675.4 7.0 slice-start
  678.1 4.4 slice-start.1
  680.3 2.8 slice-start.2
  687.9 2.5 copy-start.31
  687.9 2.6 copy-start.22
  688.0 2.6 copy-start.82
  688.0 178.7 %all-reduce.15.cloned.1.call-start = ((), (), s32[]{:S(2)}) async-start(), calls=%async_computation.16 | async-start | bytes 8388608 | tf_op jit(solution)/shard_map/psum | solution.py:303
  694.7 280.8 %reduce-scatter.7.cloned.1.call-start = ((), (), s32[]{:S(2)}) async-start(), calls=%async_computation.13 | async-start | bytes 8912896 | tf_op jit(solution)/shard_map/reduce_scatter | solution.py:259
  702.0 522.5 %reduce-scatter.5.cloned.1.call-start = ((), (), s32[]{:S(2)}) async-start(), calls=%async_computation.12 | async-start | bytes 26738688 | tf_op jit(solution)/shard_map/reduce_scatter | solution.py:289
  714.1 847.6 %reduce-scatter.11.cloned.1.call-start = ((), (), s32[]{:S(2)}) async-start(), calls=%async_computation.15 | async-start | bytes 35651584 | tf_op jit(solution)/shard_map/reduce_scatter | solution.py:260
  734.1 1164.6 %reduce-scatter.9.cloned.1.call-start = ((), (), s32[]{:S(2)}) async-start(), calls=%async_computation.14 | async-start | bytes 35651584 | tf_op jit(solution)/shard_map/reduce_scatter | solution.py:290
  755.2 6.0 copy-start.34
  755.3 68.4 %copy-start.50 = (f32[256]{0:T(256)S(1)}, f32[256]{0:T(256)}, u32[]{:S(2)}) copy-start(f32[256]{0:T(256)} %copy-done.49) | copy-start | bytes 3076
  (52 other events, 66.9 us)
Sparse Core Ops, SparseCore 0:
  10.8 106.6 all-gather.4
  119.6 51.3 all-gather.6
  176.0 61.0 all-reduce.6
  239.4 126.8 all-gather.8
  368.5 128.5 all-gather.10
  510.1 61.0 all-reduce.8
  598.5 62.9 all-reduce.10
  688.0 62.9 all-reduce.12
  754.7 112.0 all-reduce.14
  871.8 103.7 reduce-scatter.6
  980.8 243.6 reduce-scatter.4
  1229.8 331.8 reduce-scatter.10
  1567.1 331.6 reduce-scatter.8
where the time goes:
time: 1920 us; the launch traced here: 1910 us
  waiting for transfers between devices  1630 us (85%)
  matrix products  152 us (8%)
  blocking collectives  62.3 us (3%)
  local copies, waits for them, and re-layouts  23.5 us (1%)
  other arithmetic  22.2 us (1%)
    reduce_scatter x1, waiting for transfers between devices, shards(): lax.psum_scatter(grad_down_local, 'fsdp', scatter_dimension=1, tiled=True)  337 us
    reduce_scatter x1, waiting for transfers between devices, shards(): lax.psum_scatter(grad_up_local, 'fsdp', scatter_dimension=0, tiled=True)  337 us
    reduce_scatter x1, waiting for transfers between devices, shards(): lax.psum_scatter(grad_qkv_local, 'fsdp', scatter_dimension=0, tiled=True)  249 us
    psum x4, waiting for transfers between devices, tensor_total(): return lax.psum(local_term, 'tensor')  167 us
    all_gather x1, waiting for transfers between devices, shards(): lax.all_gather(up_weight, 'fsdp', axis=0, tiled=True)  125 us
    all_gather x1, waiting for transfers between devices, shards(): lax.all_gather(down_weight, 'fsdp', axis=1, tiled=True)  118 us
    reduce_scatter x1, waiting for transfers between devices, shards(): lax.psum_scatter(grad_out_local, 'fsdp', scatter_dimension=1, tiled=True)  109 us
    all_gather x1, waiting for transfers between devices, shards(): lax.all_gather(qkv_weight, 'fsdp', axis=0, tiled=True)  105 us
  transfers between devices with their start and end apart: 13, of which 12 were waited for; matrix products, arithmetic and copies ran while one was open for 6% of the time, Pallas kernels for 0%

commit v1 on v0

v1 whole, which is shorter than its diff:
```python
from functools import partial

import jax
import jax.numpy as jnp
from jax import lax
from jax.sharding import PartitionSpec as P

HEADS = 16
HD = 128
FF = 8192
NB = 4
SHARE = 4

epsilon = 1e-05
theta_base = 10000.0
highest = lax.Precision.HIGHEST
low = jnp.bfloat16
wide = jnp.float32


def norm_piece(values_in, gain_row):
    return (
        values_in
        * lax.rsqrt(jnp.mean(values_in * values_in, axis=-1, keepdims=True) + epsilon)
        * gain_row
    )


def route_piece(hidden_in, router_in, router_out, bucket):
    inner = jax.nn.silu(jnp.dot(hidden_in, router_in, precision=highest))
    logits = jnp.dot(inner, router_out, precision=highest)
    probs_all = jax.nn.softmax(logits, axis=-1)
    onehot = (bucket[:, None] == jnp.arange(NB, dtype=jnp.int32)[None, :]).astype(wide)
    return NB * jnp.sum(probs_all * onehot, axis=-1)


def dot(left_in, right_in):
    return jnp.dot(left_in, right_in, preferred_element_type=wide)


def dot_rows(left_in, right_in):
    return lax.dot_general(
        left_in, right_in, (((0,), (0,)), ((), ())), preferred_element_type=wide
    )


def dot_cols(left_in, right_in):
    return lax.dot_general(
        left_in, right_in, (((1,), (1,)), ((), ())), preferred_element_type=wide
    )


def rotate(operand, cosine, sine_table):
    half_dim = operand.shape[-1] // 2
    lead_half = operand[..., :half_dim]
    tail_half = operand[..., half_dim:]
    return jnp.concatenate(
        [lead_half * cosine - tail_half * sine_table, tail_half * cosine + lead_half * sine_table],
        axis=-1,
    )


def layout(length_rows, slot_ids):
    seq_count = length_rows.shape[1]
    order = jnp.arange(seq_count, dtype=jnp.int32)
    seq_ends = jnp.sum(
        jnp.where(order[None, None, :] <= order[None, :, None], length_rows[:, None, :], 0), axis=2
    )
    seq_starts = seq_ends - length_rows
    slots = slot_ids[None, :, None]
    member = (slots >= seq_starts[:, None, :]) & (slots < seq_ends[:, None, :])
    seq_of = jnp.sum(jnp.where(member, jnp.arange(seq_count, dtype=jnp.int32), 0), axis=2)
    live_rows = jnp.any(member, axis=2)
    seq_begin = jnp.sum(jnp.where(member, seq_starts[:, None, :], 0), axis=2)
    segment = jnp.where(live_rows, seq_of, seq_count + slot_ids[None, :])
    position = slot_ids[None, :] - seq_begin
    return segment, position, live_rows


def solution(mesh):
    fsdp = mesh.shape["fsdp"]
    ring_size = fsdp // SHARE

    def hop(moved, bits):
        return lax.ppermute(moved, "fsdp", [(i, i ^ bits) for i in range(fsdp)])

    def cross(moved):
        return lax.ppermute(moved, "tensor", [(0, 1), (1, 0)])

    def shards(
        tokens,
        head_bucket,
        ffn_bucket,
        lengths,
        norm_gains,
        qkv_weight,
        out_weight,
        up_weight,
        down_weight,
        router_first,
        router_second,
        cotangent,
    ):
        rows, width = tokens.shape
        half = rows // 2
        rank = lax.axis_index("fsdp")
        side = lax.axis_index("tensor")
        share = rank % SHARE
        place = rank // SHARE
        local_units = up_weight.shape[1]
        units = local_units // SHARE
        local_width = out_weight.shape[0]
        head_width = local_width // SHARE
        heads = head_width // HD
        owned = width // fsdp
        block = width // ring_size

        chain = [None, None]

        def ring(moved, stream):
            if chain[stream] is not None:
                moved, _ = lax.optimization_barrier((moved, chain[stream]))
            got = lax.ppermute(
                moved, "fsdp", [(i, (i + SHARE) % fsdp) for i in range(fsdp)]
            )
            chain[stream] = got
            return got

        def place_at(step):
            return (place - step) % ring_size

        def own_half(arr):
            return lax.dynamic_slice_in_dim(arr, side * half, half, 0)

        def relative(arr):
            return jnp.concatenate(
                [own_half(arr), lax.dynamic_slice_in_dim(arr, (1 - side) * half, half, 0)], axis=0
            )

        def gather_rows(arr):
            other = hop(arr, 2)
            plane = jnp.concatenate([arr[:half], other[:half], arr[half:], other[half:]], axis=0)
            return jnp.concatenate([plane, hop(plane, 1)], axis=0)

        def gather_halves(arr):
            pair = jnp.concatenate([arr, hop(arr, 2)], axis=0)
            plane = jnp.concatenate([pair, cross(pair)], axis=0)
            return jnp.concatenate([plane, hop(plane, 1)], axis=0)

        def reduce_rows(keep, send):
            total = keep + hop(send.astype(low), 1).astype(wide)
            total = total[: 2 * half] + cross(total[2 * half :].astype(low)).astype(wide)
            return total[:half] + hop(total[half:].astype(low), 2).astype(wide)

        def whole_rows(arr):
            other = cross(arr)
            return jnp.where(
                side == 0,
                jnp.concatenate([arr, other], axis=0),
                jnp.concatenate([other, arr], axis=0),
            )

        def spread(pieces_for, axis):
            out = None
            for bits in range(SHARE):
                piece = pieces_for(share ^ bits)
                got = piece if bits == 0 else hop(piece, bits)
                if out is None:
                    dims = list(got.shape)
                    dims[axis] *= SHARE
                    out = jnp.zeros(dims, got.dtype)
                out = lax.dynamic_update_slice_in_dim(
                    out, got, (share ^ bits) * got.shape[axis], axis
                )
            return out

        def ring_gather(own, axis):
            dims = list(own.shape)
            dims[axis] = width
            out = jnp.zeros(dims, own.dtype)
            mid = own.shape[0] // 2
            moving = [own[:mid], own[mid:]]
            for step in range(ring_size):
                if step:
                    moving = [ring(moving[s], s) for s in range(2)]
                base = place_at(step) * block
                for s in range(2):
                    if axis == 0:
                        at = (base + s * mid, 0)
                    else:
                        at = (s * mid, base)
                    out = lax.dynamic_update_slice(out, moving[s], at)
            return out

        def ring_reduce(term):
            moving = [None, None]
            for step in range(1, ring_size):
                for s in range(2):
                    part = term(place_at(step), s)
                    if moving[s] is not None:
                        part = part + moving[s].astype(wide)
                    moving[s] = part.astype(low)
                for s in range(2):
                    moving[s] = ring(moving[s], s)
            return [term(place, s) + moving[s].astype(wide) for s in range(2)]

        def scatter_back(parts, axis):
            joined = jnp.concatenate(parts, axis=0)
            other = 1 - axis
            out_dims = list(joined.shape)
            out_dims[axis] = owned
            stride = out_dims[other]
            out_dims[other] *= SHARE
            out = jnp.zeros(out_dims, wide)
            for bits in range(SHARE):
                piece = lax.dynamic_slice_in_dim(joined, (share ^ bits) * owned, owned, axis)
                if bits:
                    piece = hop(piece.astype(low), bits).astype(wide)
                out = lax.dynamic_update_slice_in_dim(out, piece, (share ^ bits) * stride, other)
            return out

        def qkv_piece(target):
            return lax.dynamic_slice_in_dim(
                qkv_weight, target * head_width, head_width, 2
            ).reshape(owned, 3 * head_width)

        qkv_block = spread(qkv_piece, 0)
        rel_tokens = relative(tokens)
        rel_cot = relative(cotangent)
        ints = relative(jnp.stack([head_bucket, ffn_bucket], axis=1))
        qkv_full = ring_gather(qkv_block, 0)
        all_tokens = gather_rows(rel_tokens)
        buckets = gather_rows(ints)
        pair_lengths = jnp.concatenate([lengths, hop(lengths, 2)], axis=0)
        group_lengths = jnp.concatenate([pair_lengths, hop(pair_lengths, 1)], axis=0)

        out_block = spread(
            lambda t: lax.dynamic_slice_in_dim(out_weight, t * head_width, head_width, 0), 1
        )
        out_full = ring_gather(out_block, 1)
        up_block = spread(lambda t: lax.dynamic_slice_in_dim(up_weight, t * units, units, 1), 0)
        up_full = ring_gather(up_block, 0)
        down_block = spread(
            lambda t: lax.dynamic_slice_in_dim(down_weight, t * units, units, 0), 1
        )
        down_full = ring_gather(down_block, 1)
        all_cot = gather_rows(rel_cot)

        slot_ids = jnp.concatenate(
            [
                side * half + jnp.arange(half, dtype=jnp.int32),
                (1 - side) * half + jnp.arange(half, dtype=jnp.int32),
            ]
        )
        segment, position, live_groups = layout(group_lengths, slot_ids)

        def to_groups(arr):
            tail = arr.shape[1:]
            arr = arr.reshape((2, 2, 2, half) + tail)
            return jnp.swapaxes(arr, 1, 2).reshape((SHARE, rows) + tail)

        def from_groups(arr):
            tail = arr.shape[2:]
            arr = arr.reshape((2, 2, 2, half) + tail)
            return jnp.swapaxes(arr, 1, 2).reshape((8 * half,) + tail)

        live_all = from_groups(live_groups)
        all_heads = buckets[:, 0]
        all_widths = buckets[:, 1]

        own_tokens = rel_tokens[:half].astype(wide)
        own_heads = all_heads[:half]
        own_widths = all_widths[:half]
        own_live = live_all[:half]

        block_in = all_tokens.astype(wide)
        hidden_heads = norm_piece(block_in, norm_gains[0]).astype(low)
        own_normed, norm_heads_back = jax.vjp(norm_piece, own_tokens, norm_gains[0])
        gate_heads, route_heads_back = jax.vjp(
            partial(route_piece, bucket=own_heads),
            own_normed.astype(low).astype(wide),
            router_first[0],
            router_second[0],
        )
        head_ids = side * (local_width // HD) + share * heads + jnp.arange(heads, dtype=jnp.int32)
        head_used = head_ids[None, :] < HEADS // NB * (all_heads[:, None] + 1)
        unit_ids = side * local_units + share * units + jnp.arange(units, dtype=jnp.int32)
        unit_used = unit_ids[None, :] < FF // NB * (all_widths[:, None] + 1)

        half_dim = HD // 2
        frequency = theta_base ** (-2.0 * jnp.arange(half_dim, dtype=wide) / HD)
        angles = position.astype(wide)[:, :, None] * frequency
        cosine = jnp.cos(angles)[:, :, None, :]
        sine_table = jnp.sin(angles)[:, :, None, :]
        qkv_all = to_groups(dot(hidden_heads, qkv_full).reshape(8 * half, 3, heads, HD))
        query = rotate(qkv_all[:, :, 0], cosine, sine_table).astype(low)
        keyed = rotate(qkv_all[:, :, 1], cosine, sine_table).astype(low)
        value = qkv_all[:, :, 2].astype(low)
        group_used = to_groups(head_used)
        same_seq = segment[:, :, None] == segment[:, None, :]
        causal = slot_ids[None, :] <= slot_ids[:, None]
        diagonal = slot_ids[None, :] == slot_ids[:, None]
        key_used = jnp.swapaxes(group_used, 1, 2)
        allowed = (same_seq & causal)[:, None] & (key_used[:, :, None, :] | diagonal)
        scale = HD ** (-0.5)
        scores = jnp.einsum("gqhe,gkhe->ghqk", query, keyed, preferred_element_type=wide) * scale
        scores = jnp.where(allowed, scores, -1e30)
        row_top = jnp.max(scores, axis=-1, keepdims=True)
        weights = jnp.exp(scores - row_top)
        probs = weights / jnp.sum(weights, axis=-1, keepdims=True)
        probs_low = probs.astype(low)
        mixed = jnp.einsum("ghqk,gkhe->gqhe", probs_low, value, preferred_element_type=wide)
        mixed = jnp.where(group_used[..., None], mixed, 0.0).astype(low)
        attended = from_groups(mixed).reshape(8 * half, head_width)

        def partial_rows(left_in, matrix, product):
            keep = product(left_in[: 4 * half], matrix)
            send = product(left_in[4 * half :], matrix)
            return reduce_rows(keep, send)

        projected = partial_rows(attended, out_full, dot)

        middle = own_tokens + gate_heads[:, None] * projected
        normed_units, norm_units_back = jax.vjp(norm_piece, middle, norm_gains[1])
        own_units = normed_units.astype(low)
        hidden_units = gather_halves(own_units)
        gate_units, route_units_back = jax.vjp(
            partial(route_piece, bucket=own_widths),
            own_units.astype(wide),
            router_first[1],
            router_second[1],
        )
        all_gates = gather_halves(gate_units[:, None])
        upward = dot(hidden_units, up_full)
        activated = jnp.where(unit_used, jnp.square(jax.nn.relu(upward)), 0.0).astype(low)
        grad_top_all = jnp.where(live_all[:, None], all_cot.astype(wide), 0.0)
        grad_down_in = (all_gates * grad_top_all).astype(low)

        def down_term(at, s):
            mid = units // 2
            return dot_rows(
                activated[:, s * mid : (s + 1) * mid],
                lax.dynamic_slice_in_dim(grad_down_in, at * block, block, 1),
            )

        grad_down = scatter_back(ring_reduce(down_term), 1)

        downward = partial_rows(activated, down_full, dot)
        own_out = jnp.where(
            own_live[:, None], middle + gate_units[:, None] * downward, 0.0
        ).astype(low)
        block_out = whole_rows(own_out)
        grad_top = jnp.where(own_live[:, None], rel_cot[:half].astype(wide), 0.0)
        grad_gate_units = jnp.sum(grad_top * downward, axis=1)

        grad_act = dot_cols(grad_down_in, down_full)
        grad_up_in = jnp.where(unit_used, 2.0 * jax.nn.relu(upward) * grad_act, 0.0).astype(low)

        def up_term(at, s):
            mid = block // 2
            return dot_rows(
                lax.dynamic_slice_in_dim(hidden_units, at * block + s * mid, mid, 1), grad_up_in
            )

        grad_up = scatter_back(ring_reduce(up_term), 0)
        route_units_grads = route_units_back(grad_gate_units)
        grad_hidden_units = partial_rows(grad_up_in, up_full, dot_cols) + route_units_grads[0]
        norm_units_grads = norm_units_back(grad_hidden_units)
        grad_middle = grad_top + norm_units_grads[0]
        grad_gate_heads = jnp.sum(grad_middle * projected, axis=1)
        grad_projected = gather_halves((gate_heads[:, None] * grad_middle).astype(low))

        def out_term(at, s):
            mid = head_width // 2
            return dot_rows(
                attended[:, s * mid : (s + 1) * mid],
                lax.dynamic_slice_in_dim(grad_projected, at * block, block, 1),
            )

        grad_out = scatter_back(ring_reduce(out_term), 1)
        grad_attended = to_groups(
            dot_cols(grad_projected, out_full).astype(low).reshape(8 * half, heads, HD)
        )
        grad_attended = jnp.where(group_used[..., None], grad_attended, jnp.zeros((), low))
        grad_value = jnp.einsum(
            "ghqk,gqhe->gkhe", probs_low, grad_attended, preferred_element_type=wide
        )
        grad_probs = jnp.einsum(
            "gqhe,gkhe->ghqk", grad_attended, value, preferred_element_type=wide
        )
        row_dot = jnp.sum(probs * grad_probs, axis=-1, keepdims=True)
        grad_scores = (probs * (grad_probs - row_dot)).astype(low)
        grad_query = (
            jnp.einsum("ghqk,gkhe->gqhe", grad_scores, keyed, preferred_element_type=wide) * scale
        )
        grad_keyed = (
            jnp.einsum("ghqk,gqhe->gkhe", grad_scores, query, preferred_element_type=wide) * scale
        )
        grad_qkv_in = jnp.stack(
            [
                rotate(grad_query, cosine, -sine_table),
                rotate(grad_keyed, cosine, -sine_table),
                grad_value,
            ],
            axis=2,
        ).astype(low)
        grad_qkv_in = from_groups(grad_qkv_in).reshape(8 * half, 3 * head_width)

        def qkv_term(at, s):
            mid = block // 2
            return dot_rows(
                lax.dynamic_slice_in_dim(hidden_heads, at * block + s * mid, mid, 1), grad_qkv_in
            )

        qkv_parts = ring_reduce(qkv_term)
        joined = jnp.concatenate(qkv_parts, axis=0)
        grad_qkv = jnp.zeros((owned, 3, local_width), wide)
        for bits in range(SHARE):
            piece = lax.dynamic_slice_in_dim(joined, (share ^ bits) * owned, owned, 0)
            if bits:
                piece = hop(piece.astype(low), bits).astype(wide)
            grad_qkv = lax.dynamic_update_slice_in_dim(
                grad_qkv, piece.reshape(owned, 3, head_width), (share ^ bits) * head_width, 2
            )

        route_heads_grads = route_heads_back(grad_gate_heads)
        grad_hidden_heads = partial_rows(grad_qkv_in, qkv_full, dot_cols) + route_heads_grads[0]
        norm_heads_grads = norm_heads_back(grad_hidden_heads)
        input_grad = whole_rows((grad_middle + norm_heads_grads[0]).astype(low))

        def total_small(arr):
            arr = arr + cross(arr)
            bits = 1
            while bits < fsdp:
                arr = arr + hop(arr, bits)
                bits *= 2
            return arr

        def total_large(arr):
            steps = [1, "tensor"] + [2**i for i in range(1, fsdp.bit_length() - 1)]
            for bits in steps:
                mid = arr.shape[0] // 2
                me = side if bits == "tensor" else (rank // bits) % 2
                send = lax.dynamic_slice_in_dim(arr, (1 - me) * mid, mid, 0)
                keep = lax.dynamic_slice_in_dim(arr, me * mid, mid, 0)
                arr = keep + (cross(send) if bits == "tensor" else hop(send, bits))
            for bits in reversed(steps):
                me = side if bits == "tensor" else (rank // bits) % 2
                other = cross(arr) if bits == "tensor" else hop(arr, bits)
                arr = jnp.where(
                    me == 0,
                    jnp.concatenate([arr, other], axis=0),
                    jnp.concatenate([other, arr], axis=0),
                )
            return arr

        bucket_ids = jnp.arange(NB, dtype=jnp.int32)[None, :]
        head_counts = jnp.sum(
            jnp.where(own_live[:, None] & (own_heads[:, None] == bucket_ids), 1.0, 0.0), axis=0
        )
        width_counts = jnp.sum(
            jnp.where(own_live[:, None] & (own_widths[:, None] == bucket_ids), 1.0, 0.0), axis=0
        )
        units_small = total_small(
            jnp.concatenate(
                [norm_units_grads[1], route_units_grads[2].reshape(-1), head_counts, width_counts]
            )
        )
        heads_small = total_small(
            jnp.concatenate([norm_heads_grads[1], route_heads_grads[2].reshape(-1)])
        )
        first_units = total_large(route_units_grads[1])
        first_heads = total_large(route_heads_grads[1])
        second_shape = router_second.shape[1:]
        second_size = second_shape[0] * second_shape[1]
        grad_gains = jnp.stack([heads_small[:width], units_small[:width]])
        grad_second = jnp.stack(
            [
                heads_small[width : width + second_size].reshape(second_shape),
                units_small[width : width + second_size].reshape(second_shape),
            ]
        )
        usage = units_small[width + second_size :].reshape(2, NB)
        grad_first = jnp.stack([first_heads, first_units])
        return (
            block_out,
            input_grad,
            grad_gains,
            grad_qkv,
            grad_out,
            grad_up,
            grad_down,
            grad_first,
            grad_second,
            usage,
        )

    in_specs = (
        P("fsdp", None),
        P("fsdp"),
        P("fsdp"),
        P("fsdp", None),
        P(),
        P("fsdp", None, "tensor"),
        P("tensor", "fsdp"),
        P("fsdp", "tensor"),
        P("tensor", "fsdp"),
        P(),
        P(),
        P("fsdp", None),
    )
    out_specs = (
        P("fsdp", None),
        P("fsdp", None),
        P(),
        P("fsdp", None, "tensor"),
        P("tensor", "fsdp"),
        P("fsdp", "tensor"),
        P("tensor", "fsdp"),
        P(),
        P(),
        P(),
    )
    return jax.shard_map(shards, mesh=mesh, in_specs=in_specs, out_specs=out_specs, check_vma=False)
```

time: 1920 us -> 868 us (0.45)
  waiting for transfers between devices: 1630 us -> 517 us
  starting transfers between devices: 1.98 us -> 75.7 us
  local copies, waits for them, and re-layouts: 23.5 us -> 88.1 us
  blocking collectives: 62.3 us -> 0 us
  matrix products: 152 us -> 99 us
  other arithmetic: 22.2 us -> 74.3 us
    reduce_scatter x4 -> x0, waiting for transfers between devices: 1030 us -> none  [the longest x1 337 us: shards(): lax.psum_scatter(grad_down_local, 'fsdp', scatter_dimension=1, tiled=True)]
    ppermute x0 -> x133, waiting for transfers between devices: none -> 517 us  [the longest x48 316 us: ring(): lax.ppermute(moved, 'fsdp', [(i, (i + SHARE) % fsdp) for i in range(fsdp)])]
    all_gather x4 -> x0, waiting for transfers between devices: 392 us -> none  [the longest x1 125 us: shards(): lax.all_gather(up_weight, 'fsdp', axis=0, tiled=True)]
    psum x5 -> x0, waiting for transfers between devices: 207 us -> none  [the longest x4 167 us: tensor_total(): return lax.psum(local_term, 'tensor')]
    ppermute x0 -> x133, starting transfers between devices: none -> 75.7 us  [the longest x70 48.2 us: hop(): return lax.ppermute(moved, 'fsdp', [(i, i ^ bits) for i in range(fsdp)])]
    psum x1 -> x0, blocking collectives: 62.3 us -> none  [shards(): lax.psum((gain_local, first_local, second_local, usage_local), 'fsdp')]
    dot_general x18 -> x49, matrix products: 126 us -> 80.1 us  [the longest x32 27 us: dot_rows(): lax.dot_general(left_in, right_in, (((0,), (0,)), ((), ())), preferred_el...]
  transfers between devices with their start and end apart: 13 -> 133, of which waited for: 12 -> 78; matrix products, arithmetic and copies ran while one was open for 6% -> 25% of each run, Pallas kernels for 0% -> 0%
where the time goes in v1:
time: 868 us; the launch traced here: 858 us
  waiting for transfers between devices  517 us (60%)
  matrix products  99 us (11%)
  local copies, waits for them, and re-layouts  88.1 us (10%)
  starting transfers between devices  75.7 us (9%)
  other arithmetic  74.3 us (9%)
    ppermute x48, waiting for transfers between devices, ring(): lax.ppermute(moved, 'fsdp', [(i, (i + SHARE) % fsdp) for i in range(fsdp)])  316 us
    ppermute x70, waiting for transfers between devices, hop(): return lax.ppermute(moved, 'fsdp', [(i, i ^ bits) for i in range(fsdp)])  132 us
    ppermute x15, waiting for transfers between devices, cross(): return lax.ppermute(moved, 'tensor', [(0, 1), (1, 0)])  69.4 us
    ppermute x70, starting transfers between devices, hop(): return lax.ppermute(moved, 'fsdp', [(i, i ^ bits) for i in range(fsdp)])  48.2 us
    dot_general x32, matrix products, dot_rows(): lax.dot_general(left_in, right_in, (((0,), (0,)), ((), ())), preferred_el...  27 us
    dot_general x6, matrix products, dot(): return jnp.dot(left_in, right_in, preferred_element_type=wide)  26.8 us
    unnamed x255, local copies, waits for them, and re-layouts  22.1 us
    dot_general x6, matrix products, dot_cols(): lax.dot_general(left_in, right_in, (((1,), (1,)), ((), ())), preferred_el...  19.8 us
  transfers between devices with their start and end apart: 133, of which 78 were waited for; matrix products, arithmetic and copies ran while one was open for 25% of the time, Pallas kernels for 0%

profile of v1, /device:TPU:0, one launch (start us, length us, event | category | flops | bytes accessed | tf_op | source)
XLA Modules:
  0.0 858.4 jit_solution(9867622703227753469)
XLA Ops:
  14.2 25.0 %collective-permute-done = s32[1,2]{0,1:T(2,128)S(1)} collective-permute-done((s32[1,2]{0,1:T(2,128)S(1)}, s32[1,2]{0,1:T(2,128)S(1)}, u32[]{:S(2)}, u32[]{:S(2)}) %collective-permute-start) | collective-permute-done | bytes 40 | tf_op jit(solution)/shard_map/ppermute | solution.py:85
  64.6 10.5 %collective-permute-done.9 = bf16[256,768]{0,1:T(8,128)(2,1)S(1)} collective-permute-done((bf16[256,768]{0,1:T(8,128)(2,1)S(1)}, bf16[256,768]{0,1:T(8,128)(2,1)S(1)}, u32[]{:S(2)}, u32[]{:S(2)}) %collective-permute-start.9) | collective-permute-done | bytes 393248 | tf_op jit(solution)/shard_map/ppermute | solution.py:123
  75.1 8.4 collective-permute-done.10
  85.3 6.6 collective-permute-done.11
  91.9 8.4 collective-permute-done.12
  101.6 13.6 %collective-permute-done.14 = bf16[256,768]{0,1:T(8,128)(2,1)S(1)} collective-permute-done((bf16[256,768]{0,1:T(8,128)(2,1)S(1)}, bf16[256,768]{0,1:T(8,128)(2,1)S(1)}, u32[]{:S(2)}, u32[]{:S(2)}) %collective-permute-start.14) | collective-permute-done | bytes 393248 | tf_op jit(solution)/shard_map/ppermute | solution.py:123
  116.7 6.8 collective-permute-done.18
  123.5 6.7 collective-permute-done.20
  143.7 5.1 fusion.282
  148.8 5.4 reshape_reshape.12
  185.8 18.7 %collective-permute-done.25 = bf16[256,2048]{1,0:T(8,128)(2,1)S(1)} collective-permute-done((bf16[256,2048]{1,0:T(8,128)(2,1)S(1)}, bf16[256,2048]{1,0:T(8,128)(2,1)S(1)}, u32[]{:S(2)}, u32[]{:S(2)}) %collective-permute-start.25) | collective-permute-done | bytes 1048608 | tf_op jit(solution)/shard_map/ppermute | solution.py:88
  207.8 11.1 %collective-permute-done.26 = bf16[128,2048]{1,0:T(8,128)(2,1)S(1)} collective-permute-done((bf16[128,2048]{1,0:T(8,128)(2,1)S(1)}, bf16[128,2048]{1,0:T(8,128)(2,1)S(1)}, u32[]{:S(2)}, u32[]{:S(2)}) %collective-permute-start.26) | collective-permute-done | bytes 524320 | tf_op jit(solution)/shard_map/ppermute | solution.py:85
  224.4 11.2 %collective-permute-done.34 = bf16[256,1024]{1,0:T(8,128)(2,1)S(1)} collective-permute-done((bf16[256,1024]{1,0:T(8,128)(2,1)S(1)}, bf16[256,1024]{1,0:T(8,128)(2,1)S(1)}, u32[]{:S(2)}, u32[]{:S(2)}) %collective-permute-start.34) | collective-permute-done | bytes 524320 | tf_op jit(solution)/shard_map/ppermute | solution.py:123
  237.2 9.7 %collective-permute-done.35 = bf16[256,1024]{1,0:T(8,128)(2,1)S(1)} collective-permute-done((bf16[256,1024]{1,0:T(8,128)(2,1)S(1)}, bf16[256,1024]{1,0:T(8,128)(2,1)S(1)}, u32[]{:S(2)}, u32[]{:S(2)}) %collective-permute-start.35) | collective-permute-done | bytes 524320 | tf_op jit(solution)/shard_map/ppermute | solution.py:123
  247.8 8.8 %collective-permute-done.36 = bf16[256,1024]{1,0:T(8,128)(2,1)S(1)} collective-permute-done((bf16[256,1024]{1,0:T(8,128)(2,1)S(1)}, bf16[256,1024]{1,0:T(8,128)(2,1)S(1)}, u32[]{:S(2)}, u32[]{:S(2)}) %collective-permute-start.36) | collective-permute-done | bytes 524320 | tf_op jit(solution)/shard_map/ppermute | solution.py:123
  258.6 14.7 %collective-permute-done.37 = bf16[256,1024]{1,0:T(8,128)(2,1)S(1)} collective-permute-done((bf16[256,1024]{1,0:T(8,128)(2,1)S(1)}, bf16[256,1024]{1,0:T(8,128)(2,1)S(1)}, u32[]{:S(2)}, u32[]{:S(2)}) %collective-permute-start.37) | collective-permute-done | bytes 524320 | tf_op jit(solution)/shard_map/ppermute | solution.py:123
  273.3 11.2 %collective-permute-done.38 = bf16[256,1024]{1,0:T(8,128)(2,1)S(1)} collective-permute-done((bf16[256,1024]{1,0:T(8,128)(2,1)S(1)}, bf16[256,1024]{1,0:T(8,128)(2,1)S(1)}, u32[]{:S(2)}, u32[]{:S(2)}) %collective-permute-start.38) | collective-permute-done | bytes 524320 | tf_op jit(solution)/shard_map/ppermute | solution.py:123
  290.0 5.9 collective-permute-done.42
  297.9 9.2 %collective-permute-done.43 = bf16[512,512]{1,0:T(8,128)(2,1)} collective-permute-done((bf16[512,512]{1,0:T(8,128)(2,1)}, bf16[512,512]{1,0:T(8,128)(2,1)}, u32[]{:S(2)}, u32[]{:S(2)}) %collective-permute-start.43) | collective-permute-done | bytes 524320 | tf_op jit(solution)/shard_map/ppermute | solution.py:123
  311.6 6.7 collective-permute-done.44
  319.1 10.4 %collective-permute-done.45 = bf16[512,512]{1,0:T(8,128)(2,1)S(1)} collective-permute-done((bf16[512,512]{1,0:T(8,128)(2,1)}, bf16[512,512]{1,0:T(8,128)(2,1)S(1)}, u32[]{:S(2)}, u32[]{:S(2)}) %collective-permute-start.45) | collective-permute-done | bytes 524320 | tf_op jit(solution)/shard_map/ppermute | solution.py:123
  331.9 8.8 %collective-permute-done.46 = bf16[512,512]{1,0:T(8,128)(2,1)S(1)} collective-permute-done((bf16[512,512]{1,0:T(8,128)(2,1)S(1)}, bf16[512,512]{1,0:T(8,128)(2,1)S(1)}, u32[]{:S(2)}, u32[]{:S(2)}) %collective-permute-start.46) | collective-permute-done | bytes 524320 | tf_op jit(solution)/shard_map/ppermute | solution.py:123
  340.8 8.8 %collective-permute-done.47 = bf16[512,512]{1,0:T(8,128)(2,1)S(1)} collective-permute-done((bf16[512,512]{1,0:T(8,128)(2,1)S(1)}, bf16[512,512]{1,0:T(8,128)(2,1)S(1)}, u32[]{:S(2)}, u32[]{:S(2)}) %collective-permute-start.47) | collective-permute-done | bytes 524320 | tf_op jit(solution)/shard_map/ppermute | solution.py:123
  349.7 8.1 fusion.4
  367.2 5.5 convert_add_fusion.2
  380.4 17.6 %collective-permute-done.49 = bf16[256,2048]{1,0:T(8,128)(2,1)S(1)} collective-permute-done((bf16[256,2048]{1,0:T(8,128)(2,1)S(1)}, bf16[256,2048]{1,0:T(8,128)(2,1)S(1)}, u32[]{:S(2)}, u32[]{:S(2)}) %collective-permute-start.49) | collective-permute-done | bytes 1048608 | tf_op jit(solution)/shard_map/ppermute | solution.py:88
  402.7 8.8 %collective-permute-done.50 = bf16[128,2048]{1,0:T(8,128)(2,1)S(1)} collective-permute-done((bf16[128,2048]{1,0:T(8,128)(2,1)S(1)}, bf16[128,2048]{1,0:T(8,128)(2,1)S(1)}, u32[]{:S(2)}, u32[]{:S(2)}) %collective-permute-start.50) | collective-permute-done | bytes 524320 | tf_op jit(solution)/shard_map/ppermute | solution.py:85
  439.4 14.9 %collective-permute-done.89 = bf16[512,512]{1,0:T(8,128)(2,1)S(1)} collective-permute-done((bf16[512,512]{1,0:T(8,128)(2,1)S(1)}, bf16[512,512]{1,0:T(8,128)(2,1)S(1)}, u32[]{:S(2)}, u32[]{:S(2)}) %collective-permute-start.89) | collective-permute-done | bytes 524320 | tf_op jit(solution)/shard_map/ppermute | solution.py:123
  455.4 10.2 %collective-permute-done.77 = bf16[512,512]{1,0:T(8,128)(2,1)S(1)} collective-permute-done((bf16[512,512]{1,0:T(8,128)(2,1)S(1)}, bf16[512,512]{1,0:T(8,128)(2,1)S(1)}, u32[]{:S(2)}, u32[]{:S(2)}) %collective-permute-start.77) | collective-permute-done | bytes 524320 | tf_op jit(solution)/shard_map/ppermute | solution.py:123
  467.6 9.2 %collective-permute-done.90 = bf16[512,512]{1,0:T(8,128)(2,1)S(1)} collective-permute-done((bf16[512,512]{1,0:T(8,128)(2,1)S(1)}, bf16[512,512]{1,0:T(8,128)(2,1)S(1)}, u32[]{:S(2)}, u32[]{:S(2)}) %collective-permute-start.90) | collective-permute-done | bytes 524320 | tf_op jit(solution)/shard_map/ppermute | solution.py:123
  477.6 10.4 %collective-permute-done.78 = bf16[512,512]{1,0:T(8,128)(2,1)S(1)} collective-permute-done((bf16[512,512]{1,0:T(8,128)(2,1)S(1)}, bf16[512,512]{1,0:T(8,128)(2,1)S(1)}, u32[]{:S(2)}, u32[]{:S(2)}) %collective-permute-start.78) | collective-permute-done | bytes 524320 | tf_op jit(solution)/shard_map/ppermute | solution.py:123
  490.5 8.8 %collective-permute-done.91 = bf16[512,512]{1,0:T(8,128)(2,1)S(1)} collective-permute-done((bf16[512,512]{1,0:T(8,128)(2,1)S(1)}, bf16[512,512]{1,0:T(8,128)(2,1)S(1)}, u32[]{:S(2)}, u32[]{:S(2)}) %collective-permute-start.91) | collective-permute-done | bytes 524320 | tf_op jit(solution)/shard_map/ppermute | solution.py:123
  500.0 10.0 %collective-permute-done.79 = bf16[512,512]{1,0:T(8,128)(2,1)S(1)} collective-permute-done((bf16[512,512]{1,0:T(8,128)(2,1)S(1)}, bf16[512,512]{1,0:T(8,128)(2,1)S(1)}, u32[]{:S(2)}, u32[]{:S(2)}) %collective-permute-start.79) | collective-permute-done | bytes 524320 | tf_op jit(solution)/shard_map/ppermute | solution.py:123
  515.9 14.4 %collective-permute-done.126 = f32[128,256]{1,0:T(8,128)S(1)} collective-permute-done((f32[128,256]{1,0:T(8,128)S(1)}, f32[128,256]{1,0:T(8,128)S(1)}, u32[]{:S(2)}, u32[]{:S(2)}) %collective-permute-start.126) | collective-permute-done | bytes 131104 | tf_op jit(solution)/shard_map/ppermute | solution.py:85
  539.2 13.8 %collective-permute-done.128 = f32[64,256]{1,0:T(8,128)S(1)} collective-permute-done((f32[64,256]{1,0:T(8,128)S(1)}, f32[64,256]{1,0:T(8,128)S(1)}, u32[]{:S(2)}, u32[]{:S(2)}) %collective-permute-start.128) | collective-permute-done | bytes 65568 | tf_op jit(solution)/shard_map/ppermute | solution.py:85
  562.4 7.9 collective-permute-done.59
  583.9 6.7 collective-permute-done.131
  592.0 13.3 %collective-permute-done.82 = bf16[256,1024]{1,0:T(8,128)(2,1)S(1)} collective-permute-done((bf16[256,1024]{1,0:T(8,128)(2,1)S(1)}, bf16[256,1024]{1,0:T(8,128)(2,1)S(1)}, u32[]{:S(2)}, u32[]{:S(2)}) %collective-permute-start.82) | collective-permute-done | bytes 524320 | tf_op jit(solution)/shard_map/ppermute | solution.py:123
  612.5 8.5 collective-permute-done.60
  634.8 10.1 %collective-permute-done.72 = f32[3080]{0:T(1024)S(1)} collective-permute-done((f32[3080]{0:T(1024)}, f32[3080]{0:T(1024)S(1)}, u32[]{:S(2)}, u32[]{:S(2)}) %collective-permute-start.72) | collective-permute-done | bytes 12352 | tf_op jit(solution)/shard_map/ppermute | solution.py:88
  686.5 5.9 collective-permute-done.121
  727.6 5.4 convolution_convert_fusion.3
  746.9 6.5 collective-permute-done.96
  755.2 5.4 collective-permute-done.97
  769.6 8.4 collective-permute-done.98
  778.7 7.7 collective-permute-done.86
  795.6 7.7 collective-permute-done.87
  804.2 7.5 collective-permute-done.100
  (800 shorter events, 389.7 us)
Async XLA Ops:
  2.9 54.7 %collective-permute-start.6 = (bf16[128,768]{0,1:T(8,128)(2,1)}, bf16[128,768]{0,1:T(8,128)(2,1)}, u32[]{:S(2)}, u32[]{:S(2)}) collective-permute-start(bf16[128,768]{0,1:T(8,128)(2,1)} %bitcast.10), channel_id=1, source_target_pairs={{0,2},{2,0},{4,6},{6,4},{8,10},{10,8},{12,14},{14,12},{16,18},{18,... | collective-permute-start | bytes 589832 | tf_op jit(solution)/shard_map/ppermute | solution.py:85
  4.2 54.5 %collective-permute-start.7 = (bf16[128,768]{0,1:T(8,128)(2,1)}, bf16[128,768]{0,1:T(8,128)(2,1)}, u32[]{:S(2)}, u32[]{:S(2)}) collective-permute-start(bf16[128,768]{0,1:T(8,128)(2,1)} %bitcast.11), channel_id=1, source_target_pairs={{0,4},{2,6},{4,0},{6,2},{8,12},{10,14},{12,8},{14,10},{16,20},{18,... | collective-permute-start | bytes 589832 | tf_op jit(solution)/shard_map/ppermute | solution.py:85
  7.5 52.1 %collective-permute-start.8 = (bf16[128,768]{0,1:T(8,128)(2,1)}, bf16[128,768]{0,1:T(8,128)(2,1)}, u32[]{:S(2)}, u32[]{:S(2)}) collective-permute-start(bf16[128,768]{0,1:T(8,128)(2,1)} %bitcast.12), channel_id=1, source_target_pairs={{0,6},{2,4},{4,2},{6,0},{8,14},{10,12},{12,10},{14,8},{16,22},{18,... | collective-permute-start | bytes 589832 | tf_op jit(solution)/shard_map/ppermute | solution.py:85
  9.4 74.1 %collective-permute-start.4 = (bf16[256,2048]{1,0:T(8,128)(2,1)}, bf16[256,2048]{1,0:T(8,128)(2,1)}, u32[]{:S(2)}, u32[]{:S(2)}) collective-permute-start(bf16[256,2048]{1,0:T(8,128)(2,1)} %pad_maximum_fusion.7), channel_id=1, source_target_pairs={{0,4},{2,6},{4,0},{6,2},{8,12},{10,14},{12,8},{14,10},{16,20},{18,... | collective-permute-start | bytes 3145736 | tf_op jit(solution)/shard_map/ppermute | solution.py:85
  11.3 28.0 %collective-permute-start = (s32[1,2]{0,1:T(2,128)S(1)}, s32[1,2]{0,1:T(2,128)S(1)}, u32[]{:S(2)}, u32[]{:S(2)}) collective-permute-start(s32[1,2]{0,1:T(2,128)S(1)} %copy.139), channel_id=1, source_target_pairs={{0,4},{2,6},{4,0},{6,2},{8,12},{10,14},{12,8},{14,10},{16,20},{18,... | collective-permute-start | bytes 32 | tf_op jit(solution)/shard_map/ppermute | solution.py:85
  85.2 54.3 %collective-permute-start.5 = (bf16[512,2048]{1,0:T(8,128)(2,1)S(1)}, bf16[512,2048]{1,0:T(8,128)(2,1)S(1)}, u32[]{:S(2)}, u32[]{:S(2)}) collective-permute-start(bf16[512,2048]{1,0:T(8,128)(2,1)S(1)} %pad_maximum_fusion.3), channel_id=1, source_target_pairs={{0,2},{2,0},{4,6},{6,4},{8,10},{10,8},{12,14},{14,12},{16,18},{18,... | collective-permute-start | bytes 6291464 | tf_op jit(solution)/shard_map/ppermute | solution.py:85
  91.9 23.3 %collective-permute-start.13 = (bf16[256,768]{0,1:T(8,128)(2,1)S(1)}, bf16[256,768]{0,1:T(8,128)(2,1)S(1)}, u32[]{:S(2)}, u32[]{:S(2)}) collective-permute-start(bf16[256,768]{0,1:T(8,128)(2,1)S(1)} %collective-permute-done.11), channel_id=1, source_target_pairs={{0,8},{2,10},{4,12},{6,14},{8,16},{10,18},{12,20},{14,22},{16,24},... | collective-permute-start | bytes 1179656 | tf_op jit(solution)/shard_map/ppermute | solution.py:123
  179.2 25.3 %collective-permute-start.25 = (bf16[256,2048]{1,0:T(8,128)(2,1)S(1)}, bf16[256,2048]{1,0:T(8,128)(2,1)S(1)}, u32[]{:S(2)}, u32[]{:S(2)}) collective-permute-start(bf16[256,2048]{1,0:T(8,128)(2,1)S(1)} %slice.550), channel_id=1, source_target_pairs={{0,1},{1,0},{2,3},{3,2},{4,5},{5,4},{6,7},{7,6},{8,9},{9,8},{10,11... | collective-permute-start | bytes 3145736 | tf_op jit(solution)/shard_map/ppermute | solution.py:88
  207.7 27.9 %collective-permute-start.34 = (bf16[256,1024]{1,0:T(8,128)(2,1)S(1)}, bf16[256,1024]{1,0:T(8,128)(2,1)S(1)}, u32[]{:S(2)}, u32[]{:S(2)}) collective-permute-start(bf16[256,1024]{1,0:T(8,128)(2,1)S(1)} %get-tuple-element.67), channel_id=1, source_target_pairs={{0,8},{2,10},{4,12},{6,14},{8,16},{10,18},{12,20},{14,22},{16,24},... | collective-permute-start | bytes 1572872 | tf_op jit(solution)/shard_map/ppermute | solution.py:123
  224.4 22.5 %collective-permute-start.35 = (bf16[256,1024]{1,0:T(8,128)(2,1)S(1)}, bf16[256,1024]{1,0:T(8,128)(2,1)S(1)}, u32[]{:S(2)}, u32[]{:S(2)}) collective-permute-start(bf16[256,1024]{1,0:T(8,128)(2,1)S(1)} %collective-permute-done.33), channel_id=1, source_target_pairs={{0,8},{2,10},{4,12},{6,14},{8,16},{10,18},{12,20},{14,22},{16,24},... | collective-permute-start | bytes 1572872 | tf_op jit(solution)/shard_map/ppermute | solution.py:123
  235.6 21.0 %collective-permute-start.36 = (bf16[256,1024]{1,0:T(8,128)(2,1)S(1)}, bf16[256,1024]{1,0:T(8,128)(2,1)S(1)}, u32[]{:S(2)}, u32[]{:S(2)}) collective-permute-start(bf16[256,1024]{1,0:T(8,128)(2,1)S(1)} %collective-permute-done.34), channel_id=1, source_target_pairs={{0,8},{2,10},{4,12},{6,14},{8,16},{10,18},{12,20},{14,22},{16,24},... | collective-permute-start | bytes 1572872 | tf_op jit(solution)/shard_map/ppermute | solution.py:123
  235.7 49.2 %collective-permute-start.28 = (bf16[256,2048]{1,0:T(8,128)(2,1)S(1)}, bf16[256,2048]{1,0:T(8,128)(2,1)S(1)}, u32[]{:S(2)}, u32[]{:S(2)}) collective-permute-start(bf16[256,2048]{1,0:T(8,128)(2,1)S(1)} %pad_maximum_fusion.8), channel_id=1, source_target_pairs={{0,1},{1,0},{2,3},{3,2},{4,5},{5,4},{6,7},{7,6},{8,9},{9,8},{10,11... | collective-permute-start | bytes 3145736 | tf_op jit(solution)/shard_map/ppermute | solution.py:88
  256.6 27.9 %collective-permute-start.38 = (bf16[256,1024]{1,0:T(8,128)(2,1)S(1)}, bf16[256,1024]{1,0:T(8,128)(2,1)S(1)}, u32[]{:S(2)}, u32[]{:S(2)}) collective-permute-start(bf16[256,1024]{1,0:T(8,128)(2,1)S(1)} %collective-permute-done.36), channel_id=1, source_target_pairs={{0,8},{2,10},{4,12},{6,14},{8,16},{10,18},{12,20},{14,22},{16,24},... | collective-permute-start | bytes 1572872 | tf_op jit(solution)/shard_map/ppermute | solution.py:123
  273.3 22.6 %collective-permute-start.42 = (bf16[512,512]{1,0:T(8,128)(2,1)}, bf16[512,512]{1,0:T(8,128)(2,1)}, u32[]{:S(2)}, u32[]{:S(2)}) collective-permute-start(bf16[512,512]{1,0:T(8,128)(2,1)} %get-tuple-element.72), channel_id=1, source_target_pairs={{0,8},{2,10},{4,12},{6,14},{8,16},{10,18},{12,20},{14,22},{16,24},... | collective-permute-start | bytes 1572872 | tf_op jit(solution)/shard_map/ppermute | solution.py:123
  284.5 22.6 %collective-permute-start.43 = (bf16[512,512]{1,0:T(8,128)(2,1)}, bf16[512,512]{1,0:T(8,128)(2,1)}, u32[]{:S(2)}, u32[]{:S(2)}) collective-permute-start(bf16[512,512]{1,0:T(8,128)(2,1)} %get-tuple-element.73), channel_id=1, source_target_pairs={{0,8},{2,10},{4,12},{6,14},{8,16},{10,18},{12,20},{14,22},{16,24},... | collective-permute-start | bytes 1572872 | tf_op jit(solution)/shard_map/ppermute | solution.py:123
  286.5 63.1 %collective-permute-start.29 = (bf16[512,2048]{1,0:T(8,128)(2,1)}, bf16[512,2048]{1,0:T(8,128)(2,1)}, u32[]{:S(2)}, u32[]{:S(2)}) collective-permute-start(bf16[512,2048]{1,0:T(8,128)(2,1)} %pad_maximum_fusion.4), channel_id=1, source_target_pairs={{0,2},{2,0},{4,6},{6,4},{8,10},{10,8},{12,14},{14,12},{16,18},{18,... | collective-permute-start | bytes 6291464 | tf_op jit(solution)/shard_map/ppermute | solution.py:85
  287.6 73.9 %collective-permute-start.55 = (bf16[256,2048]{1,0:T(8,128)(2,1)}, bf16[256,2048]{1,0:T(8,128)(2,1)}, u32[]{:S(2)}, u32[]{:S(2)}) collective-permute-start(bf16[256,2048]{1,0:T(8,128)(2,1)} %pad_maximum_fusion.9), channel_id=1, source_target_pairs={{0,4},{2,6},{4,0},{6,2},{8,12},{10,14},{12,8},{14,10},{16,20},{18,... | collective-permute-start | bytes 3145736 | tf_op jit(solution)/shard_map/ppermute | solution.py:85
  295.9 22.4 %collective-permute-start.44 = (bf16[512,512]{1,0:T(8,128)(2,1)}, bf16[512,512]{1,0:T(8,128)(2,1)S(1)}, u32[]{:S(2)}, u32[]{:S(2)}) collective-permute-start(bf16[512,512]{1,0:T(8,128)(2,1)} %collective-permute-done.42), channel_id=1, source_target_pairs={{0,8},{2,10},{4,12},{6,14},{8,16},{10,18},{12,20},{14,22},{16,24},... | collective-permute-start | bytes 1572872 | tf_op jit(solution)/shard_map/ppermute | solution.py:123
  307.1 22.4 %collective-permute-start.45 = (bf16[512,512]{1,0:T(8,128)(2,1)}, bf16[512,512]{1,0:T(8,128)(2,1)S(1)}, u32[]{:S(2)}, u32[]{:S(2)}) collective-permute-start(bf16[512,512]{1,0:T(8,128)(2,1)} %collective-permute-done.43), channel_id=1, source_target_pairs={{0,8},{2,10},{4,12},{6,14},{8,16},{10,18},{12,20},{14,22},{16,24},... | collective-permute-start | bytes 1572872 | tf_op jit(solution)/shard_map/ppermute | solution.py:123
  318.2 22.5 %collective-permute-start.46 = (bf16[512,512]{1,0:T(8,128)(2,1)S(1)}, bf16[512,512]{1,0:T(8,128)(2,1)S(1)}, u32[]{:S(2)}, u32[]{:S(2)}) collective-permute-start(bf16[512,512]{1,0:T(8,128)(2,1)S(1)} %collective-permute-done.44), channel_id=1, source_target_pairs={{0,8},{2,10},{4,12},{6,14},{8,16},{10,18},{12,20},{14,22},{16,24},... | collective-permute-start | bytes 1572872 | tf_op jit(solution)/shard_map/ppermute | solution.py:123
  372.9 25.1 %collective-permute-start.49 = (bf16[256,2048]{1,0:T(8,128)(2,1)S(1)}, bf16[256,2048]{1,0:T(8,128)(2,1)S(1)}, u32[]{:S(2)}, u32[]{:S(2)}) collective-permute-start(bf16[256,2048]{1,0:T(8,128)(2,1)S(1)} %slice.549), channel_id=1, source_target_pairs={{0,1},{1,0},{2,3},{3,2},{4,5},{5,4},{6,7},{7,6},{8,9},{9,8},{10,11... | collective-permute-start | bytes 3145736 | tf_op jit(solution)/shard_map/ppermute | solution.py:88
  423.0 43.3 %collective-permute-start.123 = (f32[1024,256]{1,0:T(8,128)}, f32[1024,256]{1,0:T(8,128)S(1)}, u32[]{:S(2)}, u32[]{:S(2)}) collective-permute-start(f32[1024,256]{1,0:T(8,128)} %constant_dynamic-slice_fusion.6), channel_id=1, source_target_pairs={{0,2},{2,0},{4,6},{6,4},{8,10},{10,8},{12,14},{14,12},{16,18},{18,... | collective-permute-start | bytes 3145736 | tf_op jit(solution)/shard_map/ppermute | solution.py:85
  437.7 75.7 %collective-permute-start.57 = (bf16[512,2048]{1,0:T(8,128)(2,1)S(1)}, bf16[512,2048]{1,0:T(8,128)(2,1)S(1)}, u32[]{:S(2)}, u32[]{:S(2)}) collective-permute-start(bf16[512,2048]{1,0:T(8,128)(2,1)S(1)} %convolution_convert_fusion), channel_id=1, source_target_pairs={{0,2},{2,0},{4,6},{6,4},{8,10},{10,8},{12,14},{14,12},{16,18},{18,... | collective-permute-start | bytes 6291464 | tf_op jit(solution)/shard_map/ppermute | solution.py:85
  437.8 27.7 %collective-permute-start.77 = (bf16[512,512]{1,0:T(8,128)(2,1)S(1)}, bf16[512,512]{1,0:T(8,128)(2,1)S(1)}, u32[]{:S(2)}, u32[]{:S(2)}) collective-permute-start(bf16[512,512]{1,0:T(8,128)(2,1)S(1)} %convolution_convert_fusion.8), channel_id=1, source_target_pairs={{0,8},{2,10},{4,12},{6,14},{8,16},{10,18},{12,20},{14,22},{16,24},... | collective-permute-start | bytes 1572872 | tf_op jit(solution)/shard_map/ppermute | solution.py:123
  455.1 21.7 %collective-permute-start.90 = (bf16[512,512]{1,0:T(8,128)(2,1)S(1)}, bf16[512,512]{1,0:T(8,128)(2,1)S(1)}, u32[]{:S(2)}, u32[]{:S(2)}) collective-permute-start(bf16[512,512]{1,0:T(8,128)(2,1)S(1)} %add_convert_fusion.1), channel_id=1, source_target_pairs={{0,8},{2,10},{4,12},{6,14},{8,16},{10,18},{12,20},{14,22},{16,24},... | collective-permute-start | bytes 1572872 | tf_op jit(solution)/shard_map/ppermute | solution.py:123
  466.3 21.7 %collective-permute-start.78 = (bf16[512,512]{1,0:T(8,128)(2,1)S(1)}, bf16[512,512]{1,0:T(8,128)(2,1)S(1)}, u32[]{:S(2)}, u32[]{:S(2)}) collective-permute-start(bf16[512,512]{1,0:T(8,128)(2,1)S(1)} %add_convert_fusion.3), channel_id=1, source_target_pairs={{0,8},{2,10},{4,12},{6,14},{8,16},{10,18},{12,20},{14,22},{16,24},... | collective-permute-start | bytes 1572872 | tf_op jit(solution)/shard_map/ppermute | solution.py:123
  466.6 22.3 %collective-permute-start.124 = (f32[512,256]{1,0:T(8,128)S(1)}, f32[512,256]{1,0:T(8,128)S(1)}, u32[]{:S(2)}, u32[]{:S(2)}) collective-permute-start(f32[512,256]{1,0:T(8,128)S(1)} %constant_dynamic-slice_fusion.5), channel_id=1, source_target_pairs={{0,1},{1,0},{2,3},{3,2},{4,5},{5,4},{6,7},{7,6},{8,9},{9,8},{10,11... | collective-permute-start | bytes 1572872 | tf_op jit(solution)/shard_map/ppermute | solution.py:88
  477.6 21.7 %collective-permute-start.91 = (bf16[512,512]{1,0:T(8,128)(2,1)S(1)}, bf16[512,512]{1,0:T(8,128)(2,1)S(1)}, u32[]{:S(2)}, u32[]{:S(2)}) collective-permute-start(bf16[512,512]{1,0:T(8,128)(2,1)S(1)} %add_convert_fusion), channel_id=1, source_target_pairs={{0,8},{2,10},{4,12},{6,14},{8,16},{10,18},{12,20},{14,22},{16,24},... | collective-permute-start | bytes 1572872 | tf_op jit(solution)/shard_map/ppermute | solution.py:123
  488.8 21.3 %collective-permute-start.79 = (bf16[512,512]{1,0:T(8,128)(2,1)S(1)}, bf16[512,512]{1,0:T(8,128)(2,1)S(1)}, u32[]{:S(2)}, u32[]{:S(2)}) collective-permute-start(bf16[512,512]{1,0:T(8,128)(2,1)S(1)} %add_convert_fusion.2), channel_id=1, source_target_pairs={{0,8},{2,10},{4,12},{6,14},{8,16},{10,18},{12,20},{14,22},{16,24},... | collective-permute-start | bytes 1572872 | tf_op jit(solution)/shard_map/ppermute | solution.py:123
  489.0 24.2 %collective-permute-start.125 = (f32[256,256]{1,0:T(8,128)S(1)}, f32[256,256]{1,0:T(8,128)S(1)}, u32[]{:S(2)}, u32[]{:S(2)}) collective-permute-start(f32[256,256]{1,0:T(8,128)S(1)} %constant_dynamic-slice_fusion.4), channel_id=1, source_target_pairs={{0,4},{2,6},{4,0},{6,2},{8,12},{10,14},{12,8},{14,10},{16,20},{18,... | collective-permute-start | bytes 786440 | tf_op jit(solution)/shard_map/ppermute | solution.py:85
  511.1 25.8 %collective-permute-start.111 = (bf16[1024,128]{1,0:T(8,128)(2,1)S(1)}, bf16[1024,128]{1,0:T(8,128)(2,1)S(1)}, u32[]{:S(2)}, u32[]{:S(2)}) collective-permute-start(bf16[1024,128]{1,0:T(8,128)(2,1)S(1)} %get-tuple-element.150), channel_id=1, source_target_pairs={{0,4},{2,6},{4,0},{6,2},{8,12},{10,14},{12,8},{14,10},{16,20},{18,... | collective-permute-start | bytes 786440 | tf_op jit(solution)/shard_map/ppermute | solution.py:85
  512.6 63.5 %collective-permute-start.112 = (bf16[1024,128]{1,0:T(8,128)(2,1)S(1)}, bf16[1024,128]{1,0:T(8,128)(2,1)S(1)}, u32[]{:S(2)}, u32[]{:S(2)}) collective-permute-start(bf16[1024,128]{1,0:T(8,128)(2,1)S(1)} %get-tuple-element.148), channel_id=1, source_target_pairs={{0,6},{2,4},{4,2},{6,0},{8,14},{10,12},{12,10},{14,8},{16,22},{18,... | collective-permute-start | bytes 786440 | tf_op jit(solution)/shard_map/ppermute | solution.py:85
  513.2 43.7 %collective-permute-start.92 = (bf16[256,1024]{1,0:T(8,128)(2,1)S(1)}, bf16[256,1024]{1,0:T(8,128)(2,1)S(1)}, u32[]{:S(2)}, u32[]{:S(2)}) collective-permute-start(bf16[256,1024]{1,0:T(8,128)(2,1)S(1)} %convolution_convert_fusion.4), channel_id=1, source_target_pairs={{0,8},{2,10},{4,12},{6,14},{8,16},{10,18},{12,20},{14,22},{16,24},... | collective-permute-start | bytes 1572872 | tf_op jit(solution)/shard_map/ppermute | solution.py:123
  530.4 24.6 %collective-permute-start.58 = (bf16[256,2048]{1,0:T(8,128)(2,1)S(1)}, bf16[256,2048]{1,0:T(8,128)(2,1)S(1)}, u32[]{:S(2)}, u32[]{:S(2)}) collective-permute-start(bf16[256,2048]{1,0:T(8,128)(2,1)S(1)} %slice.548), channel_id=1, source_target_pairs={{0,1},{1,0},{2,3},{3,2},{4,5},{5,4},{6,7},{7,6},{8,9},{9,8},{10,11... | collective-permute-start | bytes 3145736 | tf_op jit(solution)/shard_map/ppermute | solution.py:88
  536.9 21.1 %collective-permute-start.80 = (bf16[256,1024]{1,0:T(8,128)(2,1)S(1)}, bf16[256,1024]{1,0:T(8,128)(2,1)S(1)}, u32[]{:S(2)}, u32[]{:S(2)}) collective-permute-start(bf16[256,1024]{1,0:T(8,128)(2,1)S(1)} %convolution_convert_fusion.5), channel_id=1, source_target_pairs={{0,8},{2,10},{4,12},{6,14},{8,16},{10,18},{12,20},{14,22},{16,24},... | collective-permute-start | bytes 1572872 | tf_op jit(solution)/shard_map/ppermute | solution.py:123
  558.9 24.2 %collective-permute-start.81 = (bf16[256,1024]{1,0:T(8,128)(2,1)S(1)}, bf16[256,1024]{1,0:T(8,128)(2,1)S(1)}, u32[]{:S(2)}, u32[]{:S(2)}) collective-permute-start(bf16[256,1024]{1,0:T(8,128)(2,1)S(1)} %fusion.23), channel_id=1, source_target_pairs={{0,8},{2,10},{4,12},{6,14},{8,16},{10,18},{12,20},{14,22},{16,24},... | collective-permute-start | bytes 1572872 | tf_op jit(solution)/shard_map/ppermute | solution.py:123
  578.0 29.4 %collective-permute-start.94 = (bf16[256,1024]{1,0:T(8,128)(2,1)S(1)}, bf16[256,1024]{1,0:T(8,128)(2,1)S(1)}, u32[]{:S(2)}, u32[]{:S(2)}) collective-permute-start(bf16[256,1024]{1,0:T(8,128)(2,1)S(1)} %fusion.24), channel_id=1, source_target_pairs={{0,8},{2,10},{4,12},{6,14},{8,16},{10,18},{12,20},{14,22},{16,24},... | collective-permute-start | bytes 1572872 | tf_op jit(solution)/shard_map/ppermute | solution.py:123
  583.8 21.5 %collective-permute-start.82 = (bf16[256,1024]{1,0:T(8,128)(2,1)S(1)}, bf16[256,1024]{1,0:T(8,128)(2,1)S(1)}, u32[]{:S(2)}, u32[]{:S(2)}) collective-permute-start(bf16[256,1024]{1,0:T(8,128)(2,1)S(1)} %fusion.22), channel_id=1, source_target_pairs={{0,8},{2,10},{4,12},{6,14},{8,16},{10,18},{12,20},{14,22},{16,24},... | collective-permute-start | bytes 1572872 | tf_op jit(solution)/shard_map/ppermute | solution.py:123
  590.7 89.2 %collective-permute-start.132 = (f32[1024,256]{1,0:T(8,128)S(1)}, f32[1024,256]{1,0:T(8,128)}, u32[]{:S(2)}, u32[]{:S(2)}) collective-permute-start(f32[1024,256]{1,0:T(8,128)S(1)} %maximum_select_fusion.5), channel_id=1, source_target_pairs={{0,2},{2,0},{4,6},{6,4},{8,10},{10,8},{12,14},{14,12},{16,18},{18,... | collective-permute-start | bytes 3145736 | tf_op jit(solution)/shard_map/ppermute | solution.py:85
  609.6 23.4 %collective-permute-start.107 = (bf16[128,1024]{1,0:T(8,128)(2,1)S(1)}, bf16[128,1024]{1,0:T(8,128)(2,1)}, u32[]{:S(2)}, u32[]{:S(2)}) collective-permute-start(bf16[128,1024]{1,0:T(8,128)(2,1)S(1)} %get-tuple-element.152), channel_id=1, source_target_pairs={{0,2},{2,0},{4,6},{6,4},{8,10},{10,8},{12,14},{14,12},{16,18},{18,... | collective-permute-start | bytes 786440 | tf_op jit(solution)/shard_map/ppermute | solution.py:85
  609.6 42.3 %collective-permute-start.108 = (bf16[128,1024]{1,0:T(8,128)(2,1)}, bf16[128,1024]{1,0:T(8,128)(2,1)}, u32[]{:S(2)}, u32[]{:S(2)}) collective-permute-start(bf16[128,1024]{1,0:T(8,128)(2,1)} %get-tuple-element.153), channel_id=1, source_target_pairs={{0,4},{2,6},{4,0},{6,2},{8,12},{10,14},{12,8},{14,10},{16,20},{18,... | collective-permute-start | bytes 786440 | tf_op jit(solution)/shard_map/ppermute | solution.py:85
  622.1 24.5 %collective-permute-start.61 = (bf16[256,2048]{1,0:T(8,128)(2,1)}, bf16[256,2048]{1,0:T(8,128)(2,1)}, u32[]{:S(2)}, u32[]{:S(2)}) collective-permute-start(bf16[256,2048]{1,0:T(8,128)(2,1)} %pad_maximum_fusion.10), channel_id=1, source_target_pairs={{0,1},{1,0},{2,3},{3,2},{4,5},{5,4},{6,7},{7,6},{8,9},{9,8},{10,11... | collective-permute-start | bytes 3145736 | tf_op jit(solution)/shard_map/ppermute | solution.py:88
  651.8 41.6 %collective-permute-start.62 = (bf16[512,2048]{1,0:T(8,128)(2,1)}, bf16[512,2048]{1,0:T(8,128)(2,1)}, u32[]{:S(2)}, u32[]{:S(2)}) collective-permute-start(bf16[512,2048]{1,0:T(8,128)(2,1)} %pad_maximum_fusion.6), channel_id=1, source_target_pairs={{0,2},{2,0},{4,6},{6,4},{8,10},{10,8},{12,14},{14,12},{16,18},{18,... | collective-permute-start | bytes 6291464 | tf_op jit(solution)/shard_map/ppermute | solution.py:85
  693.4 70.8 %collective-permute-start.122 = (f32[1024,256]{1,0:T(8,128)}, f32[1024,256]{1,0:T(8,128)}, u32[]{:S(2)}, u32[]{:S(2)}) collective-permute-start(f32[1024,256]{1,0:T(8,128)} %maximum_select_fusion.4), channel_id=1, source_target_pairs={{0,2},{2,0},{4,6},{6,4},{8,10},{10,8},{12,14},{14,12},{16,18},{18,... | collective-permute-start | bytes 3145736 | tf_op jit(solution)/shard_map/ppermute | solution.py:85
  732.9 54.2 %collective-permute-start.63 = (bf16[512,2048]{1,0:T(8,128)(2,1)}, bf16[512,2048]{1,0:T(8,128)(2,1)}, u32[]{:S(2)}, u32[]{:S(2)}) collective-permute-start(bf16[512,2048]{1,0:T(8,128)(2,1)} %convolution_convert_fusion.3), channel_id=1, source_target_pairs={{0,2},{2,0},{4,6},{6,4},{8,10},{10,8},{12,14},{14,12},{16,18},{18,... | collective-permute-start | bytes 6291464 | tf_op jit(solution)/shard_map/ppermute | solution.py:85
  763.4 32.1 %collective-permute-start.106 = (bf16[256,128]{1,0:T(8,128)(2,1)S(1)}, bf16[256,128]{1,0:T(8,128)(2,1)S(1)}, u32[]{:S(2)}, u32[]{:S(2)}) collective-permute-start(bf16[256,128]{1,0:T(8,128)(2,1)S(1)} %get-tuple-element.200), channel_id=1, source_target_pairs={{0,6},{2,4},{4,2},{6,0},{8,14},{10,12},{12,10},{14,8},{16,22},{18,... | collective-permute-start | bytes 196616 | tf_op jit(solution)/shard_map/ppermute | solution.py:85
  790.7 24.1 %collective-permute-start.64 = (bf16[256,2048]{1,0:T(8,128)(2,1)S(1)}, bf16[256,2048]{1,0:T(8,128)(2,1)S(1)}, u32[]{:S(2)}, u32[]{:S(2)}) collective-permute-start(bf16[256,2048]{1,0:T(8,128)(2,1)S(1)} %slice.547), channel_id=1, source_target_pairs={{0,1},{1,0},{2,3},{3,2},{4,5},{5,4},{6,7},{7,6},{8,9},{9,8},{10,11... | collective-permute-start | bytes 3145736 | tf_op jit(solution)/shard_map/ppermute | solution.py:88
  822.8 22.1 %collective-permute-start.103 = (bf16[128,768]{1,0:T(8,128)(2,1)}, bf16[128,768]{1,0:T(8,128)(2,1)}, u32[]{:S(2)}, u32[]{:S(2)}) collective-permute-start(bf16[128,768]{1,0:T(8,128)(2,1)} %get-tuple-element.162), channel_id=1, source_target_pairs={{0,6},{2,4},{4,2},{6,0},{8,14},{10,12},{12,10},{14,8},{16,22},{18,... | collective-permute-start | bytes 589832 | tf_op jit(solution)/shard_map/ppermute | solution.py:85
  (206 other events, 3783.5 us)

commit v2 on v1

--- a/solution.py
+++ b/solution.py
@@ -3,6 +3,8 @@
 import jax
 import jax.numpy as jnp
 from jax import lax
+from jax.experimental import pallas as pl
+from jax.experimental.pallas import tpu as pltpu
 from jax.sharding import PartitionSpec as P
 
 HEADS = 16
@@ -16,6 +18,7 @@
 highest = lax.Precision.HIGHEST
 low = jnp.bfloat16
 wide = jnp.float32
+MESH = pl.DeviceIdType.MESH
 
 
 def norm_piece(values_in, gain_row):
@@ -77,7 +80,7 @@
     return segment, position, live_rows
 
 
-def solution(mesh):
+def general(mesh):
     fsdp = mesh.shape["fsdp"]
     ring_size = fsdp // SHARE
 
@@ -495,6 +498,877 @@
             usage,
         )
 
+    return shards
+
+
+def xor_one(index):
+    return index + 1 - 2 * (index % 2)
+
+
+class Plane:
+    def __init__(self):
+        self.rank = lax.axis_index("fsdp")
+        self.side = lax.axis_index("tensor")
+        self.share = self.rank % SHARE
+        self.place = self.rank // SHARE
+        core = xor_one(self.share)
+        mid = (self.share + 2) % SHARE
+        self.shares = [self.share, core, mid, SHARE - 1 - self.share]
+        self.core = {"fsdp": self.place * SHARE + core}
+        self.mid = {"fsdp": self.place * SHARE + mid}
+        self.both = {"fsdp": self.place * SHARE + self.shares[3]}
+        self.members = [None, self.core, self.mid, self.both]
+        self.across = {"tensor": 1 - self.side}
+        self.near_place = xor_one(self.place)
+        self.two_place = (self.place + 2) % 4
+        self.far_place = 3 - self.place
+        self.near = {"fsdp": self.near_place * SHARE + self.share}
+        self.two = {"fsdp": self.two_place * SHARE + self.share}
+        self.far = {"fsdp": self.far_place * SHARE + self.share}
+        self.inner = (self.place == 1) | (self.place == 2)
+        self.outer = (self.place == 0) | (self.place == 3)
+
+    def greet(self):
+        barrier = pltpu.get_barrier_semaphore()
+        peers = [self.core, self.mid, self.both, self.across, self.near, self.two, self.far]
+        for peer in peers:
+            pl.semaphore_signal(barrier, inc=1, device_id=peer, device_id_type=MESH)
+        pl.semaphore_wait(barrier, len(peers))
+
+
+class Copies:
+    def __init__(self, local_sems, send_sems, recv_sems):
+        self.local_sems, self.send_sems, self.recv_sems = local_sems, send_sems, recv_sems
+        self.locals, self.sends, self.recvs = 0, 0, 0
+
+    def local(self, src, dst):
+        copy = pltpu.make_async_copy(src, dst, self.local_sems.at[self.locals])
+        self.locals += 1
+        copy.start()
+        return copy
+
+    def slot(self):
+        self.recvs += 1
+        return self.recvs - 1
+
+    def remote(self, src, dst, peer, slot=None):
+        if slot is None:
+            slot = self.slot()
+        copy = pltpu.make_async_remote_copy(
+            src_ref=src,
+            dst_ref=dst,
+            send_sem=self.send_sems.at[self.sends],
+            recv_sem=self.recv_sems.at[slot],
+            device_id=peer,
+            device_id_type=MESH,
+        )
+        self.sends += 1
+        return copy
+
+    def push(self, src, dst, peer):
+        copy = self.remote(src, dst, peer)
+        copy.start()
+        return copy
+
+
+class ZGather:
+    def __init__(self, here, copies, view):
+        self.here, self.copies, self.view = here, copies, view
+
+    def start(self):
+        here, copies, view = self.here, self.copies, self.view
+        own = view(here.place)
+        self.two = copies.push(own, own, here.two)
+        self.near = copies.push(own, own, here.near)
+        slot = copies.slot()
+        self.far = copies.remote(own, own, here.far, slot)
+        pl.when(here.inner)(self.far.start)
+        passing = view(here.two_place)
+        self.passed = copies.remote(passing, passing, here.near, slot)
+        arriving = view(here.two_place), view(here.near_place), view(here.far_place)
+        self.arrivals = [
+            pltpu.make_async_remote_copy(
+                src_ref=dst,
+                dst_ref=dst,
+                send_sem=copies.send_sems.at[0],
+                recv_sem=copies.recv_sems.at[at],
+                device_id=here.two,
+                device_id_type=MESH,
+            )
+            for dst, at in zip(arriving, (slot - 2, slot - 1, slot))
+        ]
+
+    def forward(self):
+        self.arrivals[0].wait_recv()
+        pl.when(self.here.inner)(self.passed.start)
+
+    def arrive(self):
+        self.arrivals[1].wait_recv()
+        self.arrivals[2].wait_recv()
+
+    def drain(self):
+        self.two.wait_send()
+        self.near.wait_send()
+
+        @pl.when(self.here.inner)
+        def _():
+            self.far.wait_send()
+            self.passed.wait_send()
+
+
+def tiles(count, body):
+    def step(i, carry):
+        body(i)
+        return carry
+
+    lax.fori_loop(0, count, step, 0)
+
+
+def part(index, size):
+    return pl.ds(pl.multiple_of(index * size, size), size)
+
+
+class RowReduce:
+    def __init__(self, here, copies, bufs):
+        self.here, self.copies = here, copies
+        (self.snd, self.rcv, self.acc, self.out, self.into) = bufs
+
+    def core_send(self, index):
+        rows = pl.ds(index * 256, 256)
+        copy = self.copies.push(self.snd.at[rows], self.rcv.at[rows], self.here.core)
+        self.core = getattr(self, "core", []) + [copy]
+
+    def finish(self, add_core):
+        here, copies, acc, out, into = self.here, self.copies, self.acc, self.out, self.into
+        for copy in self.core:
+            copy.wait_recv()
+        add_core(pl.ds(384, 128))
+        out[384:512, :] = acc[384:512, :].astype(low)
+        diag_x = copies.push(out.at[384:448], into.at[384:448], here.across)
+        diag_y = copies.push(out.at[448:512], into.at[448:512], here.mid)
+        add_core(pl.ds(128, 256))
+        out[128:192, :] = acc[128:192, :].astype(low)
+        out[320:384, :] = acc[320:384, :].astype(low)
+        diag_y.wait_recv()
+        out[192:256, :] = (acc[192:256, :] + into[448:512, :].astype(wide)).astype(low)
+        over_x = copies.push(out.at[128:256], into.at[128:256], here.across)
+        diag_x.wait_recv()
+        out[256:320, :] = (acc[256:320, :] + into[384:448, :].astype(wide)).astype(low)
+        over_y = copies.push(out.at[256:384], into.at[256:384], here.mid)
+        add_core(pl.ds(0, 128))
+        over_x.wait_recv()
+        over_y.wait_recv()
+        self.sent = self.core + [diag_x, diag_y, over_x, over_y]
+        return (
+            acc[0:128, :] + into[128:256, :].astype(wide) + into[256:384, :].astype(wide)
+        )
+
+    def drain(self):
+        for copy in self.sent:
+            copy.wait_send()
+
+
+class RowGather:
+    def __init__(self, here, copies, buf):
+        self.here, self.copies, self.buf = here, copies, buf
+
+    def run(self):
+        here, copies, buf = self.here, self.copies, self.buf
+        own = buf.at[0:128]
+        over_x = copies.push(own, buf.at[128:256], here.across)
+        over_y = copies.push(own, buf.at[256:384], here.mid)
+        cores = [copies.push(own, buf.at[512:640], here.core)]
+        over_y.wait_recv()
+        diag_x = copies.push(buf.at[256:320], buf.at[384:448], here.across)
+        cores.append(copies.push(buf.at[256:384], buf.at[768:896], here.core))
+        over_x.wait_recv()
+        diag_y = copies.push(buf.at[192:256], buf.at[448:512], here.mid)
+        cores.append(copies.push(buf.at[128:256], buf.at[640:768], here.core))
+        diag_x.wait_recv()
+        diag_y.wait_recv()
+        cores.append(copies.push(buf.at[384:512], buf.at[896:1024], here.core))
+        self.sent = [over_x, over_y, diag_x, diag_y] + cores
+        for copy in cores:
+            copy.wait_recv()
+
+    def drain(self):
+        for copy in self.sent:
+            copy.wait_send()
+
+
+def nn(left_in, right_in):
+    return lax.dot_general(
+        left_in, right_in, (((1,), (0,)), ((), ())), preferred_element_type=wide
+    )
+
+
+def nt(left_in, right_in):
+    return lax.dot_general(
+        left_in, right_in, (((1,), (1,)), ((), ())), preferred_element_type=wide
+    )
+
+
+def tn(left_in, right_in):
+    return lax.dot_general(
+        left_in, right_in, (((0,), (0,)), ((), ())), preferred_element_type=wide
+    )
+
+
+def forward_kernel(
+    tok, col, row, qkvw, outw, upw, downw, gains, gate,
+    o_hid, o_qkv, o_probs, o_att, o_proj, o_mid, o_units, o_up, o_col, o_row,
+    o_wq, o_wo, o_wu, o_wd,
+    toks, hid, wq, wo, wu, wd, cols, rows_info, qkvb, probs, att,
+    snd, rcv, acc, out_buf, in_buf, proj, mid_buf, units, up,
+    local_sems, send_sems, recv_sems,
+):
+    here = Plane()
+    copies = Copies(local_sems, send_sems, recv_sems)
+    here.greet()
+    rank, share = here.rank, here.share
+    owned = 128
+    block = owned * SHARE
+    head_width = wo.shape[0]
+    unit_width = wu.shape[1]
+    own_rows = part(rank, owned)
+
+    def spread(src_of, dst):
+        got = []
+        for d in range(SHARE):
+            src = src_of(here.shares[d])
+            if d == 0:
+                got.append(copies.local(src, dst))
+            else:
+                got.append(copies.push(src, dst, here.members[d]))
+        return got
+
+    def landed(got):
+        got[0].wait()
+        for copy in got[1:]:
+            copy.wait_recv()
+
+    got_q = spread(lambda t: qkvw.at[:, :, part(t, head_width)], wq.at[:, own_rows, :])
+    own_tok = copies.local(tok, toks.at[0:256])
+    own_col = copies.local(col, cols.at[0:256])
+    own_row = copies.local(row, rows_info.at[0])
+    tok_mid = copies.push(tok, toks.at[256:512], here.mid)
+    tok_core = copies.push(tok, toks.at[512:768], here.core)
+    col_mid = copies.push(col, cols.at[256:512], here.mid)
+    col_core = copies.push(col, cols.at[512:768], here.core)
+    row_mid = copies.push(row, rows_info.at[1], here.mid)
+    row_core = copies.push(row, rows_info.at[2], here.core)
+    got_o = spread(lambda t: outw.at[part(t, head_width), :], wo.at[:, own_rows])
+    got_u = spread(lambda t: upw.at[:, part(t, unit_width)], wu.at[own_rows, :])
+    got_d = spread(lambda t: downw.at[part(t, unit_width), :], wd.at[:, own_rows])
+
+    def up_view(h):
+        return lambda k: wu.at[pl.ds(pl.multiple_of(k * block + h * 256, 256), 256), :]
+
+    def down_view(h):
+        return lambda k: wd.at[h * 512 : (h + 1) * 512, part(k, block)]
+
+    z_q = ZGather(here, copies, lambda k: wq.at[:, part(k, block), :])
+    z_o = ZGather(here, copies, lambda k: wo.at[:, part(k, block)])
+    z_u = [ZGather(here, copies, up_view(h)) for h in range(2)]
+    z_d = [ZGather(here, copies, down_view(h)) for h in range(2)]
+
+    landed(got_q)
+    z_q.start()
+    landed(got_o)
+    z_o.start()
+
+    def normalise(base, count):
+        def body(i):
+            at = pl.ds(pl.multiple_of(base + i * 64, 64), 64)
+            x = toks[at, :].astype(wide)
+            r = lax.rsqrt(jnp.mean(x * x, axis=-1, keepdims=True) + epsilon)
+            hid[at, :] = (x * r * gains[0:1, :]).astype(low)
+
+        tiles(count, body)
+
+    own_tok.wait()
+    normalise(0, 4)
+    tok_core.wait_recv()
+    normalise(512, 4)
+    tok_mid.wait_recv()
+    tok_fwd = copies.push(toks.at[256:512], toks.at[768:1024], here.core)
+    normalise(256, 4)
+    tok_fwd.wait_recv()
+    normalise(768, 4)
+    own_col.wait()
+    own_row.wait()
+    col_mid.wait_recv()
+    row_mid.wait_recv()
+    col_fwd = copies.push(cols.at[256:512], cols.at[768:1024], here.core)
+    row_fwd = copies.push(rows_info.at[1], rows_info.at[3], here.core)
+    col_core.wait_recv()
+    row_core.wait_recv()
+    col_fwd.wait_recv()
+    row_fwd.wait_recv()
+    outs = [copies.local(hid, o_hid), copies.local(cols, o_col), copies.local(rows_info, o_row)]
+
+    z_q.forward()
+    landed(got_u)
+    z_u[0].start()
+    z_q.arrive()
+    outs.append(copies.local(wq, o_wq))
+
+    for j in range(3):
+
+        def qkv_tile(i, j=j):
+            at = part(i, 512)
+            made = nn(hid[at, :], wq[j])
+            if j < 2:
+                cosine = cols[at, 0:HD]
+                sine = cols[at, HD : 2 * HD]
+                for h in range(head_width // HD):
+                    one = made[:, h * HD : (h + 1) * HD]
+                    turned = one * cosine + pltpu.roll(one, HD // 2, 1) * sine
+                    qkvb[at, j * head_width + h * HD : j * head_width + (h + 1) * HD] = (
+                        turned.astype(low)
+                    )
+            else:
+                qkvb[at, j * head_width : (j + 1) * head_width] = made.astype(low)
+
+        tiles(2, qkv_tile)
+    outs.append(copies.local(qkvb, o_qkv))
+
+    z_o.forward()
+    z_u[1].start()
+
+    first_head = here.side * (SHARE * head_width // HD) + share * (head_width // HD)
+    scale = HD ** (-0.5)
+    for h in range(head_width // HD):
+        head = (first_head + h).astype(wide)
+
+        def attend_group(g, h=h, head=head):
+            at = part(g, 256)
+            query = qkvb[at, h * HD : (h + 1) * HD]
+            keyed = qkvb[at, head_width + h * HD : head_width + (h + 1) * HD]
+            value = qkvb[at, 2 * head_width + h * HD : 2 * head_width + (h + 1) * HD]
+            seg_q = cols[at, 2 * HD : 2 * HD + 1]
+            slot_q = cols[at, 2 * HD + 1 : 2 * HD + 2]
+            bucket_q = cols[at, 2 * HD + 2 : 2 * HD + 3]
+            info = rows_info[g]
+            seg_k, slot_k, bucket_k = info[0:1, :], info[1:2, :], info[2:3, :]
+            reach_k = jnp.where(4.0 * bucket_k + 4.0 > head, 1.0, 0.0)
+            same = seg_q == seg_k
+            causal = slot_k <= slot_q
+            usable = (reach_k > 0.5) | (slot_k == slot_q)
+            scores = jnp.where(same & causal & usable, nt(query, keyed) * scale, -1e30)
+            top = jnp.max(scores, axis=-1, keepdims=True)
+            weights = jnp.exp(scores - top)
+            p = weights / jnp.sum(weights, axis=-1, keepdims=True)
+            probs[part(g * (head_width // HD) + h, 256), :] = p
+            mixed = nn(p.astype(low), value)
+            att[at, h * HD : (h + 1) * HD] = jnp.where(
+                4.0 * bucket_q + 4.0 > head, mixed, 0.0
+            ).astype(low)
+
+        tiles(SHARE, attend_group)
+    outs.append(copies.local(probs, o_probs))
+    outs.append(copies.local(att, o_att))
+
+    z_o.arrive()
+    outs.append(copies.local(wo, o_wo))
+
+    reduce = RowReduce(here, copies, (snd, rcv, acc, out_buf, in_buf))
+    for i in range(2):
+
+        def send_tile(n, i=i):
+            c = part(n, 512)
+            snd[i * 256 : (i + 1) * 256, c] = nn(
+                att[512 + i * 256 : 512 + (i + 1) * 256, :], wo[:, c]
+            ).astype(low)
+
+        tiles(4, send_tile)
+        reduce.core_send(i)
+
+    def keep_tile(n):
+        c = part(n, 512)
+        acc[:, c] = nn(att[0:512, :], wo[:, c])
+
+    tiles(4, keep_tile)
+
+    def add_core(at):
+        acc[at, :] = acc[at, :] + rcv[at, :].astype(wide)
+
+    z_u[0].forward()
+    landed(got_d)
+    z_d[0].start()
+    projected = reduce.finish(add_core)
+    proj[...] = projected
+    middle = toks[0:128, :].astype(wide) + gate[:, 0:1] * projected
+    mid_buf[...] = middle
+    r = lax.rsqrt(jnp.mean(middle * middle, axis=-1, keepdims=True) + epsilon)
+    units[0:128, :] = (middle * r * gains[1:2, :]).astype(low)
+    outs.append(copies.local(proj, o_proj))
+    outs.append(copies.local(mid_buf, o_mid))
+    gather = RowGather(here, copies, units)
+    gather.run()
+    outs.append(copies.local(units, o_units))
+
+    z_u[1].forward()
+    z_d[1].start()
+    z_u[0].arrive()
+    z_u[1].arrive()
+    outs.append(copies.local(wu, o_wu))
+
+    def up_tile(i):
+        at = part(i % 2, 512)
+        c = part(i // 2, 512)
+        up[at, c] = nn(units[at, :], wu[:, c])
+
+    tiles(unit_width // 256, up_tile)
+    outs.append(copies.local(up, o_up))
+    z_d[0].forward()
+    z_d[1].forward()
+    z_d[0].arrive()
+    z_d[1].arrive()
+    outs.append(copies.local(wd, o_wd))
+
+    for one in [z_q, z_o] + z_u + z_d + [reduce, gather]:
+        one.drain()
+    sent = [tok_mid, tok_core, tok_fwd, col_mid, col_core, row_mid, row_core, col_fwd, row_fwd]
+    for got in (got_q, got_o, got_u, got_d):
+        sent += got[1:]
+    for copy in sent:
+        copy.wait_send()
+    for copy in outs:
+        copy.wait()
+
+
+def plane(mesh):
+    fsdp = mesh.shape["fsdp"]
+    ring_size = fsdp // SHARE
+
+    def hop(moved, bits):
+        return lax.ppermute(moved, "fsdp", [(i, i ^ bits) for i in range(fsdp)])
+
+    def cross(moved):
+        return lax.ppermute(moved, "tensor", [(0, 1), (1, 0)])
+
+    def shards(
+        tokens,
+        head_bucket,
+        ffn_bucket,
+        lengths,
+        norm_gains,
+        qkv_weight,
+        out_weight,
+        up_weight,
+        down_weight,
+        router_first,
+        router_second,
+        cotangent,
+    ):
+        rows, width = tokens.shape
+        half = rows // 2
+        rank = lax.axis_index("fsdp")
+        side = lax.axis_index("tensor")
+        share = rank % SHARE
+        place = rank // SHARE
+        local_units = up_weight.shape[1]
+        units = local_units // SHARE
+        local_width = out_weight.shape[0]
+        head_width = local_width // SHARE
+        heads = head_width // HD
+        owned = width // fsdp
+        block = width // ring_size
+        plane_rows = SHARE * rows
+
+        def own_half(arr):
+            return lax.dynamic_slice_in_dim(arr, side * half, half, 0)
+
+        def relative(arr):
+            return jnp.concatenate(
+                [own_half(arr), lax.dynamic_slice_in_dim(arr, (1 - side) * half, half, 0)], axis=0
+            )
+
+        slot_ids = jnp.concatenate(
+            [
+                side * half + jnp.arange(half, dtype=jnp.int32),
+                (1 - side) * half + jnp.arange(half, dtype=jnp.int32),
+            ]
+        )
+        segment, position, live_rows = (a[0] for a in layout(lengths, slot_ids))
+        frequency = theta_base ** (-2.0 * jnp.arange(HD // 2, dtype=wide) / HD)
+        angles = position.astype(wide)[:, None] * frequency
+        cosine, sine = jnp.cos(angles), jnp.sin(angles)
+        rel_heads = relative(head_bucket)
+        rel_widths = relative(ffn_bucket)
+        facts = jnp.stack(
+            [segment, slot_ids, rel_heads, rel_widths, live_rows.astype(jnp.int32)], axis=1
+        ).astype(wide)
+        col = jnp.concatenate(
+            [cosine, cosine, -sine, sine, jnp.pad(facts, ((0, 0), (0, HD - facts.shape[1])))],
+            axis=1,
+        )
+        row = jnp.pad(facts.T, ((0, 8 - facts.shape[1]), (0, 0)))
+        rel_tokens = relative(tokens)
+        own_tokens = rel_tokens[:half].astype(wide)
+        own_heads, own_widths = rel_heads[:half], rel_widths[:half]
+        own_live = live_rows[:half]
+        own_normed, norm_heads_back = jax.vjp(norm_piece, own_tokens, norm_gains[0])
+        gate_heads, route_heads_back = jax.vjp(
+            partial(route_piece, bucket=own_heads),
+            own_normed.astype(low).astype(wide),
+            router_first[0],
+            router_second[0],
+        )
+        f32, b16 = jnp.float32, jnp.bfloat16
+
+        def shape(*dims):
+            return jax.ShapeDtypeStruct(dims[1:], dims[0])
+
+        anywhere = pl.BlockSpec(memory_space=pl.ANY)
+        vmem = pl.BlockSpec(memory_space=pltpu.VMEM)
+        weights = [
+            shape(b16, 3, width, head_width),
+            shape(b16, head_width, width),
+            shape(b16, width, units),
+            shape(b16, units, width),
+        ]
+        made = [
+            shape(b16, plane_rows, width),
+            shape(b16, plane_rows, 3 * head_width),
+            shape(f32, SHARE * heads * rows, rows),
+            shape(b16, plane_rows, head_width),
+            shape(f32, half, width),
+            shape(f32, half, width),
+            shape(b16, plane_rows, width),
+            shape(f32, plane_rows, units),
+            shape(f32, plane_rows, 3 * HD),
+            shape(f32, SHARE, 8, rows),
+        ]
+        (
+            hidden_heads,
+            qkvb,
+            probs,
+            attended,
+            projected,
+            middle,
+            hidden_units,
+            upward,
+            all_col,
+            all_row,
+            qkv_full,
+            out_full,
+            up_full,
+            down_full,
+        ) = pl.pallas_call(
+            forward_kernel,
+            out_shape=made + weights,
+            in_specs=[anywhere] * 7 + [vmem] * 2,
+            out_specs=[anywhere] * 14,
+            scratch_shapes=[
+                pltpu.VMEM((plane_rows, width), b16),
+                pltpu.VMEM((plane_rows, width), b16),
+                pltpu.VMEM((3, width, head_width), b16),
+                pltpu.VMEM((head_width, width), b16),
+                pltpu.VMEM((width, units), b16),
+                pltpu.VMEM((units, width), b16),
+                pltpu.VMEM((plane_rows, 3 * HD), f32),
+                pltpu.VMEM((SHARE, 8, rows), f32),
+                pltpu.VMEM((plane_rows, 3 * head_width), b16),
+                pltpu.VMEM((SHARE * heads * rows, rows), f32),
+                pltpu.VMEM((plane_rows, head_width), b16),
+                pltpu.VMEM((plane_rows // 2, width), b16),
+                pltpu.VMEM((plane_rows // 2, width), b16),
+                pltpu.VMEM((plane_rows // 2, width), f32),
+                pltpu.VMEM((plane_rows // 2, width), b16),
+                pltpu.VMEM((plane_rows // 2, width), b16),
+                pltpu.VMEM((half, width), f32),
+                pltpu.VMEM((half, width), f32),
+                pltpu.VMEM((plane_rows, width), b16),
+                pltpu.VMEM((plane_rows, units), f32),
+                pltpu.SemaphoreType.DMA((24,)),
+                pltpu.SemaphoreType.DMA((64,)),
+                pltpu.SemaphoreType.DMA((64,)),
+            ],
+            compiler_params=pltpu.CompilerParams(
+                collective_id=0, has_side_effects=True, vmem_limit_bytes=60 * 2**20
+            ),
+        )(
+            rel_tokens,
+            col,
+            row,
+            jnp.transpose(qkv_weight, (1, 0, 2)),
+            out_weight,
+            up_weight,
+            down_weight,
+            norm_gains,
+            jnp.broadcast_to(gate_heads[:, None], (half, HD)),
+        )
+        def gather_rows(arr):
+            pair = jnp.concatenate([arr, hop(arr, 2)], axis=0)
+            return jnp.concatenate([pair, hop(pair, 1)], axis=0)
+
+        def gather_halves(arr):
+            pair = jnp.concatenate([arr, cross(arr)], axis=0)
+            return gather_rows(pair)
+
+        def reduce_rows(keep, send):
+            total = keep + hop(send.astype(low), 1).astype(wide)
+            total = total.reshape(2, 2, half, width)
+            total = total[:, 0] + cross(total[:, 1].astype(low)).astype(wide)
+            return total[0] + hop(total[1].astype(low), 2).astype(wide)
+
+        def whole_rows(arr):
+            other = cross(arr)
+            return jnp.where(
+                side == 0,
+                jnp.concatenate([arr, other], axis=0),
+                jnp.concatenate([other, arr], axis=0),
+            )
+
+        def partial_rows(left_in, matrix, product):
+            keep = product(left_in[: 4 * half], matrix)
+            send = product(left_in[4 * half :], matrix)
+            return reduce_rows(keep, send)
+
+        chain = [None, None]
+
+        def ring(moved, stream):
+            if chain[stream] is not None:
+                moved, _ = lax.optimization_barrier((moved, chain[stream]))
+            got = lax.ppermute(
+                moved, "fsdp", [(i, (i + SHARE) % fsdp) for i in range(fsdp)]
+            )
+            chain[stream] = got
+            return got
+
+        def place_at(step):
+            return (place - step) % ring_size
+
+        def ring_reduce(term):
+            moving = [None, None]
+            for step in range(1, ring_size):
+                for s in range(2):
+                    piece = term(place_at(step), s)
+                    if moving[s] is not None:
+                        piece = piece + moving[s].astype(wide)
+                    moving[s] = piece.astype(low)
+                for s in range(2):
+                    moving[s] = ring(moving[s], s)
+            return [term(place, s) + moving[s].astype(wide) for s in range(2)]
+
+        def scatter_back(parts, axis):
+            joined = jnp.concatenate(parts, axis=0)
+            other = 1 - axis
+            out_dims = list(joined.shape)
+            out_dims[axis] = owned
+            stride = out_dims[other]
+            out_dims[other] *= SHARE
+            out = jnp.zeros(out_dims, wide)
+            for bits in range(SHARE):
+                piece = lax.dynamic_slice_in_dim(joined, (share ^ bits) * owned, owned, axis)
+                if bits:
+                    piece = hop(piece.astype(low), bits).astype(wide)
+                out = lax.dynamic_update_slice_in_dim(out, piece, (share ^ bits) * stride, other)
+            return out
+
+        all_cot = gather_rows(relative(cotangent))
+        own_units = hidden_units[:half]
+        _, norm_units_back = jax.vjp(norm_piece, middle, norm_gains[1])
+        gate_units, route_units_back = jax.vjp(
+            partial(route_piece, bucket=own_widths),
+            own_units.astype(wide),
+            router_first[1],
+            router_second[1],
+        )
+        all_gates = gather_halves(gate_units[:, None])
+        all_heads = all_col[:, 2 * HD + 2].astype(jnp.int32)
+        all_widths = all_col[:, 2 * HD + 3].astype(jnp.int32)
+        live_all = all_col[:, 2 * HD + 4] > 0.5
+        cosine = all_col[:, : HD // 2].reshape(SHARE, rows, 1, HD // 2)
+        sine_table = all_col[:, HD + HD // 2 : 2 * HD].reshape(SHARE, rows, 1, HD // 2)
+        head_ids = side * (local_width // HD) + share * heads + jnp.arange(heads, dtype=jnp.int32)
+        head_used = head_ids[None, :] < HEADS // NB * (all_heads[:, None] + 1)
+        group_used = head_used.reshape(SHARE, rows, heads)
+        unit_ids = side * local_units + share * units + jnp.arange(units, dtype=jnp.int32)
+        unit_used = unit_ids[None, :] < FF // NB * (all_widths[:, None] + 1)
+        scale = HD ** (-0.5)
+        probs = probs.reshape(SHARE, heads, rows, rows)
+        probs_low = probs.astype(low)
+        groups = qkvb.reshape(SHARE, rows, 3, heads, HD)
+        query, keyed, value = groups[:, :, 0], groups[:, :, 1], groups[:, :, 2]
+        qkv_mat = jnp.transpose(qkv_full, (1, 0, 2)).reshape(width, 3 * head_width)
+
+        def to_groups(arr):
+            return arr.reshape((SHARE, rows) + arr.shape[1:])
+
+        def from_groups(arr):
+            return arr.reshape((plane_rows,) + arr.shape[2:])
+
+        activated = jnp.where(unit_used, jnp.square(jax.nn.relu(upward)), 0.0).astype(low)
+        grad_top_all = jnp.where(live_all[:, None], all_cot.astype(wide), 0.0)
+        grad_down_in = (all_gates * grad_top_all).astype(low)
+
+        def down_term(at, s):
+            mid = units // 2
+            return dot_rows(
+                activated[:, s * mid : (s + 1) * mid],
+                lax.dynamic_slice_in_dim(grad_down_in, at * block, block, 1),
+            )
+
+        grad_down = scatter_back(ring_reduce(down_term), 1)
+
+        downward = partial_rows(activated, down_full, dot)
+        own_out = jnp.where(
+            own_live[:, None], middle + gate_units[:, None] * downward, 0.0
+        ).astype(low)
+        block_out = whole_rows(own_out)
+        grad_top = jnp.where(own_live[:, None], own_half(cotangent).astype(wide), 0.0)
+        grad_gate_units = jnp.sum(grad_top * downward, axis=1)
+
+        grad_act = dot_cols(grad_down_in, down_full)
+        grad_up_in = jnp.where(unit_used, 2.0 * jax.nn.relu(upward) * grad_act, 0.0).astype(low)
+
+        def up_term(at, s):
+            mid = block // 2
+            return dot_rows(
+                lax.dynamic_slice_in_dim(hidden_units, at * block + s * mid, mid, 1), grad_up_in
+            )
+
+        grad_up = scatter_back(ring_reduce(up_term), 0)
+        route_units_grads = route_units_back(grad_gate_units)
+        grad_hidden_units = partial_rows(grad_up_in, up_full, dot_cols) + route_units_grads[0]
+        norm_units_grads = norm_units_back(grad_hidden_units)
+        grad_middle = grad_top + norm_units_grads[0]
+        grad_gate_heads = jnp.sum(grad_middle * projected, axis=1)
+        grad_projected = gather_halves((gate_heads[:, None] * grad_middle).astype(low))
+
+        def out_term(at, s):
+            mid = head_width // 2
+            return dot_rows(
+                attended[:, s * mid : (s + 1) * mid],
+                lax.dynamic_slice_in_dim(grad_projected, at * block, block, 1),
+            )
+
+        grad_out = scatter_back(ring_reduce(out_term), 1)
+        grad_attended = to_groups(
+            dot_cols(grad_projected, out_full).astype(low).reshape(plane_rows, heads, HD)
+        )
+        grad_attended = jnp.where(group_used[..., None], grad_attended, jnp.zeros((), low))
+        grad_value = jnp.einsum(
+            "ghqk,gqhe->gkhe", probs_low, grad_attended, preferred_element_type=wide
+        )
+        grad_probs = jnp.einsum(
+            "gqhe,gkhe->ghqk", grad_attended, value, preferred_element_type=wide
+        )
+        row_dot = jnp.sum(probs * grad_probs, axis=-1, keepdims=True)
+        grad_scores = (probs * (grad_probs - row_dot)).astype(low)
+        grad_query = (
+            jnp.einsum("ghqk,gkhe->gqhe", grad_scores, keyed, preferred_element_type=wide) * scale
+        )
+        grad_keyed = (
+            jnp.einsum("ghqk,gqhe->gkhe", grad_scores, query, preferred_element_type=wide) * scale
+        )
+        grad_qkv_in = jnp.stack(
+            [
+                rotate(grad_query, cosine, -sine_table),
+                rotate(grad_keyed, cosine, -sine_table),
+                grad_value,
+            ],
+            axis=2,
+        ).astype(low)
+        grad_qkv_in = from_groups(grad_qkv_in).reshape(plane_rows, 3 * head_width)
+
+        def qkv_term(at, s):
+            mid = block // 2
+            return dot_rows(
+                lax.dynamic_slice_in_dim(hidden_heads, at * block + s * mid, mid, 1), grad_qkv_in
+            )
+
+        qkv_parts = ring_reduce(qkv_term)
+        joined = jnp.concatenate(qkv_parts, axis=0)
+        grad_qkv = jnp.zeros((owned, 3, local_width), wide)
+        for bits in range(SHARE):
+            piece = lax.dynamic_slice_in_dim(joined, (share ^ bits) * owned, owned, 0)
+            if bits:
+                piece = hop(piece.astype(low), bits).astype(wide)
+            grad_qkv = lax.dynamic_update_slice_in_dim(
+                grad_qkv, piece.reshape(owned, 3, head_width), (share ^ bits) * head_width, 2
+            )
+
+        route_heads_grads = route_heads_back(grad_gate_heads)
+        grad_hidden_heads = partial_rows(grad_qkv_in, qkv_mat, dot_cols) + route_heads_grads[0]
+        norm_heads_grads = norm_heads_back(grad_hidden_heads)
+        input_grad = whole_rows((grad_middle + norm_heads_grads[0]).astype(low))
+
+        def total_small(arr):
+            arr = arr + cross(arr)
+            bits = 1
+            while bits < fsdp:
+                arr = arr + hop(arr, bits)
+                bits *= 2
+            return arr
+
+        def total_large(arr):
+            steps = [1, "tensor"] + [2**i for i in range(1, fsdp.bit_length() - 1)]
+            for bits in steps:
+                mid = arr.shape[0] // 2
+                me = side if bits == "tensor" else (rank // bits) % 2
+                send = lax.dynamic_slice_in_dim(arr, (1 - me) * mid, mid, 0)
+                keep = lax.dynamic_slice_in_dim(arr, me * mid, mid, 0)
+                arr = keep + (cross(send) if bits == "tensor" else hop(send, bits))
+            for bits in reversed(steps):
+                me = side if bits == "tensor" else (rank // bits) % 2
+                other = cross(arr) if bits == "tensor" else hop(arr, bits)
+                arr = jnp.where(
+                    me == 0,
+                    jnp.concatenate([arr, other], axis=0),
+                    jnp.concatenate([other, arr], axis=0),
+                )
+            return arr
+
+        bucket_ids = jnp.arange(NB, dtype=jnp.int32)[None, :]
+        head_counts = jnp.sum(
+            jnp.where(own_live[:, None] & (own_heads[:, None] == bucket_ids), 1.0, 0.0), axis=0
+        )
+        width_counts = jnp.sum(
+            jnp.where(own_live[:, None] & (own_widths[:, None] == bucket_ids), 1.0, 0.0), axis=0
+        )
+        units_small = total_small(
+            jnp.concatenate(
+                [norm_units_grads[1], route_units_grads[2].reshape(-1), head_counts, width_counts]
+            )
+        )
+        heads_small = total_small(
+            jnp.concatenate([norm_heads_grads[1], route_heads_grads[2].reshape(-1)])
+        )
+        first_units = total_large(route_units_grads[1])
+        first_heads = total_large(route_heads_grads[1])
+        second_shape = router_second.shape[1:]
+        second_size = second_shape[0] * second_shape[1]
+        grad_gains = jnp.stack([heads_small[:width], units_small[:width]])
+        grad_second = jnp.stack(
+            [
+                heads_small[width : width + second_size].reshape(second_shape),
+                units_small[width : width + second_size].reshape(second_shape),
+            ]
+        )
+        usage = units_small[width + second_size :].reshape(2, NB)
+        grad_first = jnp.stack([first_heads, first_units])
+        return (
+            block_out,
+            input_grad,
+            grad_gains,
+            grad_qkv,
+            grad_out,
+            grad_up,
+            grad_down,
+            grad_first,
+            grad_second,
+            usage,
+        )
+
+    return shards
+
+
+def solution(mesh):
+    shards = plane(mesh) if mesh.shape["fsdp"] == 4 * SHARE else general(mesh)
     in_specs = (
         P("fsdp", None),
         P("fsdp"),
@@ -521,4 +1395,6 @@
         P(),
         P(),
     )
-    return jax.shard_map(shards, mesh=mesh, in_specs=in_specs, out_specs=out_specs, check_vma=False)
+    return jax.shard_map(
+        shards, mesh=mesh, in_specs=in_specs, out_specs=out_specs, check_vma=False
+    )

time: 868 us -> 817 us (0.941)
  Pallas kernels: 0 us -> 224 us
  waiting for transfers between devices: 517 us -> 298 us
  matrix products: 99 us -> 77.1 us
  starting transfers between devices: 75.7 us -> 53.8 us
  local copies, waits for them, and re-layouts: 88.1 us -> 70.2 us
    pallas_call x0 -> x1, Pallas kernels: none -> 224 us  [shards(): pl.pallas_call(forward_kernel, out_shape=made + weights, in_specs=[anywhe...]
    ppermute x48 -> x24, waiting for transfers between devices: 316 us -> 152 us  [ring(): lax.ppermute(moved, 'fsdp', [(i, (i + SHARE) % fsdp) for i in range(fsdp)])]
    ppermute x70 -> x48, waiting for transfers between devices: 132 us -> 81.9 us  [hop(): return lax.ppermute(moved, 'fsdp', [(i, i ^ bits) for i in range(fsdp)])]
    dot_general x6 -> x2, matrix products: 26.8 us -> 4.72 us  [dot(): return jnp.dot(left_in, right_in, preferred_element_type=wide)]
    ppermute x70 -> x48, starting transfers between devices: 48.2 us -> 31.4 us  [hop(): return lax.ppermute(moved, 'fsdp', [(i, i ^ bits) for i in range(fsdp)])]
    dynamic_update_slice x43 -> x0, local copies, waits for them, and re-layouts: 15.9 us -> none  [the longest x30 12.5 us: ring_gather(): out = lax.dynamic_update_slice(out, moving[s], at)]
    another operation x8 -> x3, local copies, waits for them, and re-layouts: 12.1 us -> 2.21 us  [the longest x2 2.18 us: to_groups(): return arr.reshape((SHARE, rows) + arr.shape[1:])]
    unnamed x255 -> x230, local copies, waits for them, and re-layouts: 22.1 us -> 15.4 us
  transfers between devices with their start and end apart: 133 -> 85, of which waited for: 78 -> 54; matrix products, arithmetic and copies ran while one was open for 25% -> 23% of each run, Pallas kernels for 0% -> 0%
where the time goes in v2:
time: 817 us; the launch traced here: 808 us
  waiting for transfers between devices  298 us (36%)
  Pallas kernels  224 us (27%)
  other arithmetic  81.8 us (10%)
  matrix products  77.1 us (9%)
  local copies, waits for them, and re-layouts  70.2 us (9%)
  starting transfers between devices  53.8 us (7%)
    pallas_call x1, Pallas kernels, shards(): pl.pallas_call(forward_kernel, out_shape=made + weights, in_specs=[anywhe...  224 us
    ppermute x24, waiting for transfers between devices, ring(): lax.ppermute(moved, 'fsdp', [(i, (i + SHARE) % fsdp) for i in range(fsdp)])  152 us
    ppermute x48, waiting for transfers between devices, hop(): return lax.ppermute(moved, 'fsdp', [(i, i ^ bits) for i in range(fsdp)])  81.9 us
    ppermute x13, waiting for transfers between devices, cross(): return lax.ppermute(moved, 'tensor', [(0, 1), (1, 0)])  64.3 us
    ppermute x48, starting transfers between devices, hop(): return lax.ppermute(moved, 'fsdp', [(i, i ^ bits) for i in range(fsdp)])  31.4 us
    dot_general x32, matrix products, dot_rows(): lax.dot_general(left_in, right_in, (((0,), (0,)), ((), ())), preferred_el...  30.9 us
    dot_general x6, matrix products, dot_cols(): lax.dot_general(left_in, right_in, (((1,), (1,)), ((), ())), preferred_el...  20 us
  transfers between devices with their start and end apart: 85, of which 54 were waited for; matrix products, arithmetic and copies ran while one was open for 23% of the time, Pallas kernels for 0%

profile of v2, /device:TPU:0, one launch (start us, length us, event | category | flops | bytes accessed | tf_op | source)
XLA Modules:
  0.0 808.0 jit_solution(3262023542378505423)
XLA Ops:
  11.6 223.5 %shard_map.195 = (bf16[1024,2048]{1,0:T(8,128)(2,1)}, bf16[1024,768]{1,0:T(8,128)(2,1)}, f32[2048,256]{1,0:T(8,128)}, bf16[1024,256]{1,0:T(8,128)(2,1)}, f32[128...) custom-call(bf16[256,2048]{1,0:T(8,128)(2,1)} %pad_maximum_fusion.4., ...), custom_call_target="tpu_custom_call" | custom-call | tf_op jit(solution)/shard_map/pallas_call | solution.py:1059
  237.1 3.0 fusion
  244.0 3.8 collective-permute-done
  256.4 21.4 %collective-permute-done.1 = bf16[2,128,2048]{2,1,0:T(8,128)(2,1)S(1)} collective-permute-done((bf16[2,128,2048]{2,1,0:T(8,128)(2,1)S(1)}, bf16[2,128,2048]{2,1,0:T(8,128)(2,1)S(1)}, u32[]{:S(2)}, u32[]{:S(2)}) %collective-permute-start.1) | collective-permute-done | bytes 1048608 | tf_op jit(solution)/shard_map/ppermute | solution.py:949
  280.8 12.4 %collective-permute-done.2 = bf16[128,2048]{1,0:T(8,128)(2,1)S(1)} collective-permute-done((bf16[128,2048]{1,0:T(8,128)(2,1)S(1)}, bf16[128,2048]{1,0:T(8,128)(2,1)S(1)}, u32[]{:S(2)}, u32[]{:S(2)}) %collective-permute-start.2) | collective-permute-done | bytes 524320 | tf_op jit(solution)/shard_map/ppermute | solution.py:946
  305.6 3.5 reshape.842
  312.5 5.5 collective-permute-done.76
  321.0 6.5 collective-permute-done.77
  327.8 5.2 collective-permute-done.78
  333.1 15.2 %collective-permute-done.7 = bf16[256,2048]{1,0:T(8,128)(2,1)S(1)} collective-permute-done((bf16[256,2048]{1,0:T(8,128)(2,1)S(1)}, bf16[256,2048]{1,0:T(8,128)(2,1)S(1)}, u32[]{:S(2)}, u32[]{:S(2)}) %collective-permute-start.7) | collective-permute-done | bytes 1048608 | tf_op jit(solution)/shard_map/ppermute | solution.py:946
  360.1 4.8 copy.121
  383.7 4.8 fusion.5
  392.1 3.7 collective-permute-done.83
  397.8 7.3 multiply_convert_fusion
  405.1 5.2 fusion.1
  417.2 10.5 %collective-permute-done.41 = bf16[512,512]{1,0:T(8,128)(2,1)S(1)} collective-permute-done((bf16[512,512]{1,0:T(8,128)(2,1)S(1)}, bf16[512,512]{1,0:T(8,128)(2,1)S(1)}, u32[]{:S(2)}, u32[]{:S(2)}) %collective-permute-start.41) | collective-permute-done | bytes 524320 | tf_op jit(solution)/shard_map/ppermute | solution.py:1135
  429.3 9.6 %collective-permute-done.29 = bf16[512,512]{1,0:T(8,128)(2,1)S(1)} collective-permute-done((bf16[512,512]{1,0:T(8,128)(2,1)S(1)}, bf16[512,512]{1,0:T(8,128)(2,1)S(1)}, u32[]{:S(2)}, u32[]{:S(2)}) %collective-permute-start.29) | collective-permute-done | bytes 524320 | tf_op jit(solution)/shard_map/ppermute | solution.py:1135
  439.8 10.4 %collective-permute-done.42 = bf16[512,512]{1,0:T(8,128)(2,1)S(1)} collective-permute-done((bf16[512,512]{1,0:T(8,128)(2,1)S(1)}, bf16[512,512]{1,0:T(8,128)(2,1)S(1)}, u32[]{:S(2)}, u32[]{:S(2)}) %collective-permute-start.42) | collective-permute-done | bytes 524320 | tf_op jit(solution)/shard_map/ppermute | solution.py:1135
  451.8 9.6 %collective-permute-done.30 = bf16[512,512]{1,0:T(8,128)(2,1)S(1)} collective-permute-done((bf16[512,512]{1,0:T(8,128)(2,1)S(1)}, bf16[512,512]{1,0:T(8,128)(2,1)S(1)}, u32[]{:S(2)}, u32[]{:S(2)}) %collective-permute-start.30) | collective-permute-done | bytes 524320 | tf_op jit(solution)/shard_map/ppermute | solution.py:1135
  462.7 10.0 %collective-permute-done.43 = bf16[512,512]{1,0:T(8,128)(2,1)S(1)} collective-permute-done((bf16[512,512]{1,0:T(8,128)(2,1)S(1)}, bf16[512,512]{1,0:T(8,128)(2,1)S(1)}, u32[]{:S(2)}, u32[]{:S(2)}) %collective-permute-start.43) | collective-permute-done | bytes 524320 | tf_op jit(solution)/shard_map/ppermute | solution.py:1135
  476.5 7.0 collective-permute-done.31
  489.0 11.3 %collective-permute-done.10 = bf16[2,128,2048]{2,1,0:T(8,128)(2,1)S(1)} collective-permute-done((bf16[2,128,2048]{2,1,0:T(8,128)(2,1)S(1)}, bf16[2,128,2048]{2,1,0:T(8,128)(2,1)S(1)}, u32[]{:S(2)}, u32[]{:S(2)}) %collective-permute-start.10) | collective-permute-done | bytes 1048608 | tf_op jit(solution)/shard_map/ppermute | solution.py:949
  501.8 13.4 %collective-permute-done.32 = bf16[256,1024]{1,0:T(8,128)(2,1)S(1)} collective-permute-done((bf16[256,1024]{1,0:T(8,128)(2,1)S(1)}, bf16[256,1024]{1,0:T(8,128)(2,1)S(1)}, u32[]{:S(2)}, u32[]{:S(2)}) %collective-permute-start.32) | collective-permute-done | bytes 524320 | tf_op jit(solution)/shard_map/ppermute | solution.py:1135
  523.1 9.5 %collective-permute-done.33 = bf16[256,1024]{1,0:T(8,128)(2,1)S(1)} collective-permute-done((bf16[256,1024]{1,0:T(8,128)(2,1)S(1)}, bf16[256,1024]{1,0:T(8,128)(2,1)S(1)}, u32[]{:S(2)}, u32[]{:S(2)}) %collective-permute-start.33) | collective-permute-done | bytes 524320 | tf_op jit(solution)/shard_map/ppermute | solution.py:1135
  533.4 10.4 %collective-permute-done.45 = bf16[256,1024]{1,0:T(8,128)(2,1)S(1)} collective-permute-done((bf16[256,1024]{1,0:T(8,128)(2,1)S(1)}, bf16[256,1024]{1,0:T(8,128)(2,1)S(1)}, u32[]{:S(2)}, u32[]{:S(2)}) %collective-permute-start.45) | collective-permute-done | bytes 524320 | tf_op jit(solution)/shard_map/ppermute | solution.py:1135
  547.2 7.9 collective-permute-done.34
  555.8 4.0 collective-permute-done.12
  560.8 6.3 collective-permute-done.66
  568.9 14.9 %collective-permute-done.67 = f32[256,256]{1,0:T(8,128)S(1)} collective-permute-done((f32[256,256]{1,0:T(8,128)S(1)}, f32[256,256]{1,0:T(8,128)S(1)}, u32[]{:S(2)}, u32[]{:S(2)}) %collective-permute-start.67) | collective-permute-done | bytes 262176 | tf_op jit(solution)/shard_map/ppermute | solution.py:946
  591.5 2.9 collective-permute-done.69
  618.5 3.3 fusion.9
  624.5 2.8 collective-permute-done.28
  630.1 3.0 maximum_select_fusion.2
  633.1 3.3 collective-permute-done.73
  636.4 2.8 maximum_select_fusion.4
  653.7 2.9 copy.127
  656.5 3.9 convert_element_type.389
  674.2 5.3 convolution_convert_fusion.2
  697.1 5.6 collective-permute-done.48
  704.5 5.5 collective-permute-done.49
  719.3 8.2 %collective-permute-done.50 = bf16[256,768]{1,0:T(8,128)(2,1)S(1)} collective-permute-done((bf16[256,768]{1,0:T(8,128)(2,1)S(1)}, bf16[256,768]{1,0:T(8,128)(2,1)S(1)}, u32[]{:S(2)}, u32[]{:S(2)}) %collective-permute-start.50) | collective-permute-done | bytes 393248 | tf_op jit(solution)/shard_map/ppermute | solution.py:1135
  728.2 7.7 collective-permute-done.38
  736.7 3.4 convert_add_fusion
  745.1 7.7 collective-permute-done.39
  753.5 7.7 collective-permute-done.52
  761.3 3.0 collective-permute-done.16
  775.9 4.7 collective-permute-done.17
  780.7 3.2 fusion.26
  (606 shorter events, 256.8 us)
Async XLA Ops:
  252.4 25.5 %collective-permute-start.1 = (bf16[2,128,2048]{2,1,0:T(8,128)(2,1)S(1)}, bf16[2,128,2048]{2,1,0:T(8,128)(2,1)S(1)}, u32[]{:S(2)}, u32[]{:S(2)}) collective-permute-start(bf16[2,128,2048]{2,1,0:T(8,128)(2,1)S(1)} %fusion.32), channel_id=1, source_target_pairs={{0,1},{1,0},{2,3},{3,2},{4,5},{5,4},{6,7},{7,6},{8,9},{9,8},{10,11... | collective-permute-start | bytes 3145736 | tf_op jit(solution)/shard_map/ppermute | solution.py:949
  303.9 14.2 %collective-permute-start.76 = (f32[512,256]{1,0:T(8,128)}, f32[512,256]{1,0:T(8,128)S(1)}, u32[]{:S(2)}, u32[]{:S(2)}) collective-permute-start(f32[512,256]{1,0:T(8,128)} %constant_dynamic-slice_fusion.3), channel_id=1, source_target_pairs={{0,1},{1,0},{2,3},{3,2},{4,5},{5,4},{6,7},{7,6},{8,9},{9,8},{10,11... | collective-permute-start | bytes 1572872 | tf_op jit(solution)/shard_map/ppermute | solution.py:949
  319.2 29.0 %collective-permute-start.7 = (bf16[256,2048]{1,0:T(8,128)(2,1)S(1)}, bf16[256,2048]{1,0:T(8,128)(2,1)S(1)}, u32[]{:S(2)}, u32[]{:S(2)}) collective-permute-start(bf16[256,2048]{1,0:T(8,128)(2,1)S(1)} %pad_maximum_fusion.5), channel_id=1, source_target_pairs={{0,4},{2,6},{4,0},{6,2},{8,12},{10,14},{12,8},{14,10},{16,20},{18,... | collective-permute-start | bytes 3145736 | tf_op jit(solution)/shard_map/ppermute | solution.py:946
  333.0 16.9 %collective-permute-start.79 = (f32[64,256]{1,0:T(8,128)S(1)}, f32[64,256]{1,0:T(8,128)S(1)}, u32[]{:S(2)}, u32[]{:S(2)}) collective-permute-start(f32[64,256]{1,0:T(8,128)S(1)} %constant_dynamic-slice_fusion), channel_id=1, source_target_pairs={{0,16},{2,18},{4,20},{6,22},{8,24},{10,26},{12,28},{14,30},{16,0},... | collective-permute-start | bytes 196616 | tf_op jit(solution)/shard_map/ppermute | solution.py:946
  349.9 47.8 %collective-permute-start.8 = (bf16[512,2048]{1,0:T(8,128)(2,1)}, bf16[512,2048]{1,0:T(8,128)(2,1)}, u32[]{:S(2)}, u32[]{:S(2)}) collective-permute-start(bf16[512,2048]{1,0:T(8,128)(2,1)} %pad_maximum_fusion.2), channel_id=1, source_target_pairs={{0,2},{2,0},{4,6},{6,4},{8,10},{10,8},{12,14},{14,12},{16,18},{18,... | collective-permute-start | bytes 6291464 | tf_op jit(solution)/shard_map/ppermute | solution.py:946
  350.6 14.3 %collective-permute-start.80 = (f32[64,256]{1,0:T(8,128)}, f32[64,256]{1,0:T(8,128)}, u32[]{:S(2)}, u32[]{:S(2)}) collective-permute-start(f32[64,256]{1,0:T(8,128)} %dynamic-slice_add_fusion.8), channel_id=1, source_target_pairs={{0,16},{2,18},{4,20},{6,22},{8,24},{10,26},{12,28},{14,30},{16,0},... | collective-permute-start | bytes 196616 | tf_op jit(solution)/shard_map/ppermute | solution.py:946
  397.6 86.9 %collective-permute-start.84 = (f32[1024,256]{1,0:T(8,128)S(1)}, f32[1024,256]{1,0:T(8,128)S(1)}, u32[]{:S(2)}, u32[]{:S(2)}) collective-permute-start(f32[1024,256]{1,0:T(8,128)S(1)} %maximum_select_fusion.5), channel_id=1, source_target_pairs={{0,2},{2,0},{4,6},{6,4},{8,10},{10,8},{12,14},{14,12},{16,18},{18,... | collective-permute-start | bytes 3145736 | tf_op jit(solution)/shard_map/ppermute | solution.py:946
  411.2 16.6 %collective-permute-start.41 = (bf16[512,512]{1,0:T(8,128)(2,1)S(1)}, bf16[512,512]{1,0:T(8,128)(2,1)S(1)}, u32[]{:S(2)}, u32[]{:S(2)}) collective-permute-start(bf16[512,512]{1,0:T(8,128)(2,1)S(1)} %convolution_convert_fusion.5), channel_id=1, source_target_pairs={{0,8},{2,10},{4,12},{6,14},{8,16},{10,18},{12,20},{14,22},{16,24},... | collective-permute-start | bytes 1572872 | tf_op jit(solution)/shard_map/ppermute | solution.py:1135
  414.9 58.5 %collective-permute-start.9 = (bf16[512,2048]{1,0:T(8,128)(2,1)S(1)}, bf16[512,2048]{1,0:T(8,128)(2,1)S(1)}, u32[]{:S(2)}, u32[]{:S(2)}) collective-permute-start(bf16[512,2048]{1,0:T(8,128)(2,1)S(1)} %convolution_convert_fusion), channel_id=1, source_target_pairs={{0,2},{2,0},{4,6},{6,4},{8,10},{10,8},{12,14},{14,12},{16,18},{18,... | collective-permute-start | bytes 6291464 | tf_op jit(solution)/shard_map/ppermute | solution.py:946
  416.2 22.8 %collective-permute-start.29 = (bf16[512,512]{1,0:T(8,128)(2,1)S(1)}, bf16[512,512]{1,0:T(8,128)(2,1)S(1)}, u32[]{:S(2)}, u32[]{:S(2)}) collective-permute-start(bf16[512,512]{1,0:T(8,128)(2,1)S(1)} %convolution_convert_fusion.6), channel_id=1, source_target_pairs={{0,8},{2,10},{4,12},{6,14},{8,16},{10,18},{12,20},{14,22},{16,24},... | collective-permute-start | bytes 1572872 | tf_op jit(solution)/shard_map/ppermute | solution.py:1135
  428.5 21.7 %collective-permute-start.42 = (bf16[512,512]{1,0:T(8,128)(2,1)S(1)}, bf16[512,512]{1,0:T(8,128)(2,1)S(1)}, u32[]{:S(2)}, u32[]{:S(2)}) collective-permute-start(bf16[512,512]{1,0:T(8,128)(2,1)S(1)} %add_convert_fusion.3), channel_id=1, source_target_pairs={{0,8},{2,10},{4,12},{6,14},{8,16},{10,18},{12,20},{14,22},{16,24},... | collective-permute-start | bytes 1572872 | tf_op jit(solution)/shard_map/ppermute | solution.py:1135
  439.7 21.7 %collective-permute-start.30 = (bf16[512,512]{1,0:T(8,128)(2,1)S(1)}, bf16[512,512]{1,0:T(8,128)(2,1)S(1)}, u32[]{:S(2)}, u32[]{:S(2)}) collective-permute-start(bf16[512,512]{1,0:T(8,128)(2,1)S(1)} %add_convert_fusion.7), channel_id=1, source_target_pairs={{0,8},{2,10},{4,12},{6,14},{8,16},{10,18},{12,20},{14,22},{16,24},... | collective-permute-start | bytes 1572872 | tf_op jit(solution)/shard_map/ppermute | solution.py:1135
  451.0 21.7 %collective-permute-start.43 = (bf16[512,512]{1,0:T(8,128)(2,1)S(1)}, bf16[512,512]{1,0:T(8,128)(2,1)S(1)}, u32[]{:S(2)}, u32[]{:S(2)}) collective-permute-start(bf16[512,512]{1,0:T(8,128)(2,1)S(1)} %add_convert_fusion.2), channel_id=1, source_target_pairs={{0,8},{2,10},{4,12},{6,14},{8,16},{10,18},{12,20},{14,22},{16,24},... | collective-permute-start | bytes 1572872 | tf_op jit(solution)/shard_map/ppermute | solution.py:1135
  462.2 21.3 %collective-permute-start.31 = (bf16[512,512]{1,0:T(8,128)(2,1)S(1)}, bf16[512,512]{1,0:T(8,128)(2,1)S(1)}, u32[]{:S(2)}, u32[]{:S(2)}) collective-permute-start(bf16[512,512]{1,0:T(8,128)(2,1)S(1)} %add_convert_fusion.6), channel_id=1, source_target_pairs={{0,8},{2,10},{4,12},{6,14},{8,16},{10,18},{12,20},{14,22},{16,24},... | collective-permute-start | bytes 1572872 | tf_op jit(solution)/shard_map/ppermute | solution.py:1135
  476.0 24.4 %collective-permute-start.10 = (bf16[2,128,2048]{2,1,0:T(8,128)(2,1)S(1)}, bf16[2,128,2048]{2,1,0:T(8,128)(2,1)S(1)}, u32[]{:S(2)}, u32[]{:S(2)}) collective-permute-start(bf16[2,128,2048]{2,1,0:T(8,128)(2,1)S(1)} %fusion.33), channel_id=1, source_target_pairs={{0,1},{1,0},{2,3},{3,2},{4,5},{5,4},{6,7},{7,6},{8,9},{9,8},{10,11... | collective-permute-start | bytes 3145736 | tf_op jit(solution)/shard_map/ppermute | solution.py:949
  486.1 15.6 %collective-permute-start.63 = (bf16[1024,128]{1,0:T(8,128)(2,1)S(1)}, bf16[1024,128]{1,0:T(8,128)(2,1)S(1)}, u32[]{:S(2)}, u32[]{:S(2)}) collective-permute-start(bf16[1024,128]{1,0:T(8,128)(2,1)S(1)} %get-tuple-element.115), channel_id=1, source_target_pairs={{0,4},{2,6},{4,0},{6,2},{8,12},{10,14},{12,8},{14,10},{16,20},{18,... | collective-permute-start | bytes 786440 | tf_op jit(solution)/shard_map/ppermute | solution.py:946
  487.0 36.1 %collective-permute-start.64 = (bf16[1024,128]{1,0:T(8,128)(2,1)S(1)}, bf16[1024,128]{1,0:T(8,128)(2,1)S(1)}, u32[]{:S(2)}, u32[]{:S(2)}) collective-permute-start(bf16[1024,128]{1,0:T(8,128)(2,1)S(1)} %get-tuple-element.113), channel_id=1, source_target_pairs={{0,6},{2,4},{4,2},{6,0},{8,14},{10,12},{12,10},{14,8},{16,22},{18,... | collective-permute-start | bytes 786440 | tf_op jit(solution)/shard_map/ppermute | solution.py:946
  488.0 34.3 %collective-permute-start.44 = (bf16[256,1024]{1,0:T(8,128)(2,1)S(1)}, bf16[256,1024]{1,0:T(8,128)(2,1)S(1)}, u32[]{:S(2)}, u32[]{:S(2)}) collective-permute-start(bf16[256,1024]{1,0:T(8,128)(2,1)S(1)} %convolution_convert_fusion.3), channel_id=1, source_target_pairs={{0,8},{2,10},{4,12},{6,14},{8,16},{10,18},{12,20},{14,22},{16,24},... | collective-permute-start | bytes 1572872 | tf_op jit(solution)/shard_map/ppermute | solution.py:1135
  488.2 26.9 %collective-permute-start.32 = (bf16[256,1024]{1,0:T(8,128)(2,1)S(1)}, bf16[256,1024]{1,0:T(8,128)(2,1)S(1)}, u32[]{:S(2)}, u32[]{:S(2)}) collective-permute-start(bf16[256,1024]{1,0:T(8,128)(2,1)S(1)} %convolution_convert_fusion.4), channel_id=1, source_target_pairs={{0,8},{2,10},{4,12},{6,14},{8,16},{10,18},{12,20},{14,22},{16,24},... | collective-permute-start | bytes 1572872 | tf_op jit(solution)/shard_map/ppermute | solution.py:1135
  500.8 15.2 %collective-permute-start.11 = (bf16[128,2048]{1,0:T(8,128)(2,1)S(1)}, bf16[128,2048]{1,0:T(8,128)(2,1)S(1)}, u32[]{:S(2)}, u32[]{:S(2)}) collective-permute-start(bf16[128,2048]{1,0:T(8,128)(2,1)S(1)} %fusion.94), channel_id=1, source_target_pairs={{0,4},{2,6},{4,0},{6,2},{8,12},{10,14},{12,8},{14,10},{16,20},{18,... | collective-permute-start | bytes 1572872 | tf_op jit(solution)/shard_map/ppermute | solution.py:946
  515.9 16.7 %collective-permute-start.33 = (bf16[256,1024]{1,0:T(8,128)(2,1)S(1)}, bf16[256,1024]{1,0:T(8,128)(2,1)S(1)}, u32[]{:S(2)}, u32[]{:S(2)}) collective-permute-start(bf16[256,1024]{1,0:T(8,128)(2,1)S(1)} %add_convert_fusion.5), channel_id=1, source_target_pairs={{0,8},{2,10},{4,12},{6,14},{8,16},{10,18},{12,20},{14,22},{16,24},... | collective-permute-start | bytes 1572872 | tf_op jit(solution)/shard_map/ppermute | solution.py:1135
  522.1 23.3 %collective-permute-start.65 = (f32[1024,256]{1,0:T(8,128)S(1)}, f32[1024,256]{1,0:T(8,128)S(1)}, u32[]{:S(2)}, u32[]{:S(2)}) collective-permute-start(f32[1024,256]{1,0:T(8,128)S(1)} %constant_dynamic-slice_fusion.9), channel_id=1, source_target_pairs={{0,2},{2,0},{4,6},{6,4},{8,10},{10,8},{12,14},{14,12},{16,18},{18,... | collective-permute-start | bytes 3145736 | tf_op jit(solution)/shard_map/ppermute | solution.py:946
  523.0 20.8 %collective-permute-start.45 = (bf16[256,1024]{1,0:T(8,128)(2,1)S(1)}, bf16[256,1024]{1,0:T(8,128)(2,1)S(1)}, u32[]{:S(2)}, u32[]{:S(2)}) collective-permute-start(bf16[256,1024]{1,0:T(8,128)(2,1)S(1)} %add_convert_fusion.1), channel_id=1, source_target_pairs={{0,8},{2,10},{4,12},{6,14},{8,16},{10,18},{12,20},{14,22},{16,24},... | collective-permute-start | bytes 1572872 | tf_op jit(solution)/shard_map/ppermute | solution.py:1135
  533.4 21.7 %collective-permute-start.34 = (bf16[256,1024]{1,0:T(8,128)(2,1)S(1)}, bf16[256,1024]{1,0:T(8,128)(2,1)S(1)}, u32[]{:S(2)}, u32[]{:S(2)}) collective-permute-start(bf16[256,1024]{1,0:T(8,128)(2,1)S(1)} %add_convert_fusion.4), channel_id=1, source_target_pairs={{0,8},{2,10},{4,12},{6,14},{8,16},{10,18},{12,20},{14,22},{16,24},... | collective-permute-start | bytes 1572872 | tf_op jit(solution)/shard_map/ppermute | solution.py:1135
  544.6 23.5 %collective-permute-start.46 = (bf16[256,1024]{1,0:T(8,128)(2,1)S(1)}, bf16[256,1024]{1,0:T(8,128)(2,1)S(1)}, u32[]{:S(2)}, u32[]{:S(2)}) collective-permute-start(bf16[256,1024]{1,0:T(8,128)(2,1)S(1)} %add_convert_fusion), channel_id=1, source_target_pairs={{0,8},{2,10},{4,12},{6,14},{8,16},{10,18},{12,20},{14,22},{16,24},... | collective-permute-start | bytes 1572872 | tf_op jit(solution)/shard_map/ppermute | solution.py:1135
  544.8 14.9 %collective-permute-start.12 = (bf16[128,2048]{1,0:T(8,128)(2,1)S(1)}, bf16[128,2048]{1,0:T(8,128)(2,1)S(1)}, u32[]{:S(2)}, u32[]{:S(2)}) collective-permute-start(bf16[128,2048]{1,0:T(8,128)(2,1)S(1)} %get-tuple-element.104), channel_id=1, source_target_pairs={{0,1},{1,0},{2,3},{3,2},{4,5},{5,4},{6,7},{7,6},{8,9},{9,8},{10,11... | collective-permute-start | bytes 1572872 | tf_op jit(solution)/shard_map/ppermute | solution.py:949
  545.6 21.4 %collective-permute-start.66 = (f32[512,256]{1,0:T(8,128)S(1)}, f32[512,256]{1,0:T(8,128)S(1)}, u32[]{:S(2)}, u32[]{:S(2)}) collective-permute-start(f32[512,256]{1,0:T(8,128)S(1)} %constant_dynamic-slice_fusion.8), channel_id=1, source_target_pairs={{0,1},{1,0},{2,3},{3,2},{4,5},{5,4},{6,7},{7,6},{8,9},{9,8},{10,11... | collective-permute-start | bytes 1572872 | tf_op jit(solution)/shard_map/ppermute | solution.py:949
  559.8 30.0 %collective-permute-start.13 = (bf16[256,2048]{1,0:T(8,128)(2,1)S(1)}, bf16[256,2048]{1,0:T(8,128)(2,1)S(1)}, u32[]{:S(2)}, u32[]{:S(2)}) collective-permute-start(bf16[256,2048]{1,0:T(8,128)(2,1)S(1)} %pad_maximum_fusion.6), channel_id=1, source_target_pairs={{0,4},{2,6},{4,0},{6,2},{8,12},{10,14},{12,8},{14,10},{16,20},{18,... | collective-permute-start | bytes 3145736 | tf_op jit(solution)/shard_map/ppermute | solution.py:946
  567.1 16.6 %collective-permute-start.67 = (f32[256,256]{1,0:T(8,128)S(1)}, f32[256,256]{1,0:T(8,128)S(1)}, u32[]{:S(2)}, u32[]{:S(2)}) collective-permute-start(f32[256,256]{1,0:T(8,128)S(1)} %constant_dynamic-slice_fusion.7), channel_id=1, source_target_pairs={{0,4},{2,6},{4,0},{6,2},{8,12},{10,14},{12,8},{14,10},{16,20},{18,... | collective-permute-start | bytes 786440 | tf_op jit(solution)/shard_map/ppermute | solution.py:946
  585.1 17.0 %collective-permute-start.59 = (bf16[128,1024]{1,0:T(8,128)(2,1)}, bf16[128,1024]{1,0:T(8,128)(2,1)}, u32[]{:S(2)}, u32[]{:S(2)}) collective-permute-start(bf16[128,1024]{1,0:T(8,128)(2,1)} %get-tuple-element.117), channel_id=1, source_target_pairs={{0,2},{2,0},{4,6},{6,4},{8,10},{10,8},{12,14},{14,12},{16,18},{18,... | collective-permute-start | bytes 786440 | tf_op jit(solution)/shard_map/ppermute | solution.py:946
  585.1 23.6 %collective-permute-start.60 = (bf16[128,1024]{1,0:T(8,128)(2,1)}, bf16[128,1024]{1,0:T(8,128)(2,1)}, u32[]{:S(2)}, u32[]{:S(2)}) collective-permute-start(bf16[128,1024]{1,0:T(8,128)(2,1)} %get-tuple-element.118), channel_id=1, source_target_pairs={{0,4},{2,6},{4,0},{6,2},{8,12},{10,14},{12,8},{14,10},{16,20},{18,... | collective-permute-start | bytes 786440 | tf_op jit(solution)/shard_map/ppermute | solution.py:946
  586.0 25.2 %collective-permute-start.61 = (bf16[128,1024]{1,0:T(8,128)(2,1)}, bf16[128,1024]{1,0:T(8,128)(2,1)}, u32[]{:S(2)}, u32[]{:S(2)}) collective-permute-start(bf16[128,1024]{1,0:T(8,128)(2,1)} %get-tuple-element.116), channel_id=1, source_target_pairs={{0,6},{2,4},{4,2},{6,0},{8,14},{10,12},{12,10},{14,8},{16,22},{18,... | collective-permute-start | bytes 786440 | tf_op jit(solution)/shard_map/ppermute | solution.py:946
  591.5 47.7 %collective-permute-start.14 = (bf16[512,2048]{1,0:T(8,128)(2,1)}, bf16[512,2048]{1,0:T(8,128)(2,1)}, u32[]{:S(2)}, u32[]{:S(2)}) collective-permute-start(bf16[512,2048]{1,0:T(8,128)(2,1)} %pad_maximum_fusion.3), channel_id=1, source_target_pairs={{0,2},{2,0},{4,6},{6,4},{8,10},{10,8},{12,14},{14,12},{16,18},{18,... | collective-permute-start | bytes 6291464 | tf_op jit(solution)/shard_map/ppermute | solution.py:946
  613.0 17.1 %collective-permute-start.3 = (bf16[128,2048]{1,0:T(8,128)(2,1)}, bf16[128,2048]{1,0:T(8,128)(2,1)}, u32[]{:S(2)}, u32[]{:S(2)}) collective-permute-start(bf16[128,2048]{1,0:T(8,128)(2,1)} %get-tuple-element.133), channel_id=1, source_target_pairs={{0,1},{1,0},{2,3},{3,2},{4,5},{5,4},{6,7},{7,6},{8,9},{9,8},{10,11... | collective-permute-start | bytes 1572872 | tf_op jit(solution)/shard_map/ppermute | solution.py:949
  616.9 19.4 %collective-permute-start.73 = (f32[512,256]{1,0:T(8,128)}, f32[512,256]{1,0:T(8,128)}, u32[]{:S(2)}, u32[]{:S(2)}) collective-permute-start(f32[512,256]{1,0:T(8,128)} %maximum_select_fusion.6), channel_id=1, source_target_pairs={{0,1},{1,0},{2,3},{3,2},{4,5},{5,4},{6,7},{7,6},{8,9},{9,8},{10,11... | collective-permute-start | bytes 1572872 | tf_op jit(solution)/shard_map/ppermute | solution.py:949
  639.2 74.6 %collective-permute-start.74 = (f32[1024,256]{1,0:T(8,128)}, f32[1024,256]{1,0:T(8,128)}, u32[]{:S(2)}, u32[]{:S(2)}) collective-permute-start(f32[1024,256]{1,0:T(8,128)} %maximum_select_fusion.4), channel_id=1, source_target_pairs={{0,2},{2,0},{4,6},{6,4},{8,10},{10,8},{12,14},{14,12},{16,18},{18,... | collective-permute-start | bytes 3145736 | tf_op jit(solution)/shard_map/ppermute | solution.py:946
  679.6 57.1 %collective-permute-start.15 = (bf16[512,2048]{1,0:T(8,128)(2,1)}, bf16[512,2048]{1,0:T(8,128)(2,1)}, u32[]{:S(2)}, u32[]{:S(2)}) collective-permute-start(bf16[512,2048]{1,0:T(8,128)(2,1)} %convolution_convert_fusion.2), channel_id=1, source_target_pairs={{0,2},{2,0},{4,6},{6,4},{8,10},{10,8},{12,14},{14,12},{16,18},{18,... | collective-permute-start | bytes 6291464 | tf_op jit(solution)/shard_map/ppermute | solution.py:946
  713.2 31.8 %collective-permute-start.58 = (bf16[256,128]{1,0:T(8,128)(2,1)S(1)}, bf16[256,128]{1,0:T(8,128)(2,1)S(1)}, u32[]{:S(2)}, u32[]{:S(2)}) collective-permute-start(bf16[256,128]{1,0:T(8,128)(2,1)S(1)} %get-tuple-element.134), channel_id=1, source_target_pairs={{0,6},{2,4},{4,2},{6,0},{8,14},{10,12},{12,10},{14,8},{16,22},{18,... | collective-permute-start | bytes 196616 | tf_op jit(solution)/shard_map/ppermute | solution.py:946
  719.2 16.8 %collective-permute-start.38 = (bf16[256,768]{1,0:T(8,128)(2,1)S(1)}, bf16[256,768]{1,0:T(8,128)(2,1)S(1)}, u32[]{:S(2)}, u32[]{:S(2)}) collective-permute-start(bf16[256,768]{1,0:T(8,128)(2,1)S(1)} %copy-done.44), channel_id=1, source_target_pairs={{0,8},{2,10},{4,12},{6,14},{8,16},{10,18},{12,20},{14,22},{16,24},... | collective-permute-start | bytes 1179656 | tf_op jit(solution)/shard_map/ppermute | solution.py:1135
  728.2 16.2 %collective-permute-start.51 = (bf16[256,768]{1,0:T(8,128)(2,1)S(1)}, bf16[256,768]{1,0:T(8,128)(2,1)S(1)}, u32[]{:S(2)}, u32[]{:S(2)}) collective-permute-start(bf16[256,768]{1,0:T(8,128)(2,1)S(1)} %add_convert_fusion.9), channel_id=1, source_target_pairs={{0,8},{2,10},{4,12},{6,14},{8,16},{10,18},{12,20},{14,22},{16,24},... | collective-permute-start | bytes 1179656 | tf_op jit(solution)/shard_map/ppermute | solution.py:1135
  736.6 16.2 %collective-permute-start.39 = (bf16[256,768]{1,0:T(8,128)(2,1)S(1)}, bf16[256,768]{1,0:T(8,128)(2,1)S(1)}, u32[]{:S(2)}, u32[]{:S(2)}) collective-permute-start(bf16[256,768]{1,0:T(8,128)(2,1)S(1)} %add_convert_fusion.11), channel_id=1, source_target_pairs={{0,8},{2,10},{4,12},{6,14},{8,16},{10,18},{12,20},{14,22},{16,24},... | collective-permute-start | bytes 1179656 | tf_op jit(solution)/shard_map/ppermute | solution.py:1135
  740.2 24.1 %collective-permute-start.16 = (bf16[2,128,2048]{2,1,0:T(8,128)(2,1)S(1)}, bf16[2,128,2048]{2,1,0:T(8,128)(2,1)S(1)}, u32[]{:S(2)}, u32[]{:S(2)}) collective-permute-start(bf16[2,128,2048]{2,1,0:T(8,128)(2,1)S(1)} %fusion.34), channel_id=1, source_target_pairs={{0,1},{1,0},{2,3},{3,2},{4,5},{5,4},{6,7},{7,6},{8,9},{9,8},{10,11... | collective-permute-start | bytes 3145736 | tf_op jit(solution)/shard_map/ppermute | solution.py:949
  745.0 16.2 %collective-permute-start.52 = (bf16[256,768]{1,0:T(8,128)(2,1)S(1)}, bf16[256,768]{1,0:T(8,128)(2,1)S(1)}, u32[]{:S(2)}, u32[]{:S(2)}) collective-permute-start(bf16[256,768]{1,0:T(8,128)(2,1)S(1)} %add_convert_fusion.8), channel_id=1, source_target_pairs={{0,8},{2,10},{4,12},{6,14},{8,16},{10,18},{12,20},{14,22},{16,24},... | collective-permute-start | bytes 1179656 | tf_op jit(solution)/shard_map/ppermute | solution.py:1135
  753.4 15.7 %collective-permute-start.40 = (bf16[256,768]{1,0:T(8,128)(2,1)S(1)}, bf16[256,768]{1,0:T(8,128)(2,1)S(1)}, u32[]{:S(2)}, u32[]{:S(2)}) collective-permute-start(bf16[256,768]{1,0:T(8,128)(2,1)S(1)} %add_convert_fusion.10), channel_id=1, source_target_pairs={{0,8},{2,10},{4,12},{6,14},{8,16},{10,18},{12,20},{14,22},{16,24},... | collective-permute-start | bytes 1179656 | tf_op jit(solution)/shard_map/ppermute | solution.py:1135
  765.5 15.2 %collective-permute-start.17 = (bf16[128,2048]{1,0:T(8,128)(2,1)}, bf16[128,2048]{1,0:T(8,128)(2,1)}, u32[]{:S(2)}, u32[]{:S(2)}) collective-permute-start(bf16[128,2048]{1,0:T(8,128)(2,1)} %fusion.95), channel_id=1, source_target_pairs={{0,4},{2,6},{4,0},{6,2},{8,12},{10,14},{12,8},{14,10},{16,20},{18,... | collective-permute-start | bytes 1572872 | tf_op jit(solution)/shard_map/ppermute | solution.py:946
  770.6 15.9 %collective-permute-start.54 = (bf16[128,768]{1,0:T(8,128)(2,1)}, bf16[128,768]{1,0:T(8,128)(2,1)}, u32[]{:S(2)}, u32[]{:S(2)}) collective-permute-start(bf16[128,768]{1,0:T(8,128)(2,1)} %get-tuple-element.121), channel_id=1, source_target_pairs={{0,4},{2,6},{4,0},{6,2},{8,12},{10,14},{12,8},{14,10},{16,20},{18,... | collective-permute-start | bytes 589832 | tf_op jit(solution)/shard_map/ppermute | solution.py:946
  772.0 22.9 %collective-permute-start.55 = (bf16[128,768]{1,0:T(8,128)(2,1)}, bf16[128,768]{1,0:T(8,128)(2,1)}, u32[]{:S(2)}, u32[]{:S(2)}) collective-permute-start(bf16[128,768]{1,0:T(8,128)(2,1)} %get-tuple-element.119), channel_id=1, source_target_pairs={{0,6},{2,4},{4,2},{6,0},{8,14},{10,12},{12,10},{14,8},{16,22},{18,... | collective-permute-start | bytes 589832 | tf_op jit(solution)/shard_map/ppermute | solution.py:946
  792.6 13.8 %collective-permute-start.18 = (bf16[128,2048]{1,0:T(8,128)(2,1)S(1)}, bf16[128,2048]{1,0:T(8,128)(2,1)S(1)}, u32[]{:S(2)}, u32[]{:S(2)}) collective-permute-start(bf16[128,2048]{1,0:T(8,128)(2,1)S(1)} %fusion.29), channel_id=1, source_target_pairs={{0,1},{1,0},{2,3},{3,2},{4,5},{5,4},{6,7},{7,6},{8,9},{9,8},{10,11... | collective-permute-start | bytes 1572872 | tf_op jit(solution)/shard_map/ppermute | solution.py:949
  (152 other events, 2662.6 us)

commit v3 on v2

--- a/solution.py
+++ b/solution.py
@@ -541,6 +541,11 @@
         self.local_sems, self.send_sems, self.recv_sems = local_sems, send_sems, recv_sems
         self.locals, self.sends, self.recvs = 0, 0, 0
 
+    def check(self):
+        assert self.locals <= self.local_sems.shape[0]
+        assert self.sends <= self.send_sems.shape[0]
+        assert self.recvs <= self.recv_sems.shape[0]
+
     def local(self, src, dst):
         copy = pltpu.make_async_copy(src, dst, self.local_sems.at[self.locals])
         self.locals += 1
@@ -629,39 +634,83 @@
 
 
 class RowReduce:
-    def __init__(self, here, copies, bufs):
-        self.here, self.copies = here, copies
+    def __init__(self, here, copies, bufs, acks=None):
+        self.here, self.copies, self.acks = here, copies, acks
         (self.snd, self.rcv, self.acc, self.out, self.into) = bufs
+        self.sent = []
+
+    def begin(self):
+        for copy in self.sent:
+            copy.wait_send()
+        self.sent, self.core = [], []
 
     def core_send(self, index):
         rows = pl.ds(index * 256, 256)
-        copy = self.copies.push(self.snd.at[rows], self.rcv.at[rows], self.here.core)
-        self.core = getattr(self, "core", []) + [copy]
-
-    def finish(self, add_core):
-        here, copies, acc, out, into = self.here, self.copies, self.acc, self.out, self.into
+        self.core.append(self.copies.push(self.snd.at[rows], self.rcv.at[rows], self.here.core))
+
+    def add_core(self, first, count):
+        acc, rcv = self.acc, self.rcv
+
+        def body(i):
+            at = pl.ds(pl.multiple_of(first + i * 64, 64), 64)
+            acc[at, :] = acc[at, :] + rcv[at, :].astype(wide)
+
+        tiles(count // 64, body)
+
+    def round_out(self, first, count, extra=None):
+        acc, out, into = self.acc, self.out, self.into
+
+        def body(i):
+            at = pl.ds(pl.multiple_of(first + i * 64, 64), 64)
+            value = acc[at, :]
+            if extra is not None:
+                value = value + into[pl.ds(extra, 64), :].astype(wide)
+            out[pl.ds(pl.multiple_of(first - 128 + i * 64, 64), 64), :] = value.astype(low)
+
+        tiles(count // 64, body)
+
+    def diagonal(self):
         for copy in self.core:
             copy.wait_recv()
-        add_core(pl.ds(384, 128))
-        out[384:512, :] = acc[384:512, :].astype(low)
-        diag_x = copies.push(out.at[384:448], into.at[384:448], here.across)
-        diag_y = copies.push(out.at[448:512], into.at[448:512], here.mid)
-        add_core(pl.ds(128, 256))
-        out[128:192, :] = acc[128:192, :].astype(low)
-        out[320:384, :] = acc[320:384, :].astype(low)
-        diag_y.wait_recv()
-        out[192:256, :] = (acc[192:256, :] + into[448:512, :].astype(wide)).astype(low)
-        over_x = copies.push(out.at[128:256], into.at[128:256], here.across)
-        diag_x.wait_recv()
-        out[256:320, :] = (acc[256:320, :] + into[384:448, :].astype(wide)).astype(low)
-        over_y = copies.push(out.at[256:384], into.at[256:384], here.mid)
-        add_core(pl.ds(0, 128))
-        over_x.wait_recv()
-        over_y.wait_recv()
-        self.sent = self.core + [diag_x, diag_y, over_x, over_y]
+        self.add_core(384, 128)
+        self.round_out(384, 128)
+        self.diag_x = self.copies.push(self.out.at[256:320], self.into.at[256:320], self.here.across)
+        self.diag_y = self.copies.push(self.out.at[320:384], self.into.at[320:384], self.here.mid)
+        self.add_core(128, 256)
+        self.round_out(128, 64)
+        self.round_out(320, 64)
+        self.add_core(0, 128)
+
+    def sides(self):
+        self.diag_y.wait_recv()
+        self.round_out(192, 64, 320)
+        self.over_x = self.copies.push(self.out.at[0:128], self.into.at[0:128], self.here.across)
+        self.diag_x.wait_recv()
+        self.round_out(256, 64, 256)
+        self.over_y = self.copies.push(self.out.at[128:256], self.into.at[128:256], self.here.mid)
+        self.sent = self.core + [self.diag_x, self.diag_y, self.over_x, self.over_y]
+
+    def arrive(self):
+        self.over_x.wait_recv()
+        self.over_y.wait_recv()
+
+    def total(self, at, size):
+        acc, into = self.acc, self.into
         return (
-            acc[0:128, :] + into[128:256, :].astype(wide) + into[256:384, :].astype(wide)
-        )
+            acc[pl.ds(at, size), :]
+            + into[pl.ds(at, size), :].astype(wide)
+            + into[pl.ds(at + 128, size), :].astype(wide)
+        )
+
+    def release(self):
+        for index, peer in enumerate((self.here.core, self.here.across, self.here.mid)):
+            pl.semaphore_signal(
+                self.acks.at[index], inc=1, device_id=peer, device_id_type=MESH
+            )
+
+    def await_release(self):
+        for index in range(3):
+            pl.semaphore_wait(self.acks.at[index], 1)
 
     def drain(self):
         for copy in self.sent:
@@ -715,8 +764,8 @@
 
 
 def forward_kernel(
-    tok, col, row, qkvw, outw, upw, downw, gains, gate,
-    o_hid, o_qkv, o_probs, o_att, o_proj, o_mid, o_units, o_up, o_col, o_row,
+    tok, col, row, cot, qkvw, outw, upw, downw, gains, gate,
+    o_hid, o_qkv, o_probs, o_att, o_proj, o_mid, o_units, o_up, o_col, o_row, o_cot,
     o_wq, o_wo, o_wu, o_wd,
     toks, hid, wq, wo, wu, wd, cols, rows_info, qkvb, probs, att,
     snd, rcv, acc, out_buf, in_buf, proj, mid_buf, units, up,
@@ -743,11 +792,18 @@
         return got
 
     def landed(got):
-        got[0].wait()
-        for copy in got[1:]:
-            copy.wait_recv()
-
-    got_q = spread(lambda t: qkvw.at[:, :, part(t, head_width)], wq.at[:, own_rows, :])
+        for i, copy in enumerate(got):
+            if i % SHARE:
+                copy.wait_recv()
+            else:
+                copy.wait()
+
+    got_q = []
+    for j in range(3):
+        got_q += spread(
+            lambda t: qkvw.at[j, :, part(t, head_width)],
+            wq.at[own_rows, j * head_width : (j + 1) * head_width],
+        )
     own_tok = copies.local(tok, toks.at[0:256])
     own_col = copies.local(col, cols.at[0:256])
     own_row = copies.local(row, rows_info.at[0])
@@ -760,6 +816,9 @@
     got_o = spread(lambda t: outw.at[part(t, head_width), :], wo.at[:, own_rows])
     got_u = spread(lambda t: upw.at[:, part(t, unit_width)], wu.at[own_rows, :])
     got_d = spread(lambda t: downw.at[part(t, unit_width), :], wd.at[:, own_rows])
+    own_cot = copies.local(cot, o_cot.at[0:256])
+    cot_mid = copies.push(cot, o_cot.at[256:512], here.mid)
+    cot_core = copies.push(cot, o_cot.at[512:768], here.core)
 
     def up_view(h):
         return lambda k: wu.at[pl.ds(pl.multiple_of(k * block + h * 256, 256), 256), :]
@@ -767,7 +826,7 @@
     def down_view(h):
         return lambda k: wd.at[h * 512 : (h + 1) * 512, part(k, block)]
 
-    z_q = ZGather(here, copies, lambda k: wq.at[:, part(k, block), :])
+    z_q = ZGather(here, copies, lambda k: wq.at[part(k, block), :])
     z_o = ZGather(here, copies, lambda k: wo.at[:, part(k, block)])
     z_u = [ZGather(here, copies, up_view(h)) for h in range(2)]
     z_d = [ZGather(here, copies, down_view(h)) for h in range(2)]
@@ -817,7 +876,7 @@
 
         def qkv_tile(i, j=j):
             at = part(i, 512)
-            made = nn(hid[at, :], wq[j])
+            made = nn(hid[at, :], wq[:, j * head_width : (j + 1) * head_width])
             if j < 2:
                 cosine = cols[at, 0:HD]
                 sine = cols[at, HD : 2 * HD]
@@ -873,6 +932,7 @@
     outs.append(copies.local(wo, o_wo))
 
     reduce = RowReduce(here, copies, (snd, rcv, acc, out_buf, in_buf))
+    reduce.begin()
     for i in range(2):
 
         def send_tile(n, i=i):
@@ -890,18 +950,24 @@
 
     tiles(4, keep_tile)
 
-    def add_core(at):
-        acc[at, :] = acc[at, :] + rcv[at, :].astype(wide)
-
     z_u[0].forward()
     landed(got_d)
     z_d[0].start()
-    projected = reduce.finish(add_core)
-    proj[...] = projected
-    middle = toks[0:128, :].astype(wide) + gate[:, 0:1] * projected
-    mid_buf[...] = middle
-    r = lax.rsqrt(jnp.mean(middle * middle, axis=-1, keepdims=True) + epsilon)
-    units[0:128, :] = (middle * r * gains[1:2, :]).astype(low)
+    reduce.diagonal()
+    reduce.sides()
+    reduce.arrive()
+
+    def middle_tile(i):
+        at = pl.multiple_of(i * 64, 64)
+        rows64 = pl.ds(at, 64)
+        projected = reduce.total(at, 64)
+        proj[rows64, :] = projected
+        middle = toks[rows64, :].astype(wide) + gate[rows64, 0:1] * projected
+        mid_buf[rows64, :] = middle
+        r = lax.rsqrt(jnp.mean(middle * middle, axis=-1, keepdims=True) + epsilon)
+        units[rows64, :] = (middle * r * gains[1:2, :]).astype(low)
+
+    tiles(2, middle_tile)
     outs.append(copies.local(proj, o_proj))
     outs.append(copies.local(mid_buf, o_mid))
     gather = RowGather(here, copies, units)
@@ -914,10 +980,14 @@
     z_u[1].arrive()
     outs.append(copies.local(wu, o_wu))
 
+    cot_mid.wait_recv()
+    cot_fwd = copies.push(o_cot.at[256:512], o_cot.at[768:1024], here.core)
+
     def up_tile(i):
         at = part(i % 2, 512)
         c = part(i // 2, 512)
-        up[at, c] = nn(units[at, :], wu[:, c])
+        made = nn(units[at, :], wu[:, c])
+        up[:, part((i % 2) * 2 + i // 2, 512)] = made
 
     tiles(unit_width // 256, up_tile)
     outs.append(copies.local(up, o_up))
@@ -929,13 +999,426 @@
 
     for one in [z_q, z_o] + z_u + z_d + [reduce, gather]:
         one.drain()
-    sent = [tok_mid, tok_core, tok_fwd, col_mid, col_core, row_mid, row_core, col_fwd, row_fwd]
+    own_cot.wait()
+    cot_core.wait_recv()
+    cot_fwd.wait_recv()
+    sent = [cot_mid, cot_core, cot_fwd, tok_mid, tok_core, tok_fwd, col_mid, col_core, row_mid, row_core, col_fwd, row_fwd]
     for got in (got_q, got_o, got_u, got_d):
-        sent += got[1:]
+        sent += [copy for i, copy in enumerate(got) if i % SHARE]
     for copy in sent:
         copy.wait_send()
     for copy in outs:
         copy.wait()
+    copies.check()
+
+
+class ZReduce:
+    def __init__(self, here, copies, grads, landing, pieces):
+        self.here, self.copies = here, copies
+        self.grads, self.landing, self.pieces = grads, landing, pieces
+        self.slot_y1, self.slot_y2 = copies.slot(), copies.slot()
+
+    def send_far(self):
+        here, copies = self.here, self.copies
+        self.y1 = copies.remote(self.grads.at[3], self.landing.at[2], here.far, self.slot_y1)
+        self.y2 = copies.remote(self.grads.at[3], self.landing.at[3], here.near, self.slot_y2)
+        pl.when(here.inner)(self.y1.start)
+        pl.when(here.outer)(self.y2.start)
+
+    def send_near(self):
+        self.near = self.copies.push(self.grads.at[1], self.landing.at[0], self.here.near)
+
+    def load(self, index, stage, slot):
+        loads = []
+        for piece, (rows, first, columns) in self.pieces:
+            loads.append(
+                self.copies.local(
+                    self.landing.at[(index,) + piece],
+                    stage.at[slot, 0:rows, first : first + columns],
+                )
+            )
+        return loads
+
+    def add(self, target, stage, slots):
+        for piece, (rows, first, columns) in self.pieces:
+
+            def body(i, piece=piece, first=first, columns=columns):
+                at = pl.ds(pl.multiple_of(i * 64, 64), 64)
+                lead = (target,) + piece[:-2] if len(piece) > 2 else (target,)
+                base = piece[-2].start or 0
+                here_at = pl.ds(pl.multiple_of(base + i * 64, 64), 64)
+                value = self.grads[lead + (here_at, slice(None))].astype(wide)
+                for slot in slots:
+                    value = value + stage[slot, at, first : first + columns].astype(wide)
+                self.grads[lead + (here_at, slice(None))] = value.astype(low)
+
+            tiles(rows // 64, body)
+
+    def send_two(self, stage):
+        here, copies = self.here, self.copies
+
+        @pl.when(here.inner)
+        def _():
+            self.y2.wait_recv()
+            for copy in self.load(3, stage, 0):
+                copy.wait()
+            self.add(2, stage, [0])
+
+        self.two = copies.push(self.grads.at[2], self.landing.at[1], here.two)
+
+    def finish(self, stage):
+        here = self.here
+        self.near.wait_recv()
+        self.two.wait_recv()
+        loads = self.load(0, stage, 0) + self.load(1, stage, 1)
+        for copy in loads:
+            copy.wait()
+        self.add(0, stage, [0, 1])
+
+        @pl.when(here.inner)
+        def _():
+            self.y1.wait_recv()
+            for copy in self.load(2, stage, 2):
+                copy.wait()
+            self.add(0, stage, [2])
+
+    def drain(self):
+        here = self.here
+        self.near.wait_send()
+        self.two.wait_send()
+        pl.when(here.inner)(self.y1.wait_send)
+        pl.when(here.outer)(self.y2.wait_send)
+
+
+def norm_back(value, grad, gain):
+    r = lax.rsqrt(jnp.mean(value * value, axis=-1, keepdims=True) + epsilon)
+    u = gain * grad
+    lean = jnp.mean(u * value, axis=-1, keepdims=True)
+    return r * u - value * (r * r * r * lean), grad * value * r
+
+
+def backward_kernel(
+    hid_h, qkv_h, probs_h, att_h, proj_h, mid_h, units_h, up_h, col_h, cot_h, tok_h,
+    wq_h, wo_h, wu_h, wd_h, gains, gate_heads, gate_all, slope_units, slope_heads,
+    o_block, o_input, o_gq, o_go, o_gu, o_gd, o_small, o_gains, l_q, l_o, l_u, l_d,
+    hid, wo, wu, wd, cols, qkvb, probs, att, cot, act, gup, acc,
+    snd, rcv, out_buf, in_buf, proj, mid_buf, gd, gu, go, gq, stage, top, own_tok, own_out,
+    gain_buf, small,
+    local_sems, send_sems, recv_sems, acks,
+):
+    here = Plane()
+    copies = Copies(local_sems, send_sems, recv_sems)
+    here.greet()
+    share, side = here.share, here.side
+    owned = 128
+    head_width = wo.shape[0]
+    unit_width = wu.shape[1]
+    heads = head_width // HD
+    units, wq, gqkv, gatt = hid, wu, act, gup
+    blocks = [here.place, here.near_place, here.two_place, here.far_place]
+
+    in_col = copies.local(col_h, cols)
+    in_up = copies.local(up_h, acc)
+    in_cot = copies.local(cot_h, cot)
+    in_wd = copies.local(wd_h, wd)
+    in_units = copies.local(units_h, units)
+    in_wu = copies.local(wu_h, wu)
+    in_own = [
+        copies.local(mid_h, mid_buf),
+        copies.local(proj_h, proj),
+        copies.local(tok_h.at[0:owned], own_tok),
+    ]
+    in_wo = copies.local(wo_h, wo)
+    in_att = copies.local(att_h, att)
+    in_qkv = copies.local(qkv_h, qkvb)
+    in_probs = copies.local(probs_h, probs)
+
+    def fact(at, index):
+        return cols[at, 2 * HD + index : 2 * HD + index + 1]
+
+    first_unit = (side * SHARE + share) * unit_width
+
+    def used_units(at, base, rows, columns):
+        lane = lax.broadcasted_iota(jnp.int32, (rows, columns), 1) + base
+        return lane.astype(wide) < (FF // NB) * (fact(at, 3) + 1.0)
+
+    in_col.wait()
+    in_up.wait()
+
+    def act_tile(i):
+        at = part(i, 128)
+        relu = jnp.maximum(acc[part(i % 4, 128), part(i // 4, unit_width)], 0.0)
+        used = used_units(at, first_unit, 128, unit_width)
+        act[at, :] = jnp.where(used, relu * relu, 0.0).astype(low)
+
+    tiles(8, act_tile)
+    in_cot.wait()
+
+    def live_cot(at):
+        return jnp.where(fact(at, 4) > 0.5, cot[at, :].astype(wide), 0.0)
+
+    def keep_tile(i):
+        at = part(i, 64)
+        top[at, :] = live_cot(at).astype(low)
+
+    tiles(owned // 64, keep_tile)
+
+    def scale_tile(i):
+        at = part(i, 64)
+        cot[at, :] = (gate_all[at, 0:1] * live_cot(at)).astype(low)
+
+    tiles(16, scale_tile)
+
+    every = slice(None)
+    z_d = ZReduce(
+        here, copies, gd, l_d, [((pl.ds(512 * j, 512), every), (512, 512 * j, 512)) for j in range(2)]
+    )
+    z_u = ZReduce(here, copies, gu, l_u, [((pl.ds(0, 512), every), (512, 0, unit_width))])
+    z_o = ZReduce(here, copies, go, l_o, [((pl.ds(0, head_width), every), (head_width, 0, 512))])
+    z_q = ZReduce(
+        here,
+        copies,
+        gq,
+        l_q,
+        [((j, pl.ds(0, 512), every), (512, head_width * j, head_width)) for j in range(3)],
+    )
+
+    def down_block(k):
+        def body(i):
+            m = part(i, 512)
+            gd[k, m, :] = tn(act[:, m], cot[:, part(blocks[k], 512)]).astype(low)
+
+        tiles(unit_width // 512, body)
+
+    down_block(3)
+    z_d.send_far()
+    down_block(2)
+    down_block(1)
+    z_d.send_near()
+    down_block(0)
+
+    in_wd.wait()
+
+    def gup_tile(i):
+        m, n = i % 2, i // 2
+        at = part(m, 512)
+        c = part(n, 512)
+        made = nt(cot[at, :], wd[c, :])
+        used = used_units(at, first_unit + n * 512, 512, 512)
+        relu = jnp.maximum(acc[:, part(m * 2 + n, 512)], 0.0)
+        gup[at, c] = jnp.where(used, 2.0 * relu * made, 0.0).astype(low)
+
+    tiles(4, gup_tile)
+    z_d.send_two(stage)
+
+    reduce = RowReduce(here, copies, (snd, rcv, acc, out_buf, in_buf), acks)
+
+    def partial_sums(term):
+        reduce.begin()
+        for i in range(2):
+
+            def send_tile(n, i=i):
+                snd[i * 256 : (i + 1) * 256, part(n, 512)] = term(
+                    pl.ds(512 + i * 256, 256), n
+                ).astype(low)
+
+            tiles(4, send_tile)
+            reduce.core_send(i)
+
+        def own_tile(n):
+            acc[:, part(n, 512)] = term(pl.ds(0, 512), n)
+
+        tiles(4, own_tile)
+
+    partial_sums(lambda at, n: nn(act[at, :], wd[:, part(n, 512)]))
+    in_units.wait()
+    reduce.diagonal()
+
+    def up_block(k):
+        def body(i):
+            c = part(i, 512)
+            gu[k, :, c] = tn(units[:, part(blocks[k], 512)], gup[:, c]).astype(low)
+
+        tiles(unit_width // 512, body)
+
+    up_block(3)
+    z_u.send_far()
+    reduce.sides()
+    up_block(2)
+    up_block(1)
+    z_u.send_near()
+    up_block(0)
+    in_hid = copies.local(hid_h, hid)
+    for copy in in_own:
+        copy.wait()
+    reduce.arrive()
+
+    def block_tile(i):
+        at = pl.multiple_of(i * 64, 64)
+        rows = pl.ds(at, 64)
+        downward = reduce.total(at, 64)
+        live = fact(rows, 4) > 0.5
+        own_out[rows, :] = jnp.where(
+            live, mid_buf[rows, :] + gate_all[rows, 0:1] * downward, 0.0
+        ).astype(low)
+        grad_gate = jnp.sum(top[rows, :].astype(wide) * downward, axis=-1, keepdims=True)
+        small[0, rows, :] = jnp.broadcast_to(grad_gate, (64, HD))
+
+    tiles(owned // 64, block_tile)
+    reduce.release()
+    own_rows = part(side, owned)
+    shown = copies.local(own_out, o_block.at[own_rows])
+    shown_far = copies.push(own_out, o_block.at[own_rows], here.across)
+
+    in_wu.wait()
+    reduce.await_release()
+    partial_sums(lambda at, n: nt(gup[at, :], wu[part(n, 512), :]))
+    in_wq = copies.local(wq_h, wq.at[:, 0 : 3 * head_width])
+    z_u.send_two(stage)
+    reduce.diagonal()
+    reduce.sides()
+    reduce.arrive()
+    gproj = cot
+
+    def middle_tile(i):
+        at = pl.multiple_of(i * 64, 64)
+        rows = pl.ds(at, 64)
+        grad = reduce.total(at, 64) + small[0, rows, 0:1] * slope_units[rows, :]
+        back, gain_terms = norm_back(mid_buf[rows, :], grad, gains[1:2, :])
+        grad_middle = top[rows, :].astype(wide) + back
+        mid_buf[rows, :] = grad_middle
+        grad_gate = jnp.sum(grad_middle * proj[rows, :], axis=-1, keepdims=True)
+        small[1, rows, :] = jnp.broadcast_to(grad_gate, (64, HD))
+        gproj[rows, :] = (gate_heads[rows, 0:1] * grad_middle).astype(low)
+        gain_buf[1:2, :] = gain_buf[1:2, :] + jnp.sum(gain_terms, axis=0, keepdims=True)
+
+    gain_buf[...] = jnp.zeros_like(gain_buf)
+    tiles(owned // 64, middle_tile)
+    reduce.release()
+    gather = RowGather(here, copies, gproj)
+    gather.run()
+
+    in_att.wait()
+    in_wo.wait()
+
+    def out_block(k):
+        go[k] = tn(att[...], gproj[:, part(blocks[k], 512)]).astype(low)
+
+    out_block(3)
+    z_o.send_far()
+    out_block(2)
+    out_block(1)
+    z_o.send_near()
+    out_block(0)
+    first_head = (side * SHARE + share) * heads
+
+    def gatt_tile(i):
+        at = part(i, 512)
+        made = nt(gproj[at, :], wo[...]).astype(low)
+        for h in range(heads):
+            used = 4.0 * fact(at, 2) + 4.0 > (first_head + h).astype(wide)
+            gatt[at, h * HD : (h + 1) * HD] = jnp.where(
+                used, made[:, h * HD : (h + 1) * HD].astype(wide), 0.0
+            ).astype(low)
+
+    tiles(2, gatt_tile)
+    z_o.send_two(stage)
+
+    in_qkv.wait()
+    in_probs.wait()
+    scale = HD ** (-0.5)
+    for h in range(heads):
+
+        def back_group(g, h=h):
+            at = part(g, 256)
+            lanes = [pl.ds(j * head_width + h * HD, HD) for j in range(3)]
+            query, keyed, value = (qkvb[at, lane] for lane in lanes)
+            grad = gatt[at, h * HD : (h + 1) * HD]
+            p = probs[part(g * heads + h, 256), :]
+            grad_p = nt(grad, value)
+            row_dot = jnp.sum(p * grad_p, axis=-1, keepdims=True)
+            grad_s = (p * (grad_p - row_dot)).astype(low)
+            cosine = cols[at, 0:HD]
+            sine = cols[at, HD : 2 * HD]
+            for lane, turned in (
+                (lanes[0], nn(grad_s, keyed) * scale),
+                (lanes[1], tn(grad_s, query) * scale),
+            ):
+                gqkv[at, lane] = (
+                    turned * cosine - pltpu.roll(turned, HD // 2, 1) * sine
+                ).astype(low)
+            gqkv[at, lanes[2]] = tn(p.astype(low), grad).astype(low)
+
+        tiles(SHARE, back_group)
+
+    in_hid.wait()
+
+    def qkv_block(k):
+        for j in range(3):
+            gq[k, j] = tn(
+                hid[:, part(blocks[k], 512)], gqkv[:, j * head_width : (j + 1) * head_width]
+            ).astype(low)
+
+    qkv_block(3)
+    z_q.send_far()
+    qkv_block(2)
+    qkv_block(1)
+    z_q.send_near()
+    qkv_block(0)
+    z_q.send_two(stage)
+
+    in_wq.wait()
+    reduce.await_release()
+    partial_sums(lambda at, n: nt(gqkv[at, 0 : 3 * head_width], wq[part(n, 512), 0 : 3 * head_width]))
+    reduce.diagonal()
+    reduce.sides()
+    shown.wait()
+    shown_far.wait()
+    reduce.arrive()
+
+    def input_tile(i):
+        at = pl.multiple_of(i * 64, 64)
+        rows = pl.ds(at, 64)
+        grad = reduce.total(at, 64) + small[1, rows, 0:1] * slope_heads[rows, :]
+        back, gain_terms = norm_back(own_tok[rows, :].astype(wide), grad, gains[0:1, :])
+        own_out[rows, :] = (mid_buf[rows, :] + back).astype(low)
+        gain_buf[0:1, :] = gain_buf[0:1, :] + jnp.sum(gain_terms, axis=0, keepdims=True)
+
+    tiles(owned // 64, input_tile)
+    shown = copies.local(own_out, o_input.at[own_rows])
+    shown_far = copies.push(own_out, o_input.at[own_rows], here.across)
+    outs = [copies.local(small, o_small), copies.local(gain_buf, o_gains), shown]
+
+    sent = [shown_far]
+
+    def deliver(piece_of, dst):
+        for d in range(SHARE):
+            src = piece_of(here.shares[d])
+            if d == 0:
+                outs.append(copies.local(src, dst))
+            else:
+                sent.append(copies.push(src, dst, here.members[d]))
+
+    z_d.finish(stage)
+    deliver(lambda t: gd.at[0, :, part(t, owned)], o_gd.at[part(share, unit_width), :])
+    z_u.finish(stage)
+    deliver(lambda t: gu.at[0, part(t, owned), :], o_gu.at[:, part(share, unit_width)])
+    z_o.finish(stage)
+    deliver(lambda t: go.at[0, :, part(t, owned)], o_go.at[part(share, head_width), :])
+    z_q.finish(stage)
+    for j in range(3):
+        deliver(
+            lambda t, j=j: gq.at[0, j, part(t, owned), :],
+            o_gq.at[j, :, part(share, head_width)],
+        )
+
+    for one in (z_d, z_u, z_o, z_q, reduce, gather):
+        one.drain()
+    for copy in sent:
+        copy.wait()
+    for copy in outs:
+        copy.wait()
+    copies.check()
 
 
 def plane(mesh):
@@ -1009,7 +1492,7 @@
         own_tokens = rel_tokens[:half].astype(wide)
         own_heads, own_widths = rel_heads[:half], rel_widths[:half]
         own_live = live_rows[:half]
-        own_normed, norm_heads_back = jax.vjp(norm_piece, own_tokens, norm_gains[0])
+        own_normed = norm_piece(own_tokens, norm_gains[0])
         gate_heads, route_heads_back = jax.vjp(
             partial(route_piece, bucket=own_heads),
             own_normed.astype(low).astype(wide),
@@ -1024,7 +1507,7 @@
         anywhere = pl.BlockSpec(memory_space=pl.ANY)
         vmem = pl.BlockSpec(memory_space=pltpu.VMEM)
         weights = [
-            shape(b16, 3, width, head_width),
+            shape(b16, width, 3 * head_width),
             shape(b16, head_width, width),
             shape(b16, width, units),
             shape(b16, units, width),
@@ -1037,9 +1520,10 @@
             shape(f32, half, width),
             shape(f32, half, width),
             shape(b16, plane_rows, width),
-            shape(f32, plane_rows, units),
+            shape(f32, plane_rows // 2, 2 * units),
             shape(f32, plane_rows, 3 * HD),
             shape(f32, SHARE, 8, rows),
+            shape(b16, plane_rows, width),
         ]
         (
             hidden_heads,
@@ -1052,6 +1536,7 @@
             upward,
             all_col,
             all_row,
+            all_cot,
             qkv_full,
             out_full,
             up_full,
@@ -1059,12 +1544,12 @@
         ) = pl.pallas_call(
             forward_kernel,
             out_shape=made + weights,
-            in_specs=[anywhere] * 7 + [vmem] * 2,
-            out_specs=[anywhere] * 14,
+            in_specs=[anywhere] * 8 + [vmem] * 2,
+            out_specs=[anywhere] * 15,
             scratch_shapes=[
                 pltpu.VMEM((plane_rows, width), b16),
                 pltpu.VMEM((plane_rows, width), b16),
-                pltpu.VMEM((3, width, head_width), b16),
+                pltpu.VMEM((width, 3 * head_width), b16),
                 pltpu.VMEM((head_width, width), b16),
                 pltpu.VMEM((width, units), b16),
                 pltpu.VMEM((units, width), b16),
@@ -1076,15 +1561,15 @@
                 pltpu.VMEM((plane_rows // 2, width), b16),
                 pltpu.VMEM((plane_rows // 2, width), b16),
                 pltpu.VMEM((plane_rows // 2, width), f32),
-                pltpu.VMEM((plane_rows // 2, width), b16),
-                pltpu.VMEM((plane_rows // 2, width), b16),
+                pltpu.VMEM((3 * half, width), b16),
+                pltpu.VMEM((3 * half, width), b16),
                 pltpu.VMEM((half, width), f32),
                 pltpu.VMEM((half, width), f32),
                 pltpu.VMEM((plane_rows, width), b16),
-                pltpu.VMEM((plane_rows, units), f32),
-                pltpu.SemaphoreType.DMA((24,)),
-                pltpu.SemaphoreType.DMA((64,)),
-                pltpu.SemaphoreType.DMA((64,)),
+                pltpu.VMEM((plane_rows // 2, 2 * units), f32),
+                pltpu.SemaphoreType.DMA((40,)),
+                pltpu.SemaphoreType.DMA((96,)),
+                pltpu.SemaphoreType.DMA((96,)),
             ],
             compiler_params=pltpu.CompilerParams(
                 collective_id=0, has_side_effects=True, vmem_limit_bytes=60 * 2**20
@@ -1093,6 +1578,7 @@
             rel_tokens,
             col,
             row,
+            relative(cotangent),
             jnp.transpose(qkv_weight, (1, 0, 2)),
             out_weight,
             up_weight,
@@ -1100,202 +1586,114 @@
             norm_gains,
             jnp.broadcast_to(gate_heads[:, None], (half, HD)),
         )
-        def gather_rows(arr):
-            pair = jnp.concatenate([arr, hop(arr, 2)], axis=0)
-            return jnp.concatenate([pair, hop(pair, 1)], axis=0)
-
-        def gather_halves(arr):
-            pair = jnp.concatenate([arr, cross(arr)], axis=0)
-            return gather_rows(pair)
-
-        def reduce_rows(keep, send):
-            total = keep + hop(send.astype(low), 1).astype(wide)
-            total = total.reshape(2, 2, half, width)
-            total = total[:, 0] + cross(total[:, 1].astype(low)).astype(wide)
-            return total[0] + hop(total[1].astype(low), 2).astype(wide)
-
-        def whole_rows(arr):
-            other = cross(arr)
-            return jnp.where(
-                side == 0,
-                jnp.concatenate([arr, other], axis=0),
-                jnp.concatenate([other, arr], axis=0),
-            )
-
-        def partial_rows(left_in, matrix, product):
-            keep = product(left_in[: 4 * half], matrix)
-            send = product(left_in[4 * half :], matrix)
-            return reduce_rows(keep, send)
-
-        chain = [None, None]
-
-        def ring(moved, stream):
-            if chain[stream] is not None:
-                moved, _ = lax.optimization_barrier((moved, chain[stream]))
-            got = lax.ppermute(
-                moved, "fsdp", [(i, (i + SHARE) % fsdp) for i in range(fsdp)]
-            )
-            chain[stream] = got
-            return got
-
-        def place_at(step):
-            return (place - step) % ring_size
-
-        def ring_reduce(term):
-            moving = [None, None]
-            for step in range(1, ring_size):
-                for s in range(2):
-                    piece = term(place_at(step), s)
-                    if moving[s] is not None:
-                        piece = piece + moving[s].astype(wide)
-                    moving[s] = piece.astype(low)
-                for s in range(2):
-                    moving[s] = ring(moving[s], s)
-            return [term(place, s) + moving[s].astype(wide) for s in range(2)]
-
-        def scatter_back(parts, axis):
-            joined = jnp.concatenate(parts, axis=0)
-            other = 1 - axis
-            out_dims = list(joined.shape)
-            out_dims[axis] = owned
-            stride = out_dims[other]
-            out_dims[other] *= SHARE
-            out = jnp.zeros(out_dims, wide)
-            for bits in range(SHARE):
-                piece = lax.dynamic_slice_in_dim(joined, (share ^ bits) * owned, owned, axis)
-                if bits:
-                    piece = hop(piece.astype(low), bits).astype(wide)
-                out = lax.dynamic_update_slice_in_dim(out, piece, (share ^ bits) * stride, other)
-            return out
-
-        all_cot = gather_rows(relative(cotangent))
+
         own_units = hidden_units[:half]
-        _, norm_units_back = jax.vjp(norm_piece, middle, norm_gains[1])
         gate_units, route_units_back = jax.vjp(
             partial(route_piece, bucket=own_widths),
             own_units.astype(wide),
             router_first[1],
             router_second[1],
         )
-        all_gates = gather_halves(gate_units[:, None])
-        all_heads = all_col[:, 2 * HD + 2].astype(jnp.int32)
-        all_widths = all_col[:, 2 * HD + 3].astype(jnp.int32)
-        live_all = all_col[:, 2 * HD + 4] > 0.5
-        cosine = all_col[:, : HD // 2].reshape(SHARE, rows, 1, HD // 2)
-        sine_table = all_col[:, HD + HD // 2 : 2 * HD].reshape(SHARE, rows, 1, HD // 2)
-        head_ids = side * (local_width // HD) + share * heads + jnp.arange(heads, dtype=jnp.int32)
-        head_used = head_ids[None, :] < HEADS // NB * (all_heads[:, None] + 1)
-        group_used = head_used.reshape(SHARE, rows, heads)
-        unit_ids = side * local_units + share * units + jnp.arange(units, dtype=jnp.int32)
-        unit_used = unit_ids[None, :] < FF // NB * (all_widths[:, None] + 1)
-        scale = HD ** (-0.5)
-        probs = probs.reshape(SHARE, heads, rows, rows)
-        probs_low = probs.astype(low)
-        groups = qkvb.reshape(SHARE, rows, 3, heads, HD)
-        query, keyed, value = groups[:, :, 0], groups[:, :, 1], groups[:, :, 2]
-        qkv_mat = jnp.transpose(qkv_full, (1, 0, 2)).reshape(width, 3 * head_width)
-
-        def to_groups(arr):
-            return arr.reshape((SHARE, rows) + arr.shape[1:])
-
-        def from_groups(arr):
-            return arr.reshape((plane_rows,) + arr.shape[2:])
-
-        activated = jnp.where(unit_used, jnp.square(jax.nn.relu(upward)), 0.0).astype(low)
-        grad_top_all = jnp.where(live_all[:, None], all_cot.astype(wide), 0.0)
-        grad_down_in = (all_gates * grad_top_all).astype(low)
-
-        def down_term(at, s):
-            mid = units // 2
-            return dot_rows(
-                activated[:, s * mid : (s + 1) * mid],
-                lax.dynamic_slice_in_dim(grad_down_in, at * block, block, 1),
-            )
-
-        grad_down = scatter_back(ring_reduce(down_term), 1)
-
-        downward = partial_rows(activated, down_full, dot)
-        own_out = jnp.where(
-            own_live[:, None], middle + gate_units[:, None] * downward, 0.0
-        ).astype(low)
-        block_out = whole_rows(own_out)
-        grad_top = jnp.where(own_live[:, None], own_half(cotangent).astype(wide), 0.0)
-        grad_gate_units = jnp.sum(grad_top * downward, axis=1)
-
-        grad_act = dot_cols(grad_down_in, down_full)
-        grad_up_in = jnp.where(unit_used, 2.0 * jax.nn.relu(upward) * grad_act, 0.0).astype(low)
-
-        def up_term(at, s):
-            mid = block // 2
-            return dot_rows(
-                lax.dynamic_slice_in_dim(hidden_units, at * block + s * mid, mid, 1), grad_up_in
-            )
-
-        grad_up = scatter_back(ring_reduce(up_term), 0)
-        route_units_grads = route_units_back(grad_gate_units)
-        grad_hidden_units = partial_rows(grad_up_in, up_full, dot_cols) + route_units_grads[0]
-        norm_units_grads = norm_units_back(grad_hidden_units)
-        grad_middle = grad_top + norm_units_grads[0]
-        grad_gate_heads = jnp.sum(grad_middle * projected, axis=1)
-        grad_projected = gather_halves((gate_heads[:, None] * grad_middle).astype(low))
-
-        def out_term(at, s):
-            mid = head_width // 2
-            return dot_rows(
-                attended[:, s * mid : (s + 1) * mid],
-                lax.dynamic_slice_in_dim(grad_projected, at * block, block, 1),
-            )
-
-        grad_out = scatter_back(ring_reduce(out_term), 1)
-        grad_attended = to_groups(
-            dot_cols(grad_projected, out_full).astype(low).reshape(plane_rows, heads, HD)
-        )
-        grad_attended = jnp.where(group_used[..., None], grad_attended, jnp.zeros((), low))
-        grad_value = jnp.einsum(
-            "ghqk,gqhe->gkhe", probs_low, grad_attended, preferred_element_type=wide
-        )
-        grad_probs = jnp.einsum(
-            "gqhe,gkhe->ghqk", grad_attended, value, preferred_element_type=wide
-        )
-        row_dot = jnp.sum(probs * grad_probs, axis=-1, keepdims=True)
-        grad_scores = (probs * (grad_probs - row_dot)).astype(low)
-        grad_query = (
-            jnp.einsum("ghqk,gkhe->gqhe", grad_scores, keyed, preferred_element_type=wide) * scale
-        )
-        grad_keyed = (
-            jnp.einsum("ghqk,gqhe->gkhe", grad_scores, query, preferred_element_type=wide) * scale
-        )
-        grad_qkv_in = jnp.stack(
-            [
-                rotate(grad_query, cosine, -sine_table),
-                rotate(grad_keyed, cosine, -sine_table),
-                grad_value,
+        all_gates = route_piece(
+            hidden_units.astype(wide),
+            router_first[1],
+            router_second[1],
+            bucket=all_col[:, 2 * HD + 3].astype(jnp.int32),
+        )
+        ones = jnp.ones((half,), wide)
+        slope_units = route_units_back(ones)[0]
+        slope_heads = route_heads_back(ones)[0]
+        (
+            block_out,
+            input_grad,
+            raw_qkv,
+            raw_out,
+            raw_up,
+            raw_down,
+            gate_grads,
+            gain_sums,
+            *_,
+        ) = pl.pallas_call(
+            backward_kernel,
+            out_shape=[
+                shape(b16, rows, width),
+                shape(b16, rows, width),
+                shape(b16, 3, owned, local_width),
+                shape(b16, local_width, owned),
+                shape(b16, owned, local_units),
+                shape(b16, local_units, owned),
+                shape(f32, 2, half, HD),
+                shape(f32, 8, width),
+                shape(b16, 4, 3, block, head_width),
+                shape(b16, 4, head_width, block),
+                shape(b16, 4, block, units),
+                shape(b16, 4, units, block),
             ],
-            axis=2,
-        ).astype(low)
-        grad_qkv_in = from_groups(grad_qkv_in).reshape(plane_rows, 3 * head_width)
-
-        def qkv_term(at, s):
-            mid = block // 2
-            return dot_rows(
-                lax.dynamic_slice_in_dim(hidden_heads, at * block + s * mid, mid, 1), grad_qkv_in
-            )
-
-        qkv_parts = ring_reduce(qkv_term)
-        joined = jnp.concatenate(qkv_parts, axis=0)
-        grad_qkv = jnp.zeros((owned, 3, local_width), wide)
-        for bits in range(SHARE):
-            piece = lax.dynamic_slice_in_dim(joined, (share ^ bits) * owned, owned, 0)
-            if bits:
-                piece = hop(piece.astype(low), bits).astype(wide)
-            grad_qkv = lax.dynamic_update_slice_in_dim(
-                grad_qkv, piece.reshape(owned, 3, head_width), (share ^ bits) * head_width, 2
-            )
-
-        route_heads_grads = route_heads_back(grad_gate_heads)
-        grad_hidden_heads = partial_rows(grad_qkv_in, qkv_mat, dot_cols) + route_heads_grads[0]
-        norm_heads_grads = norm_heads_back(grad_hidden_heads)
-        input_grad = whole_rows((grad_middle + norm_heads_grads[0]).astype(low))
+            in_specs=[anywhere] * 15 + [vmem] * 5,
+            out_specs=[anywhere] * 12,
+            scratch_shapes=[
+                pltpu.VMEM((plane_rows, width), b16),
+                pltpu.VMEM((head_width, width), b16),
+                pltpu.VMEM((width, units), b16),
+                pltpu.VMEM((units, width), b16),
+                pltpu.VMEM((plane_rows, 3 * HD), f32),
+                pltpu.VMEM((plane_rows, 3 * head_width), b16),
+                pltpu.VMEM((SHARE * heads * rows, rows), f32),
+                pltpu.VMEM((plane_rows, head_width), b16),
+                pltpu.VMEM((plane_rows, width), b16),
+                pltpu.VMEM((plane_rows, units), b16),
+                pltpu.VMEM((plane_rows, units), b16),
+                pltpu.VMEM((plane_rows // 2, width), f32),
+                pltpu.VMEM((plane_rows // 2, width), b16),
+                pltpu.VMEM((plane_rows // 2, width), b16),
+                pltpu.VMEM((3 * half, width), b16),
+                pltpu.VMEM((3 * half, width), b16),
+                pltpu.VMEM((half, width), f32),
+                pltpu.VMEM((half, width), f32),
+                pltpu.VMEM((4, units, block), b16),
+                pltpu.VMEM((4, block, units), b16),
+                pltpu.VMEM((4, head_width, block), b16),
+                pltpu.VMEM((4, 3, block, head_width), b16),
+                pltpu.VMEM((3, block, units), b16),
+                pltpu.VMEM((half, width), b16),
+                pltpu.VMEM((half, width), b16),
+                pltpu.VMEM((half, width), b16),
+                pltpu.VMEM((8, width), f32),
+                pltpu.VMEM((2, half, HD), f32),
+                pltpu.SemaphoreType.DMA((96,)),
+                pltpu.SemaphoreType.DMA((96,)),
+                pltpu.SemaphoreType.DMA((96,)),
+                pltpu.SemaphoreType.REGULAR((3,)),
+            ],
+            compiler_params=pltpu.CompilerParams(
+                collective_id=1, has_side_effects=True, vmem_limit_bytes=63 * 2**20
+            ),
+        )(
+            hidden_heads,
+            qkvb,
+            probs,
+            attended,
+            projected,
+            middle,
+            hidden_units,
+            upward,
+            all_col,
+            all_cot,
+            rel_tokens,
+            qkv_full,
+            out_full,
+            up_full,
+            down_full,
+            norm_gains,
+            jnp.broadcast_to(gate_heads[:, None], (half, HD)),
+            jnp.broadcast_to(all_gates[:, None], (plane_rows, HD)),
+            slope_units,
+            slope_heads,
+        )
+        grad_qkv = jnp.transpose(raw_qkv, (1, 0, 2)).astype(wide)
+        grad_out, grad_up, grad_down = (a.astype(wide) for a in (raw_out, raw_up, raw_down))
+        route_units_grads = route_units_back(gate_grads[0, :, 0])
+        route_heads_grads = route_heads_back(gate_grads[1, :, 0])
 
         def total_small(arr):
             arr = arr + cross(arr)
@@ -1332,11 +1730,11 @@
         )
         units_small = total_small(
             jnp.concatenate(
-                [norm_units_grads[1], route_units_grads[2].reshape(-1), head_counts, width_counts]
+                [gain_sums[1], route_units_grads[2].reshape(-1), head_counts, width_counts]
             )
         )
         heads_small = total_small(
-            jnp.concatenate([norm_heads_grads[1], route_heads_grads[2].reshape(-1)])
+            jnp.concatenate([gain_sums[0], route_heads_grads[2].reshape(-1)])
         )
         first_units = total_large(route_units_grads[1])
         first_heads = total_large(route_heads_grads[1])

time: 817 us -> 643 us (0.79)
  waiting for transfers between devices: 298 us -> 55 us
  Pallas kernels: 224 us -> 458 us
  local copies, waits for them, and re-layouts: 70.2 us -> 12.6 us
  other arithmetic: 81.8 us -> 28.3 us
  matrix products: 77.1 us -> 26.6 us
    pallas_call x0 -> x1, Pallas kernels: none -> 233 us  [shards(): pl.pallas_call(backward_kernel, out_shape=[shape(b16, rows, width), shape...]
    ppermute x24 -> x0, waiting for transfers between devices: 152 us -> none  [ring(): lax.ppermute(moved, 'fsdp', [(i, (i + SHARE) % fsdp) for i in range(fsdp)])]
    dot_general x44 -> x0, matrix products: 58.9 us -> none  [the longest x32 30.9 us: dot_rows(): lax.dot_general(left_in, right_in, (((0,), (0,)), ((), ())), preferred_el...]
    ppermute x48 -> x24, waiting for transfers between devices: 81.9 us -> 27 us  [hop(): return lax.ppermute(moved, 'fsdp', [(i, i ^ bits) for i in range(fsdp)])]
    ppermute x13 -> x6, waiting for transfers between devices: 64.3 us -> 28.1 us  [cross(): return lax.ppermute(moved, 'tensor', [(0, 1), (1, 0)])]
    ppermute x48 -> x24, starting transfers between devices: 31.4 us -> 44.4 us  [hop(): return lax.ppermute(moved, 'fsdp', [(i, i ^ bits) for i in range(fsdp)])]
    unnamed x230 -> x28, local copies, waits for them, and re-layouts: 15.4 us -> 3.93 us
    slice x7 -> x2, local copies, waits for them, and re-layouts: 11.1 us -> 1.65 us  [the longest x1 0.93 us: shards(): gain_sums[0]]
  transfers between devices with their start and end apart: 85 -> 30, of which waited for: 54 -> 18; matrix products, arithmetic and copies ran while one was open for 23% -> 4% of each run, Pallas kernels for 0% -> 0%
where the time goes in v3:
time: 643 us; the launch traced here: 634 us
  Pallas kernels  458 us (71%)
  waiting for transfers between devices  55 us (9%)
  starting transfers between devices  52 us (8%)
  other arithmetic  28.3 us (4%)
  matrix products  26.6 us (4%)
  local copies, waits for them, and re-layouts  12.6 us (2%)
    pallas_call x1, Pallas kernels, shards(): pl.pallas_call(backward_kernel, out_shape=[shape(b16, rows, width), shape...  233 us
    pallas_call x1, Pallas kernels, shards(): pl.pallas_call(forward_kernel, out_shape=made + weights, in_specs=[anywhe...  224 us
    ppermute x24, starting transfers between devices, hop(): return lax.ppermute(moved, 'fsdp', [(i, i ^ bits) for i in range(fsdp)])  44.4 us
    ppermute x6, waiting for transfers between devices, cross(): return lax.ppermute(moved, 'tensor', [(0, 1), (1, 0)])  28.1 us
    ppermute x24, waiting for transfers between devices, hop(): return lax.ppermute(moved, 'fsdp', [(i, i ^ bits) for i in range(fsdp)])  27 us
    dot_general x7, matrix products, route_piece(): inner = jax.nn.silu(jnp.dot(hidden_in, router_in, precision=highest))  22.8 us
  transfers between devices with their start and end apart: 30, of which 18 were waited for; matrix products, arithmetic and copies ran while one was open for 4% of the time, Pallas kernels for 0%

profile of v3, /device:TPU:0, one launch (start us, length us, event | category | flops | bytes accessed | tf_op | source)
XLA Modules:
  0.0 633.6 jit_solution(6187880769678863093)
XLA Ops:
  0.7 1.2 fusion.15
  2.7 2.6 fusion.8
  12.0 224.3 %shard_map.195 = (bf16[1024,2048]{1,0:T(8,128)(2,1)}, bf16[1024,768]{1,0:T(8,128)(2,1)}, f32[2048,256]{1,0:T(8,128)}, bf16[1024,256]{1,0:T(8,128)(2,1)}, f32[128...) custom-call(bf16[256,2048]{1,0:T(8,128)(2,1)} %pad_maximum_fusion.1., ...), custom_call_target="tpu_custom_call" | custom-call | tf_op jit(solution)/shard_map/pallas_call | solution.py:1544
  236.3 2.6 fusion.2
  238.9 6.2 fusion.4
  245.9 4.8 fusion.slope_units
  250.7 1.2 fusion.146
  251.9 1.4 convert_reduce_fusion
  253.8 3.2 fusion.6.slope_heads
  258.0 233.2 %shard_map.196 = (bf16[256,2048]{1,0:T(8,128)(2,1)}, bf16[256,2048]{1,0:T(8,128)(2,1)}, bf16[3,128,1024]{2,1,0:T(8,128)(2,1)}, bf16[1024,128]{1,0:T(8,128)(2,1)}...) custom-call(bf16[1024,2048]{1,0:T(8,128)(2,1)} %get-tuple-element.32, ...), custom_call_target="tpu_custom_call" | custom-call | tf_op jit(solution)/shard_map/pallas_call | solution.py:1616
  492.7 1.2 fusion.28
  494.9 2.1 fusion.25
  497.0 1.3 copy-done.1
  499.4 1.5 dynamic-slice_add_fusion.1
  502.4 1.4 dynamic-slice_add_fusion
  505.3 10.5 %collective-permute-done.11 = f32[512,256]{1,0:T(8,128)S(1)} collective-permute-done((f32[512,256]{1,0:T(8,128)S(1)}, f32[512,256]{1,0:T(8,128)S(1)}, u32[]{:S(2)}, u32[]{:S(2)}) %collective-permute-start.11) | collective-permute-done | bytes 524320 | tf_op jit(solution)/shard_map/ppermute | solution.py:1432
  516.9 9.8 %collective-permute-done.21 = f32[512,256]{1,0:T(8,128)} collective-permute-done((f32[512,256]{1,0:T(8,128)}, f32[512,256]{1,0:T(8,128)}, u32[]{:S(2)}, u32[]{:S(2)}) %collective-permute-start.21) | collective-permute-done | bytes 524320 | tf_op jit(solution)/shard_map/ppermute | solution.py:1432
  526.7 1.1 dynamic-slice_add_fusion.2
  528.9 21.1 %collective-permute-start.13 = (f32[128,256]{1,0:T(8,128)S(1)}, f32[128,256]{1,0:T(8,128)S(1)}, u32[]{:S(2)}, u32[]{:S(2)}) collective-permute-start(f32[128,256]{1,0:T(8,128)S(1)} %constant_dynamic-slice_fusion.6), channel_id=1, source_target_pairs={{0,8},{2,10},{4,12},{6,14},{8,0},{10,2},{12,4},{14,6},{16,24},{18,... | collective-permute-start | bytes 393224 | tf_op jit(solution)/shard_map/ppermute | solution.py:1429
  550.1 7.2 %collective-permute-start.23 = (f32[128,256]{1,0:T(8,128)S(1)}, f32[128,256]{1,0:T(8,128)S(1)}, u32[]{:S(2)}, u32[]{:S(2)}) collective-permute-start(f32[128,256]{1,0:T(8,128)S(1)} %constant_dynamic-slice_fusion.1), channel_id=1, source_target_pairs={{0,8},{2,10},{4,12},{6,14},{8,0},{10,2},{12,4},{14,6},{16,24},{18,... | collective-permute-start | bytes 393224 | tf_op jit(solution)/shard_map/ppermute | solution.py:1429
  557.4 3.5 collective-permute-done.23
  561.0 1.9 collective-permute-done.14
  564.0 1.9 collective-permute-start.24
  565.9 2.3 collective-permute-done.15
  568.3 1.5 collective-permute-done.24
  569.8 2.0 collective-permute-start.25
  571.9 1.4 collective-permute-done.16
  573.3 1.3 collective-permute-start.17
  574.5 1.3 collective-permute-done.25
  576.3 4.5 collective-permute-done.26
  581.0 2.1 collective-permute-start.18
  584.1 3.3 collective-permute-done.27
  588.0 2.0 collective-permute-start
  590.1 5.8 collective-permute-done.18
  595.9 1.3 maximum_select_fusion.2
  597.9 2.1 collective-permute-start.5
  600.0 2.0 collective-permute-done.28
  602.8 1.6 collective-permute-done.1
  604.4 1.7 collective-permute-start.2
  606.5 1.6 collective-permute-done.2
  610.2 1.6 collective-permute-done.3
  611.8 1.5 collective-permute-start.4
  614.8 2.5 convert_bitcast_fusion
  617.3 2.8 convert_element_type.64
  620.1 1.5 convert_element_type.65
  624.8 1.9 maximum_select_fusion
  626.7 1.8 maximum_select_fusion.1
  628.6 2.3 pad_maximum_fusion
  (171 shorter events, 32.8 us)
Async XLA Ops:
  0.6 4.7 copy-start.9
  0.7 5.0 copy-start.10
  0.7 5.1 copy-start.12
  2.0 5.4 copy-start.11
  2.7 5.7 copy-start.4
  2.7 5.7 copy-start.7
  250.7 3.1 copy-start
  494.0 5.4 collective-permute-start.10
  497.0 1.3 copy-start.1
  499.4 3.0 collective-permute-start.20
  499.4 3.0 copy-start.2
  501.0 14.8 %collective-permute-start.11 = (f32[512,256]{1,0:T(8,128)S(1)}, f32[512,256]{1,0:T(8,128)S(1)}, u32[]{:S(2)}, u32[]{:S(2)}) collective-permute-start(f32[512,256]{1,0:T(8,128)S(1)} %constant_dynamic-slice_fusion.8), channel_id=1, source_target_pairs={{0,1},{1,0},{2,3},{3,2},{4,5},{5,4},{6,7},{7,6},{8,9},{9,8},{10,11... | collective-permute-start | bytes 1572872 | tf_op jit(solution)/shard_map/ppermute | solution.py:1432
  504.6 22.1 %collective-permute-start.21 = (f32[512,256]{1,0:T(8,128)}, f32[512,256]{1,0:T(8,128)}, u32[]{:S(2)}, u32[]{:S(2)}) collective-permute-start(f32[512,256]{1,0:T(8,128)} %constant_dynamic-slice_fusion.3), channel_id=1, source_target_pairs={{0,1},{1,0},{2,3},{3,2},{4,5},{5,4},{6,7},{7,6},{8,9},{9,8},{10,11... | collective-permute-start | bytes 1572872 | tf_op jit(solution)/shard_map/ppermute | solution.py:1432
  515.9 13.0 %collective-permute-start.12 = (f32[256,256]{1,0:T(8,128)S(1)}, f32[256,256]{1,0:T(8,128)S(1)}, u32[]{:S(2)}, u32[]{:S(2)}) collective-permute-start(f32[256,256]{1,0:T(8,128)S(1)} %constant_dynamic-slice_fusion.7), channel_id=1, source_target_pairs={{0,4},{2,6},{4,0},{6,2},{8,12},{10,14},{12,8},{14,10},{16,20},{18,... | collective-permute-start | bytes 786440 | tf_op jit(solution)/shard_map/ppermute | solution.py:1429
  527.9 22.2 %collective-permute-start.22 = (f32[256,256]{1,0:T(8,128)S(1)}, f32[256,256]{1,0:T(8,128)S(1)}, u32[]{:S(2)}, u32[]{:S(2)}) collective-permute-start(f32[256,256]{1,0:T(8,128)S(1)} %constant_dynamic-slice_fusion.2), channel_id=1, source_target_pairs={{0,4},{2,6},{4,0},{6,2},{8,12},{10,14},{12,8},{14,10},{16,20},{18,... | collective-permute-start | bytes 786440 | tf_op jit(solution)/shard_map/ppermute | solution.py:1429
  528.9 28.4 %collective-permute-start.13 = (f32[128,256]{1,0:T(8,128)S(1)}, f32[128,256]{1,0:T(8,128)S(1)}, u32[]{:S(2)}, u32[]{:S(2)}) collective-permute-start(f32[128,256]{1,0:T(8,128)S(1)} %constant_dynamic-slice_fusion.6), channel_id=1, source_target_pairs={{0,8},{2,10},{4,12},{6,14},{8,0},{10,2},{12,4},{14,6},{16,24},{18,... | collective-permute-start | bytes 393224 | tf_op jit(solution)/shard_map/ppermute | solution.py:1429
  550.1 10.8 %collective-permute-start.23 = (f32[128,256]{1,0:T(8,128)S(1)}, f32[128,256]{1,0:T(8,128)S(1)}, u32[]{:S(2)}, u32[]{:S(2)}) collective-permute-start(f32[128,256]{1,0:T(8,128)S(1)} %constant_dynamic-slice_fusion.1), channel_id=1, source_target_pairs={{0,8},{2,10},{4,12},{6,14},{8,0},{10,2},{12,4},{14,6},{16,24},{18,... | collective-permute-start | bytes 393224 | tf_op jit(solution)/shard_map/ppermute | solution.py:1429
  557.4 5.5 collective-permute-start.14
  562.9 5.3 collective-permute-start.15
  564.0 5.8 collective-permute-start.24
  568.2 5.0 collective-permute-start.16
  569.8 6.0 collective-permute-start.25
  573.3 7.7 %collective-permute-start.17 = (f32[256,256]{1,0:T(8,128)S(1)}, f32[256,256]{1,0:T(8,128)S(1)}, u32[]{:S(2)}, u32[]{:S(2)}) collective-permute-start(f32[256,256]{1,0:T(8,128)S(1)} %maximum_select_fusion.6), channel_id=1, source_target_pairs={{0,4},{2,6},{4,0},{6,2},{8,12},{10,14},{12,8},{14,10},{16,20},{18,... | collective-permute-start | bytes 786440 | tf_op jit(solution)/shard_map/ppermute | solution.py:1429
  575.8 5.0 collective-permute-start.26
  580.9 6.4 %collective-permute-start.27 = (f32[256,256]{1,0:T(8,128)S(1)}, f32[256,256]{1,0:T(8,128)S(1)}, u32[]{:S(2)}, u32[]{:S(2)}) collective-permute-start(f32[256,256]{1,0:T(8,128)S(1)} %maximum_select_fusion.7), channel_id=1, source_target_pairs={{0,4},{2,6},{4,0},{6,2},{8,12},{10,14},{12,8},{14,10},{16,20},{18,... | collective-permute-start | bytes 786440 | tf_op jit(solution)/shard_map/ppermute | solution.py:1429
  581.0 14.8 %collective-permute-start.18 = (f32[512,256]{1,0:T(8,128)S(1)}, f32[512,256]{1,0:T(8,128)}, u32[]{:S(2)}, u32[]{:S(2)}) collective-permute-start(f32[512,256]{1,0:T(8,128)S(1)} %maximum_select_fusion.4), channel_id=1, source_target_pairs={{0,1},{1,0},{2,3},{3,2},{4,5},{5,4},{6,7},{7,6},{8,9},{9,8},{10,11... | collective-permute-start | bytes 1572872 | tf_op jit(solution)/shard_map/ppermute | solution.py:1432
  587.4 14.6 %collective-permute-start.28 = (f32[512,256]{1,0:T(8,128)S(1)}, f32[512,256]{1,0:T(8,128)S(1)}, u32[]{:S(2)}, u32[]{:S(2)}) collective-permute-start(f32[512,256]{1,0:T(8,128)S(1)} %maximum_select_fusion.5), channel_id=1, source_target_pairs={{0,1},{1,0},{2,3},{3,2},{4,5},{5,4},{6,7},{7,6},{8,9},{9,8},{10,11... | collective-permute-start | bytes 1572872 | tf_op jit(solution)/shard_map/ppermute | solution.py:1432
  588.0 14.1 %collective-permute-start = (f32[3072]{0:T(1024)S(1)}, f32[3072]{0:T(1024)S(1)}, u32[]{:S(2)}, u32[]{:S(2)}) collective-permute-start(f32[3072]{0:T(1024)S(1)} %pad_maximum_fusion.4), channel_id=1, source_target_pairs={{0,1},{1,0},{2,3},{3,2},{4,5},{5,4},{6,7},{7,6},{8,9},{9,8},{10,11... | collective-permute-start | bytes 36872 | tf_op jit(solution)/shard_map/ppermute | solution.py:1432
  597.2 27.6 %collective-permute-start.19 = (f32[1024,256]{1,0:T(8,128)S(1)}, f32[1024,256]{1,0:T(8,128)}, u32[]{:S(2)}, u32[]{:S(2)}) collective-permute-start(f32[1024,256]{1,0:T(8,128)S(1)} %maximum_select_fusion.2), channel_id=1, source_target_pairs={{0,2},{2,0},{4,6},{6,4},{8,10},{10,8},{12,14},{14,12},{16,18},{18,... | collective-permute-start | bytes 3145736 | tf_op jit(solution)/shard_map/ppermute | solution.py:1429
  597.9 4.8 collective-permute-start.5
  602.0 24.7 %collective-permute-start.29 = (f32[1024,256]{1,0:T(8,128)S(1)}, f32[1024,256]{1,0:T(8,128)}, u32[]{:S(2)}, u32[]{:S(2)}) collective-permute-start(f32[1024,256]{1,0:T(8,128)S(1)} %maximum_select_fusion.3), channel_id=1, source_target_pairs={{0,2},{2,0},{4,6},{6,4},{8,10},{10,8},{12,14},{14,12},{16,18},{18,... | collective-permute-start | bytes 3145736 | tf_op jit(solution)/shard_map/ppermute | solution.py:1429
  602.1 2.3 collective-permute-start.1
  602.6 3.5 collective-permute-start.6
  604.4 3.7 collective-permute-start.2
  606.1 3.8 collective-permute-start.7
  608.1 3.7 collective-permute-start.3
  609.9 3.9 collective-permute-start.8
  611.8 10.6 %collective-permute-start.4 = (f32[3072]{0:T(1024)S(1)}, f32[3072]{0:T(1024)S(1)}, u32[]{:S(2)}, u32[]{:S(2)}) collective-permute-start(f32[3072]{0:T(1024)S(1)} %add.224), channel_id=1, source_target_pairs={{0,16},{2,18},{4,20},{6,22},{8,24},{10,26},{12,28},{14,30},{16,0},... | collective-permute-start | bytes 36872 | tf_op jit(solution)/shard_map/ppermute | solution.py:1429
  613.8 8.8 %collective-permute-start.9 = (f32[3080]{0:T(1024)S(1)}, f32[3080]{0:T(1024)S(1)}, u32[]{:S(2)}, u32[]{:S(2)}) collective-permute-start(f32[3080]{0:T(1024)S(1)} %add.229), channel_id=1, source_target_pairs={{0,16},{2,18},{4,20},{6,22},{8,24},{10,26},{12,28},{14,30},{16,0},... | collective-permute-start | bytes 36968 | tf_op jit(solution)/shard_map/ppermute | solution.py:1429
  617.3 2.9 copy-start.3
  620.1 1.5 copy-start.8
  628.6 2.3 copy-start.6
  630.9 1.6 copy-start.5

commit v4 on v1

--- a/solution.py
+++ b/solution.py
@@ -3,6 +3,8 @@
 import jax
 import jax.numpy as jnp
 from jax import lax
+from jax.experimental import pallas as pl
+from jax.experimental.pallas import tpu as pltpu
 from jax.sharding import PartitionSpec as P
 
 HEADS = 16
@@ -16,6 +18,7 @@
 highest = lax.Precision.HIGHEST
 low = jnp.bfloat16
 wide = jnp.float32
+MESH = pl.DeviceIdType.MESH
 
 
 def norm_piece(values_in, gain_row):
@@ -77,7 +80,7 @@
     return segment, position, live_rows
 
 
-def solution(mesh):
+def general(mesh):
     fsdp = mesh.shape["fsdp"]
     ring_size = fsdp // SHARE
 
@@ -495,6 +498,1257 @@
             usage,
         )
 
+    return shards
+
+
+def xor_one(index):
+    return index + 1 - 2 * (index % 2)
+
+
+class Plane:
+    def __init__(self):
+        self.rank = lax.axis_index("fsdp")
+        self.side = lax.axis_index("tensor")
+        self.share = self.rank % SHARE
+        self.place = self.rank // SHARE
+        core = xor_one(self.share)
+        mid = (self.share + 2) % SHARE
+        self.shares = [self.share, core, mid, SHARE - 1 - self.share]
+        self.core = {"fsdp": self.place * SHARE + core}
+        self.mid = {"fsdp": self.place * SHARE + mid}
+        self.both = {"fsdp": self.place * SHARE + self.shares[3]}
+        self.members = [None, self.core, self.mid, self.both]
+        self.across = {"tensor": 1 - self.side}
+        self.near_place = xor_one(self.place)
+        self.two_place = (self.place + 2) % 4
+        self.far_place = 3 - self.place
+        self.near = {"fsdp": self.near_place * SHARE + self.share}
+        self.two = {"fsdp": self.two_place * SHARE + self.share}
+        self.far = {"fsdp": self.far_place * SHARE + self.share}
+        self.inner = (self.place == 1) | (self.place == 2)
+        self.outer = (self.place == 0) | (self.place == 3)
+
+    def greet(self):
+        barrier = pltpu.get_barrier_semaphore()
+        peers = [self.core, self.mid, self.both, self.across, self.near, self.two, self.far]
+        for peer in peers:
+            pl.semaphore_signal(barrier, inc=1, device_id=peer, device_id_type=MESH)
+        pl.semaphore_wait(barrier, len(peers))
+
+
+class Copies:
+    def __init__(self, local_sems, send_sems, recv_sems):
+        self.local_sems, self.send_sems, self.recv_sems = local_sems, send_sems, recv_sems
+        self.locals, self.sends, self.recvs = 0, 0, 0
+
+    def check(self):
+        assert self.locals <= self.local_sems.shape[0]
+        assert self.sends <= self.send_sems.shape[0]
+        assert self.recvs <= self.recv_sems.shape[0]
+
+    def local(self, src, dst):
+        copy = pltpu.make_async_copy(src, dst, self.local_sems.at[self.locals])
+        self.locals += 1
+        copy.start()
+        return copy
+
+    def slot(self):
+        self.recvs += 1
+        return self.recvs - 1
+
+    def remote(self, src, dst, peer, slot=None):
+        if slot is None:
+            slot = self.slot()
+        copy = pltpu.make_async_remote_copy(
+            src_ref=src,
+            dst_ref=dst,
+            send_sem=self.send_sems.at[self.sends],
+            recv_sem=self.recv_sems.at[slot],
+            device_id=peer,
+            device_id_type=MESH,
+        )
+        self.sends += 1
+        return copy
+
+    def push(self, src, dst, peer):
+        copy = self.remote(src, dst, peer)
+        copy.start()
+        return copy
+
+
+class ZGather:
+    def __init__(self, here, copies, view):
+        self.here, self.copies, self.view, self.drained = here, copies, view, False
+
+    def start(self):
+        here, copies, view = self.here, self.copies, self.view
+        own = view(here.place)
+        self.two = copies.push(own, own, here.two)
+        self.near = copies.push(own, own, here.near)
+        slot = copies.slot()
+        self.far = copies.remote(own, own, here.far, slot)
+        pl.when(here.inner)(self.far.start)
+        passing = view(here.two_place)
+        self.passed = copies.remote(passing, passing, here.near, slot)
+        arriving = view(here.two_place), view(here.near_place), view(here.far_place)
+        self.arrivals = [
+            pltpu.make_async_remote_copy(
+                src_ref=dst,
+                dst_ref=dst,
+                send_sem=copies.send_sems.at[0],
+                recv_sem=copies.recv_sems.at[at],
+                device_id=here.two,
+                device_id_type=MESH,
+            )
+            for dst, at in zip(arriving, (slot - 2, slot - 1, slot))
+        ]
+
+    def forward(self):
+        self.arrivals[0].wait_recv()
+        pl.when(self.here.inner)(self.passed.start)
+
+    def arrive(self):
+        self.arrivals[1].wait_recv()
+        self.arrivals[2].wait_recv()
+
+    def drain(self):
+        if self.drained:
+            return
+        self.drained = True
+        self.two.wait_send()
+        self.near.wait_send()
+
+        @pl.when(self.here.inner)
+        def _():
+            self.far.wait_send()
+            self.passed.wait_send()
+
+
+def tiles(count, body):
+    def step(i, carry):
+        body(i)
+        return carry
+
+    lax.fori_loop(0, count, step, 0)
+
+
+def part(index, size):
+    return pl.ds(pl.multiple_of(index * size, size), size)
+
+
+class RowReduce:
+    def __init__(self, here, copies, bufs, acks=None):
+        self.here, self.copies, self.acks = here, copies, acks
+        (self.snd, self.rcv, self.acc, self.out, self.into) = bufs
+        self.sent = []
+
+    def begin(self):
+        for copy in self.sent:
+            copy.wait_send()
+        self.sent, self.core = [], []
+
+    def core_send(self, index):
+        rows = pl.ds(index * 256, 256)
+        self.core.append(self.copies.push(self.snd.at[rows], self.rcv.at[rows], self.here.core))
+
+    def add_core(self, first, count):
+        acc, rcv = self.acc, self.rcv
+
+        def body(i):
+            at = pl.ds(pl.multiple_of(first + i * 64, 64), 64)
+            acc[at, :] = acc[at, :] + rcv[at, :].astype(wide)
+
+        tiles(count // 64, body)
+
+    def round_out(self, first, count, extra=None):
+        acc, out, into = self.acc, self.out, self.into
+
+        def body(i):
+            at = pl.ds(pl.multiple_of(first + i * 64, 64), 64)
+            value = acc[at, :]
+            if extra is not None:
+                value = value + into[pl.ds(extra, 64), :].astype(wide)
+            out[pl.ds(pl.multiple_of(first - 128 + i * 64, 64), 64), :] = value.astype(low)
+
+        tiles(count // 64, body)
+
+    def diagonal(self):
+        for copy in self.core:
+            copy.wait_recv()
+        self.add_core(384, 128)
+        self.round_out(384, 128)
+        self.diag_x = self.copies.push(self.out.at[256:320], self.into.at[256:320], self.here.across)
+        self.diag_y = self.copies.push(self.out.at[320:384], self.into.at[320:384], self.here.mid)
+        self.add_core(128, 256)
+        self.round_out(128, 64)
+        self.round_out(320, 64)
+        self.add_core(0, 128)
+
+    def sides(self):
+        self.diag_y.wait_recv()
+        self.round_out(192, 64, 320)
+        self.over_x = self.copies.push(self.out.at[0:128], self.into.at[0:128], self.here.across)
+        self.diag_x.wait_recv()
+        self.round_out(256, 64, 256)
+        self.over_y = self.copies.push(self.out.at[128:256], self.into.at[128:256], self.here.mid)
+        self.sent = self.core + [self.diag_x, self.diag_y, self.over_x, self.over_y]
+
+    def arrive(self):
+        self.over_x.wait_recv()
+        self.over_y.wait_recv()
+
+    def total(self, at, size):
+        acc, into = self.acc, self.into
+        return (
+            acc[pl.ds(at, size), :]
+            + into[pl.ds(at, size), :].astype(wide)
+            + into[pl.ds(at + 128, size), :].astype(wide)
+        )
+
+    def release(self):
+        for index, peer in enumerate((self.here.core, self.here.across, self.here.mid)):
+            pl.semaphore_signal(
+                self.acks.at[index], inc=1, device_id=peer, device_id_type=MESH
+            )
+
+    def await_release(self):
+        for index in range(3):
+            pl.semaphore_wait(self.acks.at[index], 1)
+
+    def drain(self):
+        for copy in self.sent:
+            copy.wait_send()
+
+
+class RowGather:
+    def __init__(self, here, copies, view, fixed=False):
+        self.here, self.copies, self.view, self.fixed = here, copies, view, fixed
+        self.sent, self.drained = [], False
+
+    def start(self):
+        here = self.here
+        self.over_x = self.pair(0, 1, here.across)
+        self.over_y = self.pair(0, 2, here.mid)
+        self.cores = [self.pair(0, 4, here.core)]
+
+    def pair(self, source, target, peer, half=None):
+        src = self.view(source, half)
+        dst = src if self.fixed else self.view(target, half)
+        copy = self.copies.push(src, dst, peer)
+        self.sent.append(copy)
+        return copy
+
+    def forward(self):
+        here = self.here
+        self.over_y.wait_recv()
+        self.diag_x = self.pair(2, 3, here.across, 0)
+        self.cores.append(self.pair(2, 6, here.core))
+        self.over_x.wait_recv()
+        self.diag_y = self.pair(1, 3, here.mid, 1)
+        self.cores.append(self.pair(1, 5, here.core))
+
+    def finish(self):
+        self.diag_x.wait_recv()
+        self.diag_y.wait_recv()
+        self.cores.append(self.pair(3, 7, self.here.core))
+        for copy in self.cores:
+            copy.wait_recv()
+
+    def drain(self):
+        if not self.drained:
+            for copy in self.sent:
+                copy.wait_send()
+        self.drained = True
+
+
+def nn(left_in, right_in):
+    return lax.dot_general(
+        left_in, right_in, (((1,), (0,)), ((), ())), preferred_element_type=wide
+    )
+
+
+def nt(left_in, right_in):
+    return lax.dot_general(
+        left_in, right_in, (((1,), (1,)), ((), ())), preferred_element_type=wide
+    )
+
+
+def tn(left_in, right_in):
+    return lax.dot_general(
+        left_in, right_in, (((0,), (0,)), ((), ())), preferred_element_type=wide
+    )
+
+
+class ZReduce:
+    def __init__(self, here, copies, base, spot, rows, columns, landing):
+        self.here, self.copies, self.base, self.spot = here, copies, base, spot
+        self.rows, self.columns, self.landing = rows, columns, landing
+        self.slot_y1, self.slot_y2 = copies.slot(), copies.slot()
+
+    def view(self, k, rows=None, columns=None):
+        r, c = self.spot(k)
+        return self.base.at[
+            pl.ds(r, self.rows) if rows is None else rows(r),
+            pl.ds(c, self.columns) if columns is None else columns(c),
+        ]
+
+    def send_far(self):
+        here, copies = self.here, self.copies
+        self.y1 = copies.remote(self.view(3), self.landing.at[2], here.far, self.slot_y1)
+        self.y2 = copies.remote(self.view(3), self.landing.at[3], here.near, self.slot_y2)
+        pl.when(here.inner)(self.y1.start)
+        pl.when(here.outer)(self.y2.start)
+
+    def send_near(self):
+        self.near = self.copies.push(self.view(1), self.landing.at[0], self.here.near)
+
+    def load(self, index, stage, slot):
+        size = min(self.rows, 512)
+        return [
+            self.copies.local(
+                self.landing.at[index, pl.ds(n * size, size), :],
+                stage.at[slot, pl.ds(0, size), pl.ds(n * self.columns, self.columns)],
+            )
+            for n in range(self.rows // size)
+        ]
+
+    def add(self, target, stage, slots):
+        size = min(self.rows, 512)
+        r, c = self.spot(target)
+        for n in range(self.rows // size):
+
+            def body(i, n=n):
+                at = pl.ds(pl.multiple_of(i * 64, 64), 64)
+                mine = pl.ds(pl.multiple_of(r + n * size + i * 64, 64), 64)
+                lanes = pl.ds(c, self.columns)
+                value = self.base[mine, lanes].astype(wide)
+                for slot in slots:
+                    value = value + stage[
+                        slot, at, pl.ds(n * self.columns, self.columns)
+                    ].astype(wide)
+                self.base[mine, lanes] = value.astype(low)
+
+            tiles(size // 64, body)
+
+    def send_two(self, stage):
+        here, copies = self.here, self.copies
+
+        @pl.when(here.inner)
+        def _():
+            self.y2.wait_recv()
+            for copy in self.load(3, stage, 0):
+                copy.wait()
+            self.add(2, stage, [0])
+
+        self.two = copies.push(self.view(2), self.landing.at[1], here.two)
+
+    def finish(self, stage):
+        here = self.here
+        self.near.wait_recv()
+        self.two.wait_recv()
+        loads = self.load(0, stage, 0) + self.load(1, stage, 1)
+        for copy in loads:
+            copy.wait()
+        self.add(0, stage, [0, 1])
+
+        @pl.when(here.inner)
+        def _():
+            self.y1.wait_recv()
+            for copy in self.load(2, stage, 0):
+                copy.wait()
+            self.add(0, stage, [0])
+
+    def drain(self):
+        here = self.here
+        self.near.wait_send()
+        self.two.wait_send()
+        pl.when(here.inner)(self.y1.wait_send)
+        pl.when(here.outer)(self.y2.wait_send)
+
+
+def norm_back(value, grad, gain):
+    r = lax.rsqrt(jnp.mean(value * value, axis=-1, keepdims=True) + epsilon)
+    u = gain * grad
+    lean = jnp.mean(u * value, axis=-1, keepdims=True)
+    return r * u - value * (r * r * r * lean), grad * value * r
+
+
+def exact(left_in, right_in, contract):
+    return lax.dot_general(
+        left_in, right_in, (contract, ((), ())), precision=highest, preferred_element_type=wide
+    )
+
+
+def layer_kernel(
+    tok, col, row, cot_in, qkvw, outw, upw, downw, first, gains, second,
+    o_block, o_input, o_gq, o_go, o_gu, o_gd, o_first, o_pack, s_hid, s_wq, l_q, l_o, l_u, l_d,
+    toks, hid, units, cot, early, wo, wu, wd, cols, rows_info, qkvb, probs, att, acc,
+    snd, rcv, out_buf, in_buf, proj, mid_buf, go, stage, top, own_tok, own_out,
+    first_buf, slope, gates, r_gate, r_inner, r_slope, r_dpre, r_rows, zpart, zland, gain_buf,
+    pack, pack_plane, pack_side, pack_ring,
+    local_sems, send_sems, recv_sems, acks,
+):
+    here = Plane()
+    copies = Copies(local_sems, send_sems, recv_sems)
+    here.greet()
+    rank, share, side = here.rank, here.share, here.side
+    owned = 128
+    block = owned * SHARE
+    head_width = wo.shape[0]
+    unit_width = wu.shape[1]
+    heads = head_width // HD
+    own_rows = part(rank, owned)
+    wq = early.at[:, 0 : 3 * head_width]
+    act, gup = early.at[0:1024], early.at[1024:2048]
+    sent, outs, done = [], [], []
+
+    def to_peer(src, dst, peer):
+        copy = copies.push(src, dst, peer)
+        sent.append(copy)
+        return copy
+
+    def spread(src_of, dst):
+        return [
+            copies.local(src_of(here.shares[d]), dst)
+            if d == 0
+            else to_peer(src_of(here.shares[d]), dst, here.members[d])
+            for d in range(SHARE)
+        ]
+
+    def landed(got):
+        for i, copy in enumerate(got):
+            if i % SHARE:
+                copy.wait_recv()
+            else:
+                copy.wait()
+
+    got_q = []
+    for j in range(3):
+        got_q += spread(
+            lambda t: qkvw.at[j, :, part(t, head_width)],
+            wq.at[own_rows, j * head_width : (j + 1) * head_width],
+        )
+    mine, other = part(side, owned), part(1 - side, owned)
+
+    class Halves:
+        def __init__(self, src, dst):
+            self.dst = dst
+            pairs = ((mine, 0), (other, owned))
+            self.own = [copies.local(src(rows), dst(at)) for rows, at in pairs]
+            self.mid = [to_peer(src(rows), dst(at + 256), here.mid) for rows, at in pairs]
+            self.core = [to_peer(src(rows), dst(at + 512), here.core) for rows, at in pairs]
+
+        def pass_on(self):
+            for copy in self.mid:
+                copy.wait_recv()
+            self.last = [
+                to_peer(self.dst(at), self.dst(at + 512), here.core) for at in (256, 384)
+            ]
+
+    tok_in = Halves(lambda r: tok.at[r, :], lambda at: toks.at[at : at + owned])
+    col_in = Halves(lambda r: col.at[r, :], lambda at: cols.at[at : at + owned])
+    row_in = Halves(
+        lambda r: row.at[:, r],
+        lambda at: rows_info.at[at // 256, :, at % 256 : at % 256 + owned],
+    )
+    got_o = spread(lambda t: outw.at[part(t, head_width), :], wo.at[:, own_rows])
+    got_u = spread(lambda t: upw.at[:, part(t, unit_width)], wu.at[own_rows, :])
+    got_d = spread(lambda t: downw.at[part(t, unit_width), :], wd.at[:, own_rows])
+    cot_rows = Halves(lambda r: cot_in.at[r, :], lambda at: cot.at[at : at + owned])
+    in_first = copies.local(first.at[0], first_buf)
+    in_tok = copies.local(tok.at[mine, :], own_tok)
+
+    g_q = ZGather(here, copies, lambda k: wq.at[part(k, block), :])
+    g_o = ZGather(here, copies, lambda k: wo.at[:, part(k, block)])
+    g_u = [
+        ZGather(
+            here,
+            copies,
+            lambda k, h=h: wu.at[pl.ds(pl.multiple_of(k * block + h * 256, 256), 256), :],
+        )
+        for h in range(2)
+    ]
+    g_d = [
+        ZGather(here, copies, lambda k, h=h: wd.at[h * 512 : (h + 1) * 512, part(k, block)])
+        for h in range(2)
+    ]
+
+    def fact(at, index):
+        return cols[at, 2 * HD + index : 2 * HD + index + 1]
+
+    landed(got_q)
+    g_q.start()
+    landed(got_o)
+    g_o.start()
+
+    def normalise(base):
+        def body(i):
+            at = pl.ds(pl.multiple_of(base + i * 64, 64), 64)
+            x = toks[at, :].astype(wide)
+            r = lax.rsqrt(jnp.mean(x * x, axis=-1, keepdims=True) + epsilon)
+            hid[at, :] = (x * r * gains[0:1, :]).astype(low)
+
+        tiles(4, body)
+
+    def wait_all(waits):
+        for wait in waits:
+            wait()
+
+    wait_all([c.wait for c in tok_in.own])
+    normalise(0)
+    wait_all([c.wait_recv for c in tok_in.core])
+    normalise(512)
+    tok_in.pass_on()
+    normalise(256)
+    wait_all([c.wait_recv for c in tok_in.last])
+    normalise(768)
+    wait_all([c.wait for c in col_in.own + row_in.own])
+    col_in.pass_on()
+    row_in.pass_on()
+    wait_all([c.wait_recv for c in col_in.core + row_in.core + col_in.last + row_in.last])
+    save_hid = copies.local(hid, s_hid)
+
+    def route(index, rows_of):
+        made = exact(rows_of[0:owned, :].astype(wide), first_buf[...], ((1,), (0,)))
+        sig = 1.0 / (1.0 + jnp.exp(-made))
+        inner = made * sig
+        logits = exact(inner, second[index], ((1,), (0,)))
+        lane = lax.broadcasted_iota(jnp.int32, (owned, HD), 1)
+        logits = jnp.where(lane < NB, logits, -1e30)
+        raised = jnp.where(
+            lane < NB, jnp.exp(logits - jnp.max(logits, axis=-1, keepdims=True)), 0.0
+        )
+        shares = raised / jnp.sum(raised, axis=-1, keepdims=True)
+        hot = jnp.where(lane.astype(wide) == fact(pl.ds(0, owned), 2 + index), 1.0, 0.0)
+        gate = NB * jnp.sum(shares * hot, axis=-1, keepdims=True)
+        lean = gate * (hot - shares)
+        r_gate[index] = jnp.broadcast_to(gate, (owned, HD))
+        r_inner[index] = inner
+        r_slope[index] = lean
+        r_dpre[index] = exact(lean, second[index], ((1,), (1,))) * (
+            sig * (1.0 + made * (1.0 - sig))
+        )
+
+    def slope_tiles(index):
+        def body(i):
+            c = part(i, 256)
+            slope[:, c] = exact(r_dpre[index], first_buf[c, :], ((1,), (1,)))
+
+        tiles(8, body)
+
+    in_first.wait()
+    route(0, hid)
+    in_first = copies.local(first.at[1], first_buf)
+
+    g_q.forward()
+    landed(got_u)
+    g_u[0].start()
+    g_q.arrive()
+    save_wq = copies.local(wq, s_wq)
+
+    for j in range(3):
+
+        def qkv_tile(i, j=j):
+            at = part(i, 512)
+            made = nn(hid[at, :], wq[:, j * head_width : (j + 1) * head_width])
+            if j < 2:
+                cosine = cols[at, 0:HD]
+                sine = cols[at, HD : 2 * HD]
+                for h in range(heads):
+                    one = made[:, h * HD : (h + 1) * HD]
+                    turned = one * cosine + pltpu.roll(one, HD // 2, 1) * sine
+                    qkvb[at, j * head_width + h * HD : j * head_width + (h + 1) * HD] = (
+                        turned.astype(low)
+                    )
+            else:
+                qkvb[at, j * head_width : (j + 1) * head_width] = made.astype(low)
+
+        tiles(2, qkv_tile)
+
+    g_o.forward()
+    g_u[1].start()
+
+    first_head = (side * SHARE + share) * heads
+    scale = HD ** (-0.5)
+    for h in range(heads):
+        head = (first_head + h).astype(wide)
+
+        def attend_group(g, h=h, head=head):
+            at = part(g, 256)
+            query, keyed, value = (
+                qkvb[at, pl.ds(j * head_width + h * HD, HD)] for j in range(3)
+            )
+            info = rows_info[g]
+            seg_k, slot_k, bucket_k = info[0:1, :], info[1:2, :], info[2:3, :]
+            reach_k = jnp.where(4.0 * bucket_k + 4.0 > head, 1.0, 0.0)
+            slot_q = fact(at, 1)
+            usable = (reach_k > 0.5) | (slot_k == slot_q)
+            allowed = (fact(at, 0) == seg_k) & (slot_k <= slot_q) & usable
+            scores = jnp.where(allowed, nt(query, keyed) * scale, -1e30)
+            weights = jnp.exp(scores - jnp.max(scores, axis=-1, keepdims=True))
+            p = weights / jnp.sum(weights, axis=-1, keepdims=True)
+            probs[part(g * heads + h, 256), :] = p
+            mixed = nn(p.astype(low), value)
+            att[at, h * HD : (h + 1) * HD] = jnp.where(
+                4.0 * fact(at, 2) + 4.0 > head, mixed, 0.0
+            ).astype(low)
+
+        tiles(SHARE, attend_group)
+
+    reduce = RowReduce(here, copies, (snd, rcv, acc, out_buf, in_buf), acks)
+
+    def partial_sums(term):
+        reduce.begin()
+        for i in range(2):
+
+            def send_tile(n, i=i):
+                snd[i * 256 : (i + 1) * 256, part(n, 512)] = term(
+                    pl.ds(512 + i * 256, 256), n
+                ).astype(low)
+
+            tiles(4, send_tile)
+            reduce.core_send(i)
+
+        def own_tile(n):
+            acc[:, part(n, 512)] = term(pl.ds(0, 512), n)
+
+        tiles(4, own_tile)
+
+    g_o.arrive()
+    partial_sums(lambda at, n: nn(att[at, :], wo[:, part(n, 512)]))
+    reduce.diagonal()
+    reduce.sides()
+    g_u[0].forward()
+    landed(got_d)
+    g_d[0].start()
+    in_tok.wait()
+    reduce.arrive()
+
+    def row_tiles(body):
+        def step(i):
+            at = pl.multiple_of(i * 64, 64)
+            body(at, pl.ds(at, 64))
+
+        tiles(owned // 64, step)
+
+    def middle_tile(at, rows):
+        projected = reduce.total(at, 64)
+        proj[rows, :] = projected
+        middle = own_tok[rows, :].astype(wide) + r_gate[0, rows, 0:1] * projected
+        mid_buf[rows, :] = middle
+        r = lax.rsqrt(jnp.mean(middle * middle, axis=-1, keepdims=True) + epsilon)
+        units[rows, :] = (middle * r * gains[1:2, :]).astype(low)
+
+    row_tiles(middle_tile)
+    reduce.release()
+
+    def row_view(buf):
+        def view(k, h):
+            if h is None:
+                return buf.at[k * owned : (k + 1) * owned]
+            return buf.at[k * owned + h * 64 : k * owned + (h + 1) * 64]
+
+        return view
+
+    units_out = RowGather(here, copies, row_view(units))
+    units_out.start()
+    in_first.wait()
+    route(1, units)
+    gates[0:owned, :] = r_gate[1]
+    gates_out = RowGather(here, copies, row_view(gates))
+    gates_out.start()
+    units_out.forward()
+    slope_tiles(1)
+    gates_out.forward()
+    units_out.finish()
+    gates_out.finish()
+    in_first = copies.local(first.at[0], first_buf)
+    g_u[1].forward()
+    g_d[1].start()
+    for one in g_u:
+        one.arrive()
+
+    first_unit = (side * SHARE + share) * unit_width
+
+    def used_units(at, base, rows, columns):
+        lane = lax.broadcasted_iota(jnp.int32, (rows, columns), 1) + base
+        return lane.astype(wide) < (FF // NB) * (fact(at, 3) + 1.0)
+
+    save_wq.wait()
+    g_q.drain()
+
+    def up_tile(i):
+        m, n = i % 2, i // 2
+        at, c = part(m, 512), part(n, 512)
+        made = nn(units[at, :], wu[:, c])
+        acc[:, part(m * 2 + n, 512)] = made
+        relu = jnp.maximum(made, 0.0)
+        used = used_units(at, first_unit + n * 512, 512, 512)
+        act[at, c] = jnp.where(used, relu * relu, 0.0).astype(low)
+
+    tiles(4, up_tile)
+    wait_all([c.wait for c in cot_rows.own])
+    cot_rows.pass_on()
+    wait_all([c.wait_recv for c in cot_rows.core + cot_rows.last])
+
+    def live_cot(at):
+        return jnp.where(fact(at, 4) > 0.5, cot[at, :].astype(wide), 0.0)
+
+    for copy in tok_in.last + cot_rows.last:
+        copy.wait_send()
+        done.append(copy)
+
+    def keep_tile(at, rows):
+        top[rows, :] = live_cot(rows).astype(low)
+
+    row_tiles(keep_tile)
+
+    def scale_tile(i):
+        at = part(i, 64)
+        cot[at, :] = (gates[at, 0:1] * live_cot(at)).astype(low)
+
+    tiles(16, scale_tile)
+    g_d[0].forward()
+
+    gd, gu, gq = toks, hid, wd
+    blocks = [here.place, here.near_place, here.two_place, here.far_place]
+    z_d = ZReduce(here, copies, gd, lambda k: (0, k * block), unit_width, block, l_d)
+    z_u = ZReduce(
+        here, copies, gu, lambda k: (k % 2 * block, k // 2 * unit_width), block, unit_width, l_u
+    )
+    z_o = ZReduce(here, copies, go, lambda k: (k * head_width, 0), head_width, block, l_o)
+    z_q = ZReduce(
+        here, copies, gq, lambda k: (k % 2 * block, k // 2 * 1024), block, 3 * head_width, l_q
+    )
+
+    def down_block(k):
+        def body(i):
+            m = part(i, 512)
+            gd[m, k * block : (k + 1) * block] = tn(
+                act[:, m], cot[:, part(blocks[k], block)]
+            ).astype(low)
+
+        tiles(unit_width // 512, body)
+
+    down_block(3)
+    z_d.send_far()
+    down_block(2)
+    down_block(1)
+    z_d.send_near()
+    down_block(0)
+    for one in g_d:
+        if one is g_d[1]:
+            one.forward()
+        one.arrive()
+
+    def gup_tile(i):
+        m, n = i % 2, i // 2
+        at, c = part(m, 512), part(n, 512)
+        made = nt(cot[at, :], wd[c, :])
+        used = used_units(at, first_unit + n * 512, 512, 512)
+        relu = jnp.maximum(acc[:, part(m * 2 + n, 512)], 0.0)
+        gup[at, c] = jnp.where(used, 2.0 * relu * made, 0.0).astype(low)
+
+    tiles(4, gup_tile)
+    z_d.send_two(stage)
+
+    reduce.await_release()
+    partial_sums(lambda at, n: nn(act[at, :], wd[:, part(n, 512)]))
+    reduce.diagonal()
+
+    save_hid.wait()
+
+    def up_block(k):
+        r, c = k % 2 * block, k // 2 * unit_width
+
+        def body(i):
+            gu[r : r + block, pl.ds(pl.multiple_of(c + i * 512, 512), 512)] = tn(
+                units[:, part(blocks[k], block)], gup[:, part(i, 512)]
+            ).astype(low)
+
+        tiles(unit_width // 512, body)
+
+    up_block(3)
+    z_u.send_far()
+    reduce.sides()
+    up_block(2)
+    up_block(1)
+    z_u.send_near()
+    up_block(0)
+    reduce.arrive()
+
+    r_rows_out = [RowGather(here, copies, row_view(r_rows.at[i])) for i in range(2)]
+
+    def keep_gate(index, rows, grad_gate):
+        r_rows[index, rows, :] = (grad_gate * r_dpre[index, rows, :]).astype(low)
+        r_slope[index, rows, :] = grad_gate * r_slope[index, rows, :]
+        r_gate[index, rows, :] = jnp.broadcast_to(grad_gate, (64, HD))
+
+    def block_tile(at, rows):
+        downward = reduce.total(at, 64)
+        own_out[rows, :] = jnp.where(
+            fact(rows, 4) > 0.5, mid_buf[rows, :] + r_gate[1, rows, 0:1] * downward, 0.0
+        ).astype(low)
+        keep_gate(
+            1, rows, jnp.sum(top[rows, :].astype(wide) * downward, axis=-1, keepdims=True)
+        )
+
+    row_tiles(block_tile)
+    reduce.release()
+    r_rows_out[1].start()
+    shown = copies.local(own_out, o_block.at[mine])
+    shown_far = to_peer(own_out, o_block.at[mine], here.across)
+
+    reduce.await_release()
+    partial_sums(lambda at, n: nt(gup[at, :], wu[part(n, 512), :]))
+    for one in g_u:
+        one.drain()
+    in_wq = copies.local(s_wq, wu.at[:, 0 : 3 * head_width])
+    r_rows_out[1].forward()
+    reduce.diagonal()
+    r_rows_out[1].finish()
+
+    column = share * 2 + side
+    places = [here.place, here.near_place, here.two_place, here.far_place]
+    planes = [None, here.near, here.two, here.far]
+
+    def first_rows(index, k, h):
+        target = here.shares[k // 4 + k // 2 % 2 * 2] * 2 + (side if k % 2 == 0 else 1 - side)
+        base = target * 256
+        if h is None:
+            return o_first.at[index, pl.ds(pl.multiple_of(base, 256), 256), :]
+        return o_first.at[index, pl.ds(pl.multiple_of(base + h * 128, 128), 128), :]
+
+    first_out = [
+        RowGather(here, copies, lambda k, h, i=i: first_rows(i, k, h), True) for i in range(2)
+    ]
+
+    class FirstSum:
+        def __init__(self, index, rows_of):
+            self.index = index
+            made = tn(rows_of[:, part(column, 256)], r_rows[index])
+            zpart[index] = made.astype(low)
+            slot = here.place
+            self.got = []
+            for k in range(4):
+                src = zpart.at[index, part(places[k], 64), :]
+                dst = zland.at[index, slot]
+                self.got.append(
+                    copies.local(src, dst) if k == 0 else to_peer(src, dst, planes[k])
+                )
+
+        def add(self):
+            index = self.index
+            landed(self.got)
+            for copy in self.got[1:]:
+                copy.wait_send()
+                done.append(copy)
+            total = zland[index, 0].astype(wide)
+            for k in range(1, 4):
+                total = total + zland[index, k].astype(wide)
+            zpart[index, 0:64, :] = total.astype(low)
+            at = pl.ds(pl.multiple_of(column * 256 + here.place * 64, 64), 64)
+            src, dst = zpart.at[index, 0:64, :], o_first.at[index, at, :]
+            self.got = [
+                copies.local(src, dst) if k == 0 else to_peer(src, dst, planes[k])
+                for k in range(4)
+            ]
+
+        def show(self):
+            landed(self.got)
+            first_out[self.index].start()
+
+    sum_units = FirstSum(1, units)
+    units_out.drain()
+    in_hid = copies.local(s_hid, units)
+    z_u.send_two(stage)
+    reduce.sides()
+    sum_units.add()
+    reduce.arrive()
+    gproj = cot
+    gain_buf[...] = jnp.zeros_like(gain_buf)
+
+    def grad_tile(at, rows):
+        grad = reduce.total(at, 64) + r_gate[1, rows, 0:1] * slope[rows, :]
+        back, gain_terms = norm_back(mid_buf[rows, :], grad, gains[1:2, :])
+        grad_middle = top[rows, :].astype(wide) + back
+        mid_buf[rows, :] = grad_middle
+        gproj[rows, :] = (r_gate[0, rows, 0:1] * grad_middle).astype(low)
+        keep_gate(0, rows, jnp.sum(grad_middle * proj[rows, :], axis=-1, keepdims=True))
+        gain_buf[1:2, :] = gain_buf[1:2, :] + jnp.sum(gain_terms, axis=0, keepdims=True)
+
+    row_tiles(grad_tile)
+    reduce.release()
+    gproj_out = RowGather(here, copies, row_view(gproj))
+    gproj_out.start()
+    r_rows_out[0].start()
+    in_first.wait()
+    slope_tiles(0)
+    gproj_out.forward()
+    sum_units.show()
+    r_rows_out[0].forward()
+    z_d.finish(stage)
+
+    def deliver(piece_of, dst):
+        for d in range(SHARE):
+            src = piece_of(here.shares[d])
+            if d == 0:
+                outs.append(copies.local(src, dst))
+            else:
+                sent.append(copies.push(src, dst, here.members[d]))
+                owed.append(sent[-1])
+
+    owed = []
+    deliver(lambda t: gd.at[:, part(t, owned)], o_gd.at[part(share, unit_width), :])
+    gproj_out.finish()
+
+    def out_block(k):
+        go[k * head_width : (k + 1) * head_width, :] = tn(
+            att[...], gproj[:, part(blocks[k], block)]
+        ).astype(low)
+
+    out_block(3)
+    z_o.send_far()
+    out_block(2)
+    out_block(1)
+    z_o.send_near()
+    out_block(0)
+    gatt, gqkv = gup, act
+
+    def gatt_tile(i):
+        at = part(i, 512)
+        made = nt(gproj[at, :], wo[...]).astype(low)
+        for h in range(heads):
+            used = 4.0 * fact(at, 2) + 4.0 > (first_head + h).astype(wide)
+            gatt[at, h * HD : (h + 1) * HD] = jnp.where(
+                used, made[:, h * HD : (h + 1) * HD].astype(wide), 0.0
+            ).astype(low)
+
+    tiles(2, gatt_tile)
+    z_o.send_two(stage)
+    r_rows_out[0].finish()
+    in_hid.wait()
+    sum_heads = FirstSum(0, units)
+
+    for h in range(heads):
+
+        def back_group(g, h=h):
+            at = part(g, 256)
+            lanes = [pl.ds(j * head_width + h * HD, HD) for j in range(3)]
+            query, keyed, value = (qkvb[at, lane] for lane in lanes)
+            grad = gatt[at, h * HD : (h + 1) * HD]
+            p = probs[part(g * heads + h, 256), :]
+            grad_p = nt(grad, value)
+            row_dot = jnp.sum(p * grad_p, axis=-1, keepdims=True)
+            grad_s = (p * (grad_p - row_dot)).astype(low)
+            cosine = cols[at, 0:HD]
+            sine = cols[at, HD : 2 * HD]
+            for lane, turned in (
+                (lanes[0], nn(grad_s, keyed) * scale),
+                (lanes[1], tn(grad_s, query) * scale),
+            ):
+                gqkv[at, lane] = (
+                    turned * cosine - pltpu.roll(turned, HD // 2, 1) * sine
+                ).astype(low)
+            gqkv[at, lanes[2]] = tn(p.astype(low), grad).astype(low)
+
+        tiles(SHARE, back_group)
+
+    def qkv_block(k):
+        r, c = k % 2 * block, k // 2 * 1024
+        for j in range(3):
+            gq[r : r + block, c + j * head_width : c + (j + 1) * head_width] = tn(
+                units[:, part(blocks[k], block)], gqkv[:, j * head_width : (j + 1) * head_width]
+            ).astype(low)
+
+    for one in g_d:
+        one.drain()
+    qkv_block(3)
+    z_q.send_far()
+    qkv_block(2)
+    qkv_block(1)
+    z_q.send_near()
+    qkv_block(0)
+    sum_heads.add()
+    first_out[1].forward()
+    z_q.send_two(stage)
+
+    in_wq.wait()
+    reduce.await_release()
+    partial_sums(
+        lambda at, n: nt(gqkv[at, 0 : 3 * head_width], wu[part(n, 512), 0 : 3 * head_width])
+    )
+    reduce.diagonal()
+    sum_heads.show()
+    first_out[1].finish()
+    reduce.sides()
+    shown.wait()
+    shown_far.wait()
+    done.append(shown_far)
+    first_out[0].forward()
+    reduce.arrive()
+
+    def input_tile(at, rows):
+        grad = reduce.total(at, 64) + r_gate[0, rows, 0:1] * slope[rows, :]
+        back, gain_terms = norm_back(own_tok[rows, :].astype(wide), grad, gains[0:1, :])
+        own_out[rows, :] = (mid_buf[rows, :] + back).astype(low)
+        gain_buf[0:1, :] = gain_buf[0:1, :] + jnp.sum(gain_terms, axis=0, keepdims=True)
+
+    row_tiles(input_tile)
+    outs.append(copies.local(own_out, o_input.at[mine]))
+    input_far = copies.push(own_out, o_input.at[mine], here.across)
+
+    for index in range(2):
+        for j in range(8):
+            pack[index * 8 + j : index * 8 + j + 1, :] = gain_buf[
+                index : index + 1, j * 256 : (j + 1) * 256
+            ]
+        made = exact(r_slope[index], r_inner[index], ((0,), (0,)))
+        pack[16 + index * 8 : 24 + index * 8, :] = made[0:8, :]
+        lane = lax.broadcasted_iota(jnp.int32, (owned, 256), 1)
+        own = pl.ds(0, owned)
+        hot = (lane.astype(wide) == fact(own, 2 + index)) & (fact(own, 4) > 0.5)
+        count = jnp.sum(jnp.where(hot, 1.0, 0.0), axis=0, keepdims=True)
+        pack[32 + index * 8 : 40 + index * 8, :] = jnp.broadcast_to(count, (8, 256))
+
+    def sum_slots(buf, count):
+        total = buf[0]
+        for k in range(1, count):
+            total = total + buf[k]
+        return total
+
+    got = [
+        copies.local(pack, pack_plane.at[share])
+        if d == 0
+        else to_peer(pack, pack_plane.at[share], here.members[d])
+        for d in range(SHARE)
+    ]
+    first_out[0].finish()
+    landed(got)
+    for copy in got[1:]:
+        copy.wait_send()
+        done.append(copy)
+    pack[...] = sum_slots(pack_plane, SHARE)
+    got = [
+        copies.local(pack, pack_side.at[side]),
+        to_peer(pack, pack_side.at[side], here.across),
+    ]
+    landed(got)
+    got[1].wait_send()
+    done.append(got[1])
+    pack[...] = pack_side[0] + pack_side[1]
+    got = [
+        copies.local(pack, pack_ring.at[here.place])
+        if k == 0
+        else to_peer(pack, pack_ring.at[here.place], planes[k])
+        for k in range(4)
+    ]
+
+    z_u.finish(stage)
+    deliver(lambda t: gu.at[part(t, owned), 0:unit_width], o_gu.at[:, part(share, unit_width)])
+    landed(got)
+    for copy in got[1:]:
+        copy.wait_send()
+        done.append(copy)
+    pack[...] = sum_slots(pack_ring, 4)
+    outs.append(copies.local(pack, o_pack))
+    z_o.finish(stage)
+    deliver(
+        lambda t: go.at[0:head_width, part(t, owned)], o_go.at[part(share, head_width), :]
+    )
+    z_q.finish(stage)
+    for j in range(3):
+        deliver(
+            lambda t, j=j: gq.at[part(t, owned), j * head_width : (j + 1) * head_width],
+            o_gq.at[j, :, part(share, head_width)],
+        )
+
+    drains = [g_q, g_o] + g_u + g_d + [z_d, z_u, z_o, z_q, reduce, units_out, gates_out]
+    for one in drains + [gproj_out] + r_rows_out + first_out:
+        one.drain()
+    input_far.wait()
+    for copy in owed:
+        copy.wait_recv()
+    for copy in outs:
+        copy.wait()
+    for copy in sent:
+        if not any(copy is one for one in done):
+            copy.wait_send()
+    copies.check()
+
+
+def plane(mesh):
+    fsdp = mesh.shape["fsdp"]
+    ring_size = fsdp // SHARE
+
+    def shards(
+        tokens,
+        head_bucket,
+        ffn_bucket,
+        lengths,
+        norm_gains,
+        qkv_weight,
+        out_weight,
+        up_weight,
+        down_weight,
+        router_first,
+        router_second,
+        cotangent,
+    ):
+        rows, width = tokens.shape
+        half = rows // 2
+        local_units = up_weight.shape[1]
+        units = local_units // SHARE
+        local_width = out_weight.shape[0]
+        head_width = local_width // SHARE
+        heads = head_width // HD
+        owned = width // fsdp
+        block = width // ring_size
+        plane_rows = SHARE * rows
+
+        slot_ids = jnp.arange(rows, dtype=jnp.int32)
+        segment, position, live_rows = (a[0] for a in layout(lengths, slot_ids))
+        frequency = theta_base ** (-2.0 * jnp.arange(HD // 2, dtype=wide) / HD)
+        angles = position.astype(wide)[:, None] * frequency
+        cosine, sine = jnp.cos(angles), jnp.sin(angles)
+        facts = jnp.stack(
+            [segment, slot_ids, head_bucket, ffn_bucket, live_rows.astype(jnp.int32)], axis=1
+        ).astype(wide)
+        col = jnp.concatenate(
+            [cosine, cosine, -sine, sine, jnp.pad(facts, ((0, 0), (0, HD - facts.shape[1])))],
+            axis=1,
+        )
+        row = jnp.pad(facts.T, ((0, 8 - facts.shape[1]), (0, 0)))
+        second = jnp.pad(router_second, ((0, 0), (0, 0), (0, HD - NB)))
+        b16, f32 = low, wide
+        hidden = router_first.shape[2]
+        small = 48
+
+        def shape(*dims):
+            return jax.ShapeDtypeStruct(dims[1:], dims[0])
+
+        def buffer(*dims):
+            return pltpu.VMEM(dims[1:], dims[0])
+
+        anywhere = pl.BlockSpec(memory_space=pl.ANY)
+        vmem = pl.BlockSpec(memory_space=pltpu.VMEM)
+        (
+            block_out,
+            input_grad,
+            raw_qkv,
+            raw_out,
+            raw_up,
+            raw_down,
+            raw_first,
+            sums,
+            *_,
+        ) = pl.pallas_call(
+            layer_kernel,
+            out_shape=[
+                shape(b16, rows, width),
+                shape(b16, rows, width),
+                shape(b16, 3, owned, local_width),
+                shape(b16, local_width, owned),
+                shape(b16, owned, local_units),
+                shape(b16, local_units, owned),
+                shape(b16, *router_first.shape),
+                shape(f32, small, 256),
+                shape(b16, plane_rows, width),
+                shape(b16, width, 3 * head_width),
+                shape(b16, 4, block, 3 * head_width),
+                shape(b16, 4, head_width, block),
+                shape(b16, 4, block, units),
+                shape(b16, 4, units, block),
+            ],
+            in_specs=[anywhere] * 9 + [vmem] * 2,
+            out_specs=[anywhere] * 14,
+            scratch_shapes=[
+                buffer(b16, plane_rows, width),
+                buffer(b16, plane_rows, width),
+                buffer(b16, plane_rows, width),
+                buffer(b16, plane_rows, width),
+                buffer(b16, 2 * plane_rows, units),
+                buffer(b16, head_width, width),
+                buffer(b16, width, units),
+                buffer(b16, units, width),
+                buffer(f32, plane_rows, 3 * HD),
+                buffer(f32, SHARE, 8, rows),
+                buffer(b16, plane_rows, 3 * head_width),
+                buffer(f32, SHARE * heads * rows, rows),
+                buffer(b16, plane_rows, head_width),
+                buffer(f32, plane_rows // 2, width),
+                buffer(b16, plane_rows // 2, width),
+                buffer(b16, plane_rows // 2, width),
+                buffer(b16, 3 * half, width),
+                buffer(b16, 3 * half, width),
+                buffer(f32, half, width),
+                buffer(f32, half, width),
+                buffer(b16, 4 * head_width, block),
+                buffer(b16, 2, block, units),
+                buffer(b16, half, width),
+                buffer(b16, half, width),
+                buffer(b16, half, width),
+                buffer(f32, width, hidden),
+                buffer(f32, half, width),
+                buffer(f32, plane_rows, HD),
+                buffer(f32, 2, half, HD),
+                buffer(f32, 2, half, hidden),
+                buffer(f32, 2, half, HD),
+                buffer(f32, 2, half, hidden),
+                buffer(b16, 2, plane_rows, hidden),
+                buffer(b16, 2, 256, hidden),
+                buffer(b16, 2, 4, 64, hidden),
+                buffer(f32, 8, width),
+                buffer(f32, small, 256),
+                buffer(f32, SHARE, small, 256),
+                buffer(f32, 2, small, 256),
+                buffer(f32, 4, small, 256),
+                pltpu.SemaphoreType.DMA((128,)),
+                pltpu.SemaphoreType.DMA((256,)),
+                pltpu.SemaphoreType.DMA((256,)),
+                pltpu.SemaphoreType.REGULAR((3,)),
+            ],
+            compiler_params=pltpu.CompilerParams(
+                collective_id=0, has_side_effects=True, vmem_limit_bytes=63 * 2**20
+            ),
+        )(
+            tokens,
+            col,
+            row,
+            cotangent,
+            jnp.transpose(qkv_weight, (1, 0, 2)),
+            out_weight,
+            up_weight,
+            down_weight,
+            router_first,
+            norm_gains,
+            second,
+        )
+        grad_qkv = jnp.transpose(raw_qkv, (1, 0, 2)).astype(wide)
+        grad_out, grad_up, grad_down, grad_first = (
+            a.astype(wide) for a in (raw_out, raw_up, raw_down, raw_first)
+        )
+        grad_gains = sums[0:16].reshape(2, width)
+        grad_second = jnp.stack([sums[16 : 16 + NB].T, sums[24 : 24 + NB].T])
+        usage = jnp.stack([sums[32, :NB], sums[40, :NB]])
+        return (
+            block_out,
+            input_grad,
+            grad_gains,
+            grad_qkv,
+            grad_out,
+            grad_up,
+            grad_down,
+            grad_first,
+            grad_second,
+            usage,
+        )
+
+    return shards
+
+
+def solution(mesh):
+    shards = plane(mesh) if mesh.shape["fsdp"] == 4 * SHARE else general(mesh)
     in_specs = (
         P("fsdp", None),
         P("fsdp"),
@@ -521,4 +1775,6 @@
         P(),
         P(),
     )
-    return jax.shard_map(shards, mesh=mesh, in_specs=in_specs, out_specs=out_specs, check_vma=False)
+    return jax.shard_map(
+        shards, mesh=mesh, in_specs=in_specs, out_specs=out_specs, check_vma=False
+    )

time: 868 us -> 516 us (0.59); the launches traced: 858 us -> 516 us
  waiting for transfers between devices: 517 us -> 0 us
  Pallas kernels: 0 us -> 493 us
  matrix products: 99 us -> 0 us
  local copies, waits for them, and re-layouts: 88.1 us -> 8.6 us
  starting transfers between devices: 75.7 us -> 0 us
  other arithmetic: 74.3 us -> 13.6 us
    ppermute x133 -> x0, waiting for transfers between devices: 517 us -> none  [the longest x48 316 us: ring(): lax.ppermute(moved, 'fsdp', [(i, (i + SHARE) % fsdp) for i in range(fsdp)])]
    pallas_call x0 -> x1, Pallas kernels: none -> 493 us  [shards(): pl.pallas_call(layer_kernel, out_shape=[shape(b16, rows, width), shape(b1...]
    dot_general x61 -> x0, matrix products: 94.7 us -> none  [the longest x32 27 us: dot_rows(): lax.dot_general(left_in, right_in, (((0,), (0,)), ((), ())), preferred_el...]
    ppermute x133 -> x0, starting transfers between devices: 75.7 us -> none  [the longest x70 48.2 us: hop(): return lax.ppermute(moved, 'fsdp', [(i, i ^ bits) for i in range(fsdp)])]
    unnamed x255 -> x13, local copies, waits for them, and re-layouts: 22.1 us -> 2.79 us
    dynamic_update_slice x47 -> x0, local copies, waits for them, and re-layouts: 18.9 us -> none  [the longest x30 12.5 us: ring_gather(): out = lax.dynamic_update_slice(out, moving[s], at)]
    concatenate x21 -> x0, other arithmetic: 17.1 us -> none  [the longest x3 5.99 us: gather_halves(): return jnp.concatenate([plane, hop(plane, 1)], axis=0)]
    slice x28 -> x2, local copies, waits for them, and re-layouts: 14.1 us -> 1.49 us  [the longest x1 0.77 us: shards(): usage = jnp.stack([sums[32, :NB], sums[40, :NB]])]
  transfers between devices with their start and end apart: 133 -> 0, of which waited for: 78 -> 0; matrix products, arithmetic and copies ran while one was open for 25% -> 0% of each run, Pallas kernels for 0% -> 0%
where the time goes in v4:
time: 516 us
  Pallas kernels  493 us (96%)
  other arithmetic  13.6 us (3%)
  local copies, waits for them, and re-layouts  8.6 us (2%)
    pallas_call x1, Pallas kernels, shards(): pl.pallas_call(layer_kernel, out_shape=[shape(b16, rows, width), shape(b1...  493 us

profile of v4, /device:TPU:0, one launch (start us, length us, event | category | flops | bytes accessed | tf_op | source)
XLA Modules:
  0.0 515.6 jit_solution(2321675333510673448)
XLA Ops:
  0.7 0.8 fusion.5
  1.4 0.7 fusion.6
  2.1 0.1 fusion.7
  2.2 0.1 select_reduce_fusion
  2.3 0.7 stack.25
  3.0 0.6 pad.13.row
  3.6 0.8 copy.24
  4.5 0.7 pad.14.second
  5.2 0.3 fusion
  5.5 0.3 fusion.1
  5.8 0.3 fusion.4
  6.1 0.3 fusion.2
  6.4 0.9 copy.25.col
  7.3 492.6 %shard_map.195 = (bf16[256,2048]{1,0:T(8,128)(2,1)}, bf16[256,2048]{1,0:T(8,128)(2,1)}, bf16[3,128,1024]{2,1,0:T(8,128)(2,1)}, bf16[1024,128]{1,0:T(8,128)(2,1)}...) custom-call(bf16[256,2048]{1,0:T(8,128)(2,1)} %tok.1, ...), custom_call_target="tpu_custom_call" | custom-call | tf_op jit(solution)/shard_map/pallas_call | solution.py:1645
  500.0 0.0 copy-start.2
  500.0 0.8 fusion.8
  500.8 0.6 pad_maximum_fusion.1
  501.3 0.7 slice_bitcast_fusion.1
  502.0 0.7 slice.15
  502.8 0.6 reshape.342
  503.4 0.6 pad_maximum_fusion
  504.0 0.0 copy-start.1
  504.0 1.9 convert_element_type.49
  505.9 2.5 convert_bitcast_fusion
  508.3 0.0 copy-done.2
  508.3 0.0 copy-start
  508.3 1.5 convert_element_type.50
  509.8 0.0 copy-done.1
  509.8 1.5 convert_element_type.51
  511.3 0.0 copy-done
  511.3 0.0 copy-start.4
  511.3 0.0 copy-start.3
  511.3 2.3 convert_element_type.52
  513.6 0.0 copy-done.4
  513.6 1.0 copy.32
  514.6 0.0 copy-done.3
  514.6 1.0 copy.33
  (7 shorter events, 0.1 us)
Async XLA Ops:
  500.0 8.3 %copy-start.2 = (bf16[128,4096]{1,0:T(8,128)(2,1)S(1)}, bf16[128,4096]{1,0:T(8,128)(2,1)}, u32[]{:S(2)}) copy-start(bf16[128,4096]{1,0:T(8,128)(2,1)} %get-tuple-element.23) | copy-start | bytes 3145732
  504.0 5.9 %copy-start.1 = (bf16[4096,128]{1,0:T(8,128)(2,1)S(1)}, bf16[4096,128]{1,0:T(8,128)(2,1)}, u32[]{:S(2)}) copy-start(bf16[4096,128]{1,0:T(8,128)(2,1)} %get-tuple-element.24) | copy-start | bytes 3145732
  508.3 3.0 copy-start
  511.3 2.4 copy-start.4
  511.3 3.3 copy-start.3

commit v5 on v4

--- a/solution.py
+++ b/solution.py
@@ -579,49 +579,53 @@
 class ZGather:
     def __init__(self, here, copies, view):
         self.here, self.copies, self.view, self.drained = here, copies, view, False
+        self.slots = [copies.slot() for _ in range(3)]
+
+    def copy(self, place, peer, slot):
+        block = self.view(place)
+        return self.copies.remote(block, block, peer, self.slots[slot])
 
     def start(self):
-        here, copies, view = self.here, self.copies, self.view
-        own = view(here.place)
-        self.two = copies.push(own, own, here.two)
-        self.near = copies.push(own, own, here.near)
-        slot = copies.slot()
-        self.far = copies.remote(own, own, here.far, slot)
+        here = self.here
+        self.near = self.copy(here.place, here.near, 0)
+        self.near.start()
+        self.far = self.copy(here.place, here.far, 1)
+        self.on_far = self.copy(here.near_place, here.far, 2)
+        self.on_near = self.copy(here.far_place, here.near, 1)
+        self.last = self.copy(here.two_place, here.near, 2)
         pl.when(here.inner)(self.far.start)
-        passing = view(here.two_place)
-        self.passed = copies.remote(passing, passing, here.near, slot)
-        arriving = view(here.two_place), view(here.near_place), view(here.far_place)
-        self.arrivals = [
-            pltpu.make_async_remote_copy(
-                src_ref=dst,
-                dst_ref=dst,
-                send_sem=copies.send_sems.at[0],
-                recv_sem=copies.recv_sems.at[at],
-                device_id=here.two,
-                device_id_type=MESH,
-            )
-            for dst, at in zip(arriving, (slot - 2, slot - 1, slot))
-        ]
-
-    def forward(self):
-        self.arrivals[0].wait_recv()
-        pl.when(self.here.inner)(self.passed.start)
+
+    def first(self):
+        @pl.when(self.here.inner)
+        def _():
+            self.near.wait_recv()
+            self.on_far.start()
+            self.far.wait_recv()
+            self.on_near.start()
+
+    def second(self):
+        @pl.when(self.here.inner)
+        def _():
+            self.on_far.wait_recv()
+            self.last.start()
 
     def arrive(self):
-        self.arrivals[1].wait_recv()
-        self.arrivals[2].wait_recv()
+        @pl.when(self.here.outer)
+        def _():
+            self.near.wait_recv()
+            self.on_near.wait_recv()
+            self.last.wait_recv()
 
     def drain(self):
         if self.drained:
             return
         self.drained = True
-        self.two.wait_send()
         self.near.wait_send()
 
         @pl.when(self.here.inner)
         def _():
-            self.far.wait_send()
-            self.passed.wait_send()
+            for copy in (self.far, self.on_far, self.on_near, self.last):
+                copy.wait_send()
 
 
 def tiles(count, body):
@@ -642,43 +646,52 @@
         (self.snd, self.rcv, self.acc, self.out, self.into) = bufs
         self.sent = []
 
-    def begin(self):
+    def begin(self, width):
+        self.lanes = pl.ds(0, width)
         for copy in self.sent:
             copy.wait_send()
         self.sent, self.core = [], []
 
     def core_send(self, index):
         rows = pl.ds(index * 256, 256)
-        self.core.append(self.copies.push(self.snd.at[rows], self.rcv.at[rows], self.here.core))
+        self.core.append(self.copies.push(
+                self.snd.at[rows, self.lanes], self.rcv.at[rows, self.lanes], self.here.core
+            ))
 
     def add_core(self, first, count):
-        acc, rcv = self.acc, self.rcv
+        acc, rcv, lanes = self.acc, self.rcv, self.lanes
 
         def body(i):
             at = pl.ds(pl.multiple_of(first + i * 64, 64), 64)
-            acc[at, :] = acc[at, :] + rcv[at, :].astype(wide)
+            acc[at, lanes] = acc[at, lanes] + rcv[at, lanes].astype(wide)
 
         tiles(count // 64, body)
 
     def round_out(self, first, count, extra=None):
-        acc, out, into = self.acc, self.out, self.into
+        acc, out, into, lanes = self.acc, self.out, self.into, self.lanes
 
         def body(i):
             at = pl.ds(pl.multiple_of(first + i * 64, 64), 64)
-            value = acc[at, :]
+            value = acc[at, lanes]
             if extra is not None:
-                value = value + into[pl.ds(extra, 64), :].astype(wide)
-            out[pl.ds(pl.multiple_of(first - 128 + i * 64, 64), 64), :] = value.astype(low)
+                value = value + into[pl.ds(extra, 64), lanes].astype(wide)
+            out[pl.ds(pl.multiple_of(first - 128 + i * 64, 64), 64), lanes] = value.astype(low)
 
         tiles(count // 64, body)
+
+    def hand(self, first, end, peer):
+        rows = pl.ds(first, end - first)
+        return self.copies.push(
+            self.out.at[rows, self.lanes], self.into.at[rows, self.lanes], peer
+        )
 
     def diagonal(self):
         for copy in self.core:
             copy.wait_recv()
         self.add_core(384, 128)
         self.round_out(384, 128)
-        self.diag_x = self.copies.push(self.out.at[256:320], self.into.at[256:320], self.here.across)
-        self.diag_y = self.copies.push(self.out.at[320:384], self.into.at[320:384], self.here.mid)
+        self.diag_x = self.hand(256, 320, self.here.across)
+        self.diag_y = self.hand(320, 384, self.here.mid)
         self.add_core(128, 256)
         self.round_out(128, 64)
         self.round_out(320, 64)
@@ -687,10 +700,10 @@
     def sides(self):
         self.diag_y.wait_recv()
         self.round_out(192, 64, 320)
-        self.over_x = self.copies.push(self.out.at[0:128], self.into.at[0:128], self.here.across)
+        self.over_x = self.hand(0, 128, self.here.across)
         self.diag_x.wait_recv()
         self.round_out(256, 64, 256)
-        self.over_y = self.copies.push(self.out.at[128:256], self.into.at[128:256], self.here.mid)
+        self.over_y = self.hand(128, 256, self.here.mid)
         self.sent = self.core + [self.diag_x, self.diag_y, self.over_x, self.over_y]
 
     def arrive(self):
@@ -698,11 +711,11 @@
         self.over_y.wait_recv()
 
     def total(self, at, size):
-        acc, into = self.acc, self.into
+        acc, into, lanes = self.acc, self.into, self.lanes
         return (
-            acc[pl.ds(at, size), :]
-            + into[pl.ds(at, size), :].astype(wide)
-            + into[pl.ds(at + 128, size), :].astype(wide)
+            acc[pl.ds(at, size), lanes]
+            + into[pl.ds(at, size), lanes].astype(wide)
+            + into[pl.ds(at + 128, size), lanes].astype(wide)
         )
 
     def release(self):
@@ -783,24 +796,17 @@
     def __init__(self, here, copies, base, spot, rows, columns, landing):
         self.here, self.copies, self.base, self.spot = here, copies, base, spot
         self.rows, self.columns, self.landing = rows, columns, landing
-        self.slot_y1, self.slot_y2 = copies.slot(), copies.slot()
-
-    def view(self, k, rows=None, columns=None):
+        self.slots = [copies.slot() for _ in range(5)]
+
+    def copy(self, k, peer, slot):
         r, c = self.spot(k)
-        return self.base.at[
-            pl.ds(r, self.rows) if rows is None else rows(r),
-            pl.ds(c, self.columns) if columns is None else columns(c),
-        ]
-
-    def send_far(self):
-        here, copies = self.here, self.copies
-        self.y1 = copies.remote(self.view(3), self.landing.at[2], here.far, self.slot_y1)
-        self.y2 = copies.remote(self.view(3), self.landing.at[3], here.near, self.slot_y2)
-        pl.when(here.inner)(self.y1.start)
-        pl.when(here.outer)(self.y2.start)
-
-    def send_near(self):
-        self.near = self.copies.push(self.view(1), self.landing.at[0], self.here.near)
+        block = self.base.at[pl.ds(r, self.rows), pl.ds(c, self.columns)]
+        return self.copies.remote(block, self.landing.at[slot], peer, self.slots[slot])
+
+    def outward(self, k):
+        copy = self.copy(k, self.here.near, {3: 1, 2: 2, 1: 0}[k])
+        setattr(self, f"out{k}", copy)
+        pl.when(self.here.outer)(copy.start)
 
     def load(self, index, stage, slot):
         size = min(self.rows, 512)
@@ -830,40 +836,57 @@
 
             tiles(size // 64, body)
 
-    def send_two(self, stage):
-        here, copies = self.here, self.copies
+    def pass_on(self, k, wait, index, stage, copy):
+        wait.wait_recv()
+        for load in self.load(index, stage, 0):
+            load.wait()
+        self.add(k, stage, [0])
+        copy.start()
+
+    def inward(self, step, stage):
+        here = self.here
+        if step == 0:
+            self.in2 = self.copy(2, here.far, 4)
+            args = (2, self.out3, 1, stage, self.in2)
+        elif step == 1:
+            self.in3 = self.copy(3, here.far, 3)
+            args = (3, self.out2, 2, stage, self.in3)
+        else:
+            self.in1 = self.copy(1, here.near, 0)
+            args = (1, self.in2, 4, stage, self.in1)
 
         @pl.when(here.inner)
         def _():
-            self.y2.wait_recv()
-            for copy in self.load(3, stage, 0):
-                copy.wait()
-            self.add(2, stage, [0])
-
-        self.two = copies.push(self.view(2), self.landing.at[1], here.two)
+            self.pass_on(*args)
 
     def finish(self, stage):
         here = self.here
-        self.near.wait_recv()
-        self.two.wait_recv()
-        loads = self.load(0, stage, 0) + self.load(1, stage, 1)
-        for copy in loads:
-            copy.wait()
-        self.add(0, stage, [0, 1])
+        self.out1.wait_recv()
+        loads = self.load(0, stage, 0)
 
         @pl.when(here.inner)
         def _():
-            self.y1.wait_recv()
-            for copy in self.load(2, stage, 0):
-                copy.wait()
+            self.in3.wait_recv()
+            for load in self.load(3, stage, 1) + loads:
+                load.wait()
+            self.add(0, stage, [0, 1])
+
+        @pl.when(here.outer)
+        def _():
+            for load in loads:
+                load.wait()
             self.add(0, stage, [0])
 
     def drain(self):
-        here = self.here
-        self.near.wait_send()
-        self.two.wait_send()
-        pl.when(here.inner)(self.y1.wait_send)
-        pl.when(here.outer)(self.y2.wait_send)
+        @pl.when(self.here.inner)
+        def _():
+            for copy in (self.in1, self.in2, self.in3):
+                copy.wait_send()
+
+        @pl.when(self.here.outer)
+        def _():
+            for copy in (self.out1, self.out2, self.out3):
+                copy.wait_send()
 
 
 def norm_back(value, grad, gain):
@@ -884,7 +907,7 @@
     o_block, o_input, o_gq, o_go, o_gu, o_gd, o_first, o_pack, s_hid, s_wq, l_q, l_o, l_u, l_d,
     toks, hid, units, cot, early, wo, wu, wd, cols, rows_info, qkvb, probs, att, acc,
     snd, rcv, out_buf, in_buf, proj, mid_buf, go, stage, top, own_tok, own_out,
-    first_buf, slope, gates, r_gate, r_inner, r_slope, r_dpre, r_rows, zpart, zland, gain_buf,
+    first_buf, slope, gates, dall, r_gate, r_inner, r_slope, r_dpre, r_rows, zpart, zland, gain_buf,
     pack, pack_plane, pack_side, pack_ring,
     local_sems, send_sems, recv_sems, acks,
 ):
@@ -893,6 +916,7 @@
     here.greet()
     rank, share, side = here.rank, here.share, here.side
     owned = 128
+    width = toks.shape[1]
     block = owned * SHARE
     head_width = wo.shape[0]
     unit_width = wu.shape[1]
@@ -922,12 +946,13 @@
             else:
                 copy.wait()
 
-    got_q = []
-    for j in range(3):
-        got_q += spread(
-            lambda t: qkvw.at[j, :, part(t, head_width)],
+    got_q = [
+        spread(
+            lambda t, j=j: qkvw.at[j, :, part(t, head_width)],
             wq.at[own_rows, j * head_width : (j + 1) * head_width],
         )
+        for j in range(3)
+    ]
     mine, other = part(side, owned), part(1 - side, owned)
 
     class Halves:
@@ -958,7 +983,10 @@
     in_first = copies.local(first.at[0], first_buf)
     in_tok = copies.local(tok.at[mine, :], own_tok)
 
-    g_q = ZGather(here, copies, lambda k: wq.at[part(k, block), :])
+    g_q = [
+        ZGather(here, copies, lambda k, d=d: wq.at[part(k * SHARE + here.shares[d], owned), :])
+        for d in range(SHARE)
+    ]
     g_o = ZGather(here, copies, lambda k: wo.at[:, part(k, block)])
     g_u = [
         ZGather(
@@ -976,10 +1004,16 @@
     def fact(at, index):
         return cols[at, 2 * HD + index : 2 * HD + index + 1]
 
-    landed(got_q)
-    g_q.start()
-    landed(got_o)
-    g_o.start()
+    def start_q(d):
+        for got in got_q:
+            if d:
+                got[d].wait_recv()
+            else:
+                got[d].wait()
+        g_q[d].start()
+
+    start_q(0)
+    start_q(1)
 
     def normalise(base):
         def body(i):
@@ -994,19 +1028,8 @@
         for wait in waits:
             wait()
 
-    wait_all([c.wait for c in tok_in.own])
+    wait_all([c.wait for c in tok_in.own + col_in.own + row_in.own])
     normalise(0)
-    wait_all([c.wait_recv for c in tok_in.core])
-    normalise(512)
-    tok_in.pass_on()
-    normalise(256)
-    wait_all([c.wait_recv for c in tok_in.last])
-    normalise(768)
-    wait_all([c.wait for c in col_in.own + row_in.own])
-    col_in.pass_on()
-    row_in.pass_on()
-    wait_all([c.wait_recv for c in col_in.core + row_in.core + col_in.last + row_in.last])
-    save_hid = copies.local(hid, s_hid)
 
     def route(index, rows_of):
         made = exact(rows_of[0:owned, :].astype(wide), first_buf[...], ((1,), (0,)))
@@ -1021,13 +1044,14 @@
         shares = raised / jnp.sum(raised, axis=-1, keepdims=True)
         hot = jnp.where(lane.astype(wide) == fact(pl.ds(0, owned), 2 + index), 1.0, 0.0)
         gate = NB * jnp.sum(shares * hot, axis=-1, keepdims=True)
-        lean = gate * (hot - shares)
+        lean = hot - shares
+        bare = exact(lean, second[index], ((1,), (1,))) * (sig * (1.0 + made * (1.0 - sig)))
         r_gate[index] = jnp.broadcast_to(gate, (owned, HD))
         r_inner[index] = inner
-        r_slope[index] = lean
-        r_dpre[index] = exact(lean, second[index], ((1,), (1,))) * (
-            sig * (1.0 + made * (1.0 - sig))
-        )
+        r_slope[index] = lean if index else gate * lean
+        r_dpre[index] = bare if index else gate * bare
+        if index == 1:
+            dall[0:owned, :] = bare.astype(low)
 
     def slope_tiles(index):
         def body(i):
@@ -1039,11 +1063,34 @@
     in_first.wait()
     route(0, hid)
     in_first = copies.local(first.at[1], first_buf)
-
-    g_q.forward()
+    start_q(2)
+    start_q(3)
+    g_q[0].first()
+    g_q[1].first()
+    wait_all([c.wait_recv for c in tok_in.core])
+    normalise(512)
+    g_q[0].second()
+    g_q[1].second()
+    g_q[2].first()
+    g_q[3].first()
+    tok_in.pass_on()
+    normalise(256)
+    g_q[2].second()
+    g_q[3].second()
+    wait_all([c.wait_recv for c in tok_in.last])
+    normalise(768)
+    save_hid = copies.local(hid, s_hid)
+    landed(got_o)
+    g_o.start()
+    col_in.pass_on()
+    row_in.pass_on()
+    wait_all([c.wait_recv for c in col_in.core + row_in.core + col_in.last + row_in.last])
+    g_o.first()
     landed(got_u)
+    g_o.second()
     g_u[0].start()
-    g_q.arrive()
+    for one in g_q:
+        one.arrive()
     save_wq = copies.local(wq, s_wq)
 
     for j in range(3):
@@ -1065,7 +1112,7 @@
 
         tiles(2, qkv_tile)
 
-    g_o.forward()
+    g_u[0].first()
     g_u[1].start()
 
     first_head = (side * SHARE + share) * heads
@@ -1097,8 +1144,9 @@
 
     reduce = RowReduce(here, copies, (snd, rcv, acc, out_buf, in_buf), acks)
 
-    def partial_sums(term):
-        reduce.begin()
+    def partial_sums(term, extra=None):
+        lanes = acc.shape[1] if extra is not None else width
+        reduce.begin(lanes)
         for i in range(2):
 
             def send_tile(n, i=i):
@@ -1107,20 +1155,29 @@
                 ).astype(low)
 
             tiles(4, send_tile)
+            if extra is not None:
+                snd[i * 256 : (i + 1) * 256, width:lanes] = extra[
+                    pl.ds(512 + i * 256, 256), :
+                ].astype(low)
             reduce.core_send(i)
 
         def own_tile(n):
             acc[:, part(n, 512)] = term(pl.ds(0, 512), n)
 
         tiles(4, own_tile)
+        if extra is not None:
+            acc[:, width:lanes] = extra[0:512, :]
 
     g_o.arrive()
     partial_sums(lambda at, n: nn(att[at, :], wo[:, part(n, 512)]))
+    g_u[0].second()
     reduce.diagonal()
+    g_u[1].first()
     reduce.sides()
-    g_u[0].forward()
+    g_u[1].second()
     landed(got_d)
     g_d[0].start()
+    g_d[1].start()
     in_tok.wait()
     reduce.arrive()
 
@@ -1156,15 +1213,28 @@
     route(1, units)
     gates[0:owned, :] = r_gate[1]
     gates_out = RowGather(here, copies, row_view(gates))
+    dall_out = RowGather(here, copies, row_view(dall))
     gates_out.start()
+    dall_out.start()
+
+    def first_low(n):
+        return go[pl.ds(pl.multiple_of(n % 2 * 512, 512), 512), part(n // 2, 256)]
+
+    def first_tile(i):
+        go[part(i % 8, 128), part(i // 8, 256)] = first_buf[part(i, 128), :].astype(low)
+
+    tiles(16, first_tile)
+    in_first = copies.local(first.at[0], first_buf)
+    g_d[0].first()
     units_out.forward()
-    slope_tiles(1)
     gates_out.forward()
+    dall_out.forward()
+    g_d[1].first()
     units_out.finish()
     gates_out.finish()
-    in_first = copies.local(first.at[0], first_buf)
-    g_u[1].forward()
-    g_d[1].start()
+    dall_out.finish()
+    g_d[0].second()
+    g_d[1].second()
     for one in g_u:
         one.arrive()
 
@@ -1175,7 +1245,8 @@
         return lane.astype(wide) < (FF // NB) * (fact(at, 3) + 1.0)
 
     save_wq.wait()
-    g_q.drain()
+    for one in g_q:
+        one.drain()
 
     def up_tile(i):
         m, n = i % 2, i // 2
@@ -1208,7 +1279,6 @@
         cot[at, :] = (gates[at, 0:1] * live_cot(at)).astype(low)
 
     tiles(16, scale_tile)
-    g_d[0].forward()
 
     gd, gu, gq = toks, hid, wd
     blocks = [here.place, here.near_place, here.two_place, here.far_place]
@@ -1230,31 +1300,30 @@
 
         tiles(unit_width // 512, body)
 
-    down_block(3)
-    z_d.send_far()
-    down_block(2)
-    down_block(1)
-    z_d.send_near()
+    for k in (3, 2, 1):
+        down_block(k)
+        z_d.outward(k)
     down_block(0)
+    z_d.inward(0, stage)
+    z_d.inward(1, stage)
     for one in g_d:
-        if one is g_d[1]:
-            one.forward()
         one.arrive()
 
-    def gup_tile(i):
-        m, n = i % 2, i // 2
-        at, c = part(m, 512), part(n, 512)
-        made = nt(cot[at, :], wd[c, :])
-        used = used_units(at, first_unit + n * 512, 512, 512)
-        relu = jnp.maximum(acc[:, part(m * 2 + n, 512)], 0.0)
-        gup[at, c] = jnp.where(used, 2.0 * relu * made, 0.0).astype(low)
-
-    tiles(4, gup_tile)
-    z_d.send_two(stage)
-
-    reduce.await_release()
-    partial_sums(lambda at, n: nn(act[at, :], wd[:, part(n, 512)]))
-    reduce.diagonal()
+    def gup_tile(m):
+        at = part(m, 512)
+        dots = jnp.zeros((512, 1), wide)
+        for n in range(unit_width // 512):
+            c = slice(n * 512, (n + 1) * 512)
+            made = nt(cot[at, :], wd[c, :])
+            used = used_units(at, first_unit + n * 512, 512, 512)
+            relu = jnp.maximum(acc[:, part(m * 2 + n, 512)], 0.0)
+            gup[at, c] = jnp.where(used, 2.0 * relu * made, 0.0).astype(low)
+            dots = dots + jnp.sum(act[at, c].astype(wide) * made, axis=-1, keepdims=True)
+        gates[at, :] = jnp.broadcast_to(dots, (512, HD))
+        r_rows[at, 256:512] = (dots * dall[at, :].astype(wide)).astype(low)
+
+    gates_out.drain()
+    tiles(2, gup_tile)
 
     save_hid.wait()
 
@@ -1269,86 +1338,78 @@
         tiles(unit_width // 512, body)
 
     up_block(3)
-    z_u.send_far()
+    z_u.outward(3)
+
+    reduce.await_release()
+    partial_sums(
+        lambda at, n: nt(gup[at, :], wu[part(n, 512), :])
+        + nt(r_rows[at, 256:512], first_low(n)),
+        gates,
+    )
+    up_block(2)
+    z_u.outward(2)
+    reduce.diagonal()
+    up_block(1)
+    z_u.outward(1)
+    z_d.inward(2, stage)
     reduce.sides()
-    up_block(2)
-    up_block(1)
-    z_u.send_near()
     up_block(0)
-    reduce.arrive()
-
-    r_rows_out = [RowGather(here, copies, row_view(r_rows.at[i])) for i in range(2)]
-
-    def keep_gate(index, rows, grad_gate):
-        r_rows[index, rows, :] = (grad_gate * r_dpre[index, rows, :]).astype(low)
-        r_slope[index, rows, :] = grad_gate * r_slope[index, rows, :]
-        r_gate[index, rows, :] = jnp.broadcast_to(grad_gate, (64, HD))
-
-    def block_tile(at, rows):
-        downward = reduce.total(at, 64)
-        own_out[rows, :] = jnp.where(
-            fact(rows, 4) > 0.5, mid_buf[rows, :] + r_gate[1, rows, 0:1] * downward, 0.0
-        ).astype(low)
-        keep_gate(
-            1, rows, jnp.sum(top[rows, :].astype(wide) * downward, axis=-1, keepdims=True)
-        )
-
-    row_tiles(block_tile)
-    reduce.release()
-    r_rows_out[1].start()
-    shown = copies.local(own_out, o_block.at[mine])
-    shown_far = to_peer(own_out, o_block.at[mine], here.across)
-
-    reduce.await_release()
-    partial_sums(lambda at, n: nt(gup[at, :], wu[part(n, 512), :]))
+
+    column = share * 2 + side
+    ucol = dall
+    dall_out.drain()
+
+    def ucol_tile(i):
+        ucol[part(i, 256), :] = units[part(i, 256), part(column, 256)]
+
+    tiles(4, ucol_tile)
+    units_out.drain()
+    in_hid = copies.local(s_hid, units)
     for one in g_u:
         one.drain()
     in_wq = copies.local(s_wq, wu.at[:, 0 : 3 * head_width])
-    r_rows_out[1].forward()
-    reduce.diagonal()
-    r_rows_out[1].finish()
-
-    column = share * 2 + side
+
+    r_rows_out = RowGather(here, copies, row_view(r_rows))
+
+    def keep_gate(index, rows, weight):
+        c = slice(index * 256, (index + 1) * 256)
+        r_rows[rows, c] = (weight * r_dpre[index, rows, :]).astype(low)
+        r_slope[index, rows, :] = weight * r_slope[index, rows, :]
+
     places = [here.place, here.near_place, here.two_place, here.far_place]
     planes = [None, here.near, here.two, here.far]
 
-    def first_rows(index, k, h):
+    def first_rows(k, h):
         target = here.shares[k // 4 + k // 2 % 2 * 2] * 2 + (side if k % 2 == 0 else 1 - side)
         base = target * 256
         if h is None:
-            return o_first.at[index, pl.ds(pl.multiple_of(base, 256), 256), :]
-        return o_first.at[index, pl.ds(pl.multiple_of(base + h * 128, 128), 128), :]
-
-    first_out = [
-        RowGather(here, copies, lambda k, h, i=i: first_rows(i, k, h), True) for i in range(2)
-    ]
+            return o_first.at[:, pl.ds(pl.multiple_of(base, 256), 256), :]
+        return o_first.at[:, pl.ds(pl.multiple_of(base + h * 128, 128), 128), :]
+
+    first_out = RowGather(here, copies, first_rows, True)
 
     class FirstSum:
-        def __init__(self, index, rows_of):
-            self.index = index
-            made = tn(rows_of[:, part(column, 256)], r_rows[index])
-            zpart[index] = made.astype(low)
-            slot = here.place
+        def __init__(self):
+            zpart[0] = tn(units[:, part(column, 256)], r_rows[:, 0:256]).astype(low)
+            zpart[1] = tn(ucol[...], r_rows[:, 256:512]).astype(low)
             self.got = []
             for k in range(4):
-                src = zpart.at[index, part(places[k], 64), :]
-                dst = zland.at[index, slot]
+                src, dst = zpart.at[:, part(places[k], 64), :], zland.at[here.place]
                 self.got.append(
                     copies.local(src, dst) if k == 0 else to_peer(src, dst, planes[k])
                 )
 
         def add(self):
-            index = self.index
             landed(self.got)
             for copy in self.got[1:]:
                 copy.wait_send()
                 done.append(copy)
-            total = zland[index, 0].astype(wide)
+            total = zland[0].astype(wide)
             for k in range(1, 4):
-                total = total + zland[index, k].astype(wide)
-            zpart[index, 0:64, :] = total.astype(low)
+                total = total + zland[k].astype(wide)
+            zpart[:, 0:64, :] = total.astype(low)
             at = pl.ds(pl.multiple_of(column * 256 + here.place * 64, 64), 64)
-            src, dst = zpart.at[index, 0:64, :], o_first.at[index, at, :]
+            src, dst = zpart.at[:, 0:64, :], o_first.at[:, at, :]
             self.got = [
                 copies.local(src, dst) if k == 0 else to_peer(src, dst, planes[k])
                 for k in range(4)
@@ -1356,38 +1417,41 @@
 
         def show(self):
             landed(self.got)
-            first_out[self.index].start()
-
-    sum_units = FirstSum(1, units)
-    units_out.drain()
-    in_hid = copies.local(s_hid, units)
-    z_u.send_two(stage)
-    reduce.sides()
-    sum_units.add()
+            first_out.start()
+
     reduce.arrive()
     gproj = cot
     gain_buf[...] = jnp.zeros_like(gain_buf)
 
     def grad_tile(at, rows):
-        grad = reduce.total(at, 64) + r_gate[1, rows, 0:1] * slope[rows, :]
+        total = reduce.total(at, 64)
+        grad = total[:, 0:width]
+        keep_gate(1, rows, total[:, width : width + 1])
         back, gain_terms = norm_back(mid_buf[rows, :], grad, gains[1:2, :])
         grad_middle = top[rows, :].astype(wide) + back
-        mid_buf[rows, :] = grad_middle
         gproj[rows, :] = (r_gate[0, rows, 0:1] * grad_middle).astype(low)
-        keep_gate(0, rows, jnp.sum(grad_middle * proj[rows, :], axis=-1, keepdims=True))
+        grad_gate = jnp.sum(grad_middle * proj[rows, :], axis=-1, keepdims=True)
+        keep_gate(0, rows, grad_gate)
+        r_gate[0, rows, :] = jnp.broadcast_to(grad_gate, (64, HD))
+        proj[rows, :] = grad_middle
         gain_buf[1:2, :] = gain_buf[1:2, :] + jnp.sum(gain_terms, axis=0, keepdims=True)
 
     row_tiles(grad_tile)
     reduce.release()
     gproj_out = RowGather(here, copies, row_view(gproj))
     gproj_out.start()
-    r_rows_out[0].start()
+    r_rows_out.start()
     in_first.wait()
     slope_tiles(0)
     gproj_out.forward()
-    sum_units.show()
-    r_rows_out[0].forward()
-    z_d.finish(stage)
+    r_rows_out.forward()
+
+    reduce.await_release()
+    partial_sums(lambda at, n: nn(act[at, :], wd[:, part(n, 512)]))
+    gproj_out.finish()
+    r_rows_out.finish()
+    in_hid.wait()
+    sum_first = FirstSum()
 
     def deliver(piece_of, dst):
         for d in range(SHARE):
@@ -1399,19 +1463,15 @@
                 owed.append(sent[-1])
 
     owed = []
-    deliver(lambda t: gd.at[:, part(t, owned)], o_gd.at[part(share, unit_width), :])
-    gproj_out.finish()
 
     def out_block(k):
         go[k * head_width : (k + 1) * head_width, :] = tn(
             att[...], gproj[:, part(blocks[k], block)]
         ).astype(low)
 
-    out_block(3)
-    z_o.send_far()
-    out_block(2)
-    out_block(1)
-    z_o.send_near()
+    for k in (3, 2, 1):
+        out_block(k)
+        z_o.outward(k)
     out_block(0)
     gatt, gqkv = gup, act
 
@@ -1425,10 +1485,6 @@
             ).astype(low)
 
     tiles(2, gatt_tile)
-    z_o.send_two(stage)
-    r_rows_out[0].finish()
-    in_hid.wait()
-    sum_heads = FirstSum(0, units)
 
     for h in range(heads):
 
@@ -1463,35 +1519,52 @@
 
     for one in g_d:
         one.drain()
-    qkv_block(3)
-    z_q.send_far()
-    qkv_block(2)
-    qkv_block(1)
-    z_q.send_near()
+    for k in (3, 2, 1):
+        qkv_block(k)
+        z_q.outward(k)
     qkv_block(0)
-    sum_heads.add()
-    first_out[1].forward()
-    z_q.send_two(stage)
+
+    reduce.diagonal()
+    z_u.inward(0, stage)
+    reduce.sides()
+    z_u.inward(1, stage)
+    reduce.arrive()
+
+    def block_tile(at, rows):
+        own_out[rows, :] = jnp.where(
+            fact(rows, 4) > 0.5,
+            mid_buf[rows, :] + r_gate[1, rows, 0:1] * reduce.total(at, 64),
+            0.0,
+        ).astype(low)
+
+    row_tiles(block_tile)
+    reduce.release()
+    shown = copies.local(own_out, o_block.at[mine])
+    shown_far = to_peer(own_out, o_block.at[mine], here.across)
 
     in_wq.wait()
     reduce.await_release()
     partial_sums(
         lambda at, n: nt(gqkv[at, 0 : 3 * head_width], wu[part(n, 512), 0 : 3 * head_width])
     )
+    z_d.finish(stage)
+    deliver(lambda t: gd.at[:, part(t, owned)], o_gd.at[part(share, unit_width), :])
     reduce.diagonal()
-    sum_heads.show()
-    first_out[1].finish()
+    z_u.inward(2, stage)
+    z_o.inward(0, stage)
+    z_o.inward(1, stage)
     reduce.sides()
+    sum_first.add()
+    z_q.inward(0, stage)
     shown.wait()
     shown_far.wait()
     done.append(shown_far)
-    first_out[0].forward()
     reduce.arrive()
 
     def input_tile(at, rows):
         grad = reduce.total(at, 64) + r_gate[0, rows, 0:1] * slope[rows, :]
         back, gain_terms = norm_back(own_tok[rows, :].astype(wide), grad, gains[0:1, :])
-        own_out[rows, :] = (mid_buf[rows, :] + back).astype(low)
+        own_out[rows, :] = (proj[rows, :] + back).astype(low)
         gain_buf[0:1, :] = gain_buf[0:1, :] + jnp.sum(gain_terms, axis=0, keepdims=True)
 
     row_tiles(input_tile)
@@ -1523,7 +1596,7 @@
         else to_peer(pack, pack_plane.at[share], here.members[d])
         for d in range(SHARE)
     ]
-    first_out[0].finish()
+    z_q.inward(1, stage)
     landed(got)
     for copy in got[1:]:
         copy.wait_send()
@@ -1544,27 +1617,32 @@
         for k in range(4)
     ]
 
+    z_o.inward(2, stage)
+    sum_first.show()
     z_u.finish(stage)
     deliver(lambda t: gu.at[part(t, owned), 0:unit_width], o_gu.at[:, part(share, unit_width)])
+    z_q.inward(2, stage)
+    first_out.forward()
+    z_o.finish(stage)
+    deliver(
+        lambda t: go.at[0:head_width, part(t, owned)], o_go.at[part(share, head_width), :]
+    )
+    first_out.finish()
+    z_q.finish(stage)
+    for j in range(3):
+        deliver(
+            lambda t, j=j: gq.at[part(t, owned), j * head_width : (j + 1) * head_width],
+            o_gq.at[j, :, part(share, head_width)],
+        )
     landed(got)
     for copy in got[1:]:
         copy.wait_send()
         done.append(copy)
     pack[...] = sum_slots(pack_ring, 4)
     outs.append(copies.local(pack, o_pack))
-    z_o.finish(stage)
-    deliver(
-        lambda t: go.at[0:head_width, part(t, owned)], o_go.at[part(share, head_width), :]
-    )
-    z_q.finish(stage)
-    for j in range(3):
-        deliver(
-            lambda t, j=j: gq.at[part(t, owned), j * head_width : (j + 1) * head_width],
-            o_gq.at[j, :, part(share, head_width)],
-        )
-
-    drains = [g_q, g_o] + g_u + g_d + [z_d, z_u, z_o, z_q, reduce, units_out, gates_out]
-    for one in drains + [gproj_out] + r_rows_out + first_out:
+
+    drains = [g_o] + g_q + g_u + g_d + [z_d, z_u, z_o, z_q, reduce, units_out, gates_out, dall_out]
+    for one in drains + [gproj_out, r_rows_out, first_out]:
         one.drain()
     input_far.wait()
     for copy in owed:
@@ -1655,10 +1733,10 @@
                 shape(f32, small, 256),
                 shape(b16, plane_rows, width),
                 shape(b16, width, 3 * head_width),
-                shape(b16, 4, block, 3 * head_width),
-                shape(b16, 4, head_width, block),
-                shape(b16, 4, block, units),
-                shape(b16, 4, units, block),
+                shape(b16, 5, block, 3 * head_width),
+                shape(b16, 5, head_width, block),
+                shape(b16, 5, block, units),
+                shape(b16, 5, units, block),
             ],
             in_specs=[anywhere] * 9 + [vmem] * 2,
             out_specs=[anywhere] * 14,
@@ -1676,11 +1754,11 @@
                 buffer(b16, plane_rows, 3 * head_width),
                 buffer(f32, SHARE * heads * rows, rows),
                 buffer(b16, plane_rows, head_width),
-                buffer(f32, plane_rows // 2, width),
-                buffer(b16, plane_rows // 2, width),
-                buffer(b16, plane_rows // 2, width),
-                buffer(b16, 3 * half, width),
-                buffer(b16, 3 * half, width),
+                buffer(f32, plane_rows // 2, width + HD),
+                buffer(b16, plane_rows // 2, width + HD),
+                buffer(b16, plane_rows // 2, width + HD),
+                buffer(b16, 3 * half, width + HD),
+                buffer(b16, 3 * half, width + HD),
                 buffer(f32, half, width),
                 buffer(f32, half, width),
                 buffer(b16, 4 * head_width, block),
@@ -1691,13 +1769,14 @@
                 buffer(f32, width, hidden),
                 buffer(f32, half, width),
                 buffer(f32, plane_rows, HD),
+                buffer(b16, plane_rows, hidden),
                 buffer(f32, 2, half, HD),
                 buffer(f32, 2, half, hidden),
                 buffer(f32, 2, half, HD),
                 buffer(f32, 2, half, hidden),
-                buffer(b16, 2, plane_rows, hidden),
+                buffer(b16, plane_rows, 2 * hidden),
                 buffer(b16, 2, 256, hidden),
-                buffer(b16, 2, 4, 64, hidden),
+                buffer(b16, 4, 2, 64, hidden),
                 buffer(f32, 8, width),
                 buffer(f32, small, 256),
                 buffer(f32, SHARE, small, 256),

time: 516 us -> 435 us (0.84)
  Pallas kernels: 493 us -> 411 us
    pallas_call x1, Pallas kernels: 493 us -> 411 us  [shards(): pl.pallas_call(layer_kernel, out_shape=[shape(b16, rows, width), shape(b1...]
where the time goes in v5:
time: 435 us; the launch traced here: 434 us
  Pallas kernels  411 us (94%)
  other arithmetic  13.6 us (3%)
  local copies, waits for them, and re-layouts  8.61 us (2%)
    pallas_call x1, Pallas kernels, shards(): pl.pallas_call(layer_kernel, out_shape=[shape(b16, rows, width), shape(b1...  411 us

profile of v5, /device:TPU:0, one launch (start us, length us, event | category | flops | bytes accessed | tf_op | source)
XLA Modules:
  0.0 433.7 jit_solution(14950381382967306968)
XLA Ops:
  0.7 0.8 fusion.5
  1.4 0.7 fusion.6
  2.1 0.1 fusion.7
  2.2 0.1 select_reduce_fusion
  2.3 0.7 stack.25
  3.0 0.6 pad.13.row
  3.6 0.8 copy.24
  4.5 0.7 pad.14.second
  5.2 0.3 fusion
  5.5 0.3 fusion.1
  5.8 0.3 fusion.4
  6.1 0.3 fusion.2
  6.4 0.9 copy.25.col
  7.3 410.7 %shard_map.195 = (bf16[256,2048]{1,0:T(8,128)(2,1)}, bf16[256,2048]{1,0:T(8,128)(2,1)}, bf16[3,128,1024]{2,1,0:T(8,128)(2,1)}, bf16[1024,128]{1,0:T(8,128)(2,1)}...) custom-call(bf16[256,2048]{1,0:T(8,128)(2,1)} %tok.1, ...), custom_call_target="tpu_custom_call" | custom-call | tf_op jit(solution)/shard_map/pallas_call | solution.py:1723
  418.1 0.0 copy-start.2
  418.1 0.8 fusion.8
  418.9 0.6 pad_maximum_fusion.1
  419.4 0.7 slice_bitcast_fusion.1
  420.1 0.7 slice.15
  420.9 0.6 reshape.342
  421.5 0.6 pad_maximum_fusion
  422.1 0.0 copy-start.1
  422.1 1.9 convert_element_type.49
  424.0 2.5 convert_bitcast_fusion
  426.4 0.0 copy-done.2
  426.4 0.0 copy-start
  426.4 1.5 convert_element_type.50
  427.9 0.0 copy-done.1
  427.9 1.5 convert_element_type.51
  429.4 0.0 copy-done
  429.4 0.0 copy-start.4
  429.4 0.0 copy-start.3
  429.4 2.3 convert_element_type.52
  431.7 0.0 copy-done.4
  431.8 1.0 copy.32
  432.7 0.0 copy-done.3
  432.7 1.0 copy.33
  (7 shorter events, 0.1 us)
Async XLA Ops:
  418.1 8.3 %copy-start.2 = (bf16[128,4096]{1,0:T(8,128)(2,1)S(1)}, bf16[128,4096]{1,0:T(8,128)(2,1)}, u32[]{:S(2)}) copy-start(bf16[128,4096]{1,0:T(8,128)(2,1)} %get-tuple-element.23) | copy-start | bytes 3145732
  422.1 5.9 %copy-start.1 = (bf16[4096,128]{1,0:T(8,128)(2,1)S(1)}, bf16[4096,128]{1,0:T(8,128)(2,1)}, u32[]{:S(2)}) copy-start(bf16[4096,128]{1,0:T(8,128)(2,1)} %get-tuple-element.24) | copy-start | bytes 3145732
  426.4 3.0 copy-start
  429.4 2.4 copy-start.4
  429.4 3.3 copy-start.3

commit v6 on v5

--- a/solution.py
+++ b/solution.py
@@ -797,15 +797,27 @@
         self.here, self.copies, self.base, self.spot = here, copies, base, spot
         self.rows, self.columns, self.landing = rows, columns, landing
         self.slots = [copies.slot() for _ in range(5)]
-
-    def copy(self, k, peer, slot):
+        self.handed = []
+
+    def copy(self, k, peer, slot, half=None):
         r, c = self.spot(k)
-        block = self.base.at[pl.ds(r, self.rows), pl.ds(c, self.columns)]
-        return self.copies.remote(block, self.landing.at[slot], peer, self.slots[slot])
+        first = self.rows // 2 if half == 1 else 0
+        rows = self.rows if half is None else self.rows // 2
+        block = self.base.at[pl.ds(r + first, rows), pl.ds(c, self.columns)]
+        dst = self.landing.at[slot, pl.ds(first, rows)]
+        return self.copies.remote(block, dst, peer, self.slots[slot])
 
     def outward(self, k):
         copy = self.copy(k, self.here.near, {3: 1, 2: 2, 1: 0}[k])
         setattr(self, f"out{k}", copy)
+        self.handed.append(copy)
+        pl.when(self.here.outer)(copy.start)
+
+    def outward_half(self, half):
+        if half == 0:
+            self.out1 = self.copy(1, self.here.near, 0)
+        copy = self.copy(1, self.here.near, 0, half)
+        self.handed.append(copy)
         pl.when(self.here.outer)(copy.start)
 
     def load(self, index, stage, slot):
@@ -885,7 +897,7 @@
 
         @pl.when(self.here.outer)
         def _():
-            for copy in (self.out1, self.out2, self.out3):
+            for copy in self.handed:
                 copy.wait_send()
 
 
@@ -1235,6 +1247,28 @@
     dall_out.finish()
     g_d[0].second()
     g_d[1].second()
+    wait_all([c.wait for c in cot_rows.own])
+    cot_rows.pass_on()
+    wait_all([c.wait_recv for c in cot_rows.core + cot_rows.last])
+
+    def live_cot(at):
+        return jnp.where(fact(at, 4) > 0.5, cot[at, :].astype(wide), 0.0)
+
+    for copy in tok_in.last + cot_rows.last:
+        copy.wait_send()
+        done.append(copy)
+
+    def keep_tile(at, rows):
+        top[rows, :] = live_cot(rows).astype(low)
+
+    row_tiles(keep_tile)
+
+    def scale_tile(i):
+        at = part(i, 64)
+        cot[at, :] = (gates[at, 0:1] * live_cot(at)).astype(low)
+
+    tiles(16, scale_tile)
+
     for one in g_u:
         one.arrive()
 
@@ -1258,27 +1292,16 @@
         act[at, c] = jnp.where(used, relu * relu, 0.0).astype(low)
 
     tiles(4, up_tile)
-    wait_all([c.wait for c in cot_rows.own])
-    cot_rows.pass_on()
-    wait_all([c.wait_recv for c in cot_rows.core + cot_rows.last])
-
-    def live_cot(at):
-        return jnp.where(fact(at, 4) > 0.5, cot[at, :].astype(wide), 0.0)
-
-    for copy in tok_in.last + cot_rows.last:
-        copy.wait_send()
-        done.append(copy)
-
-    def keep_tile(at, rows):
-        top[rows, :] = live_cot(rows).astype(low)
-
-    row_tiles(keep_tile)
-
-    def scale_tile(i):
-        at = part(i, 64)
-        cot[at, :] = (gates[at, 0:1] * live_cot(at)).astype(low)
-
-    tiles(16, scale_tile)
+    def deliver(piece_of, dst):
+        for d in range(SHARE):
+            src = piece_of(here.shares[d])
+            if d == 0:
+                outs.append(copies.local(src, dst))
+            else:
+                sent.append(copies.push(src, dst, here.members[d]))
+                owed.append(sent[-1])
+
+    owed = []
 
     gd, gu, gq = toks, hid, wd
     blocks = [here.place, here.near_place, here.two_place, here.far_place]
@@ -1350,7 +1373,7 @@
     z_u.outward(2)
     reduce.diagonal()
     up_block(1)
-    z_u.outward(1)
+    z_u.outward_half(0)
     z_d.inward(2, stage)
     reduce.sides()
     up_block(0)
@@ -1443,6 +1466,7 @@
     r_rows_out.start()
     in_first.wait()
     slope_tiles(0)
+    z_u.inward(0, stage)
     gproj_out.forward()
     r_rows_out.forward()
 
@@ -1452,27 +1476,18 @@
     r_rows_out.finish()
     in_hid.wait()
     sum_first = FirstSum()
-
-    def deliver(piece_of, dst):
-        for d in range(SHARE):
-            src = piece_of(here.shares[d])
-            if d == 0:
-                outs.append(copies.local(src, dst))
-            else:
-                sent.append(copies.push(src, dst, here.members[d]))
-                owed.append(sent[-1])
-
-    owed = []
+    z_u.outward_half(1)
+    z_d.finish(stage)
+    deliver(lambda t: gd.at[:, part(t, owned)], o_gd.at[part(share, unit_width), :])
+
 
     def out_block(k):
         go[k * head_width : (k + 1) * head_width, :] = tn(
             att[...], gproj[:, part(blocks[k], block)]
         ).astype(low)
 
-    for k in (3, 2, 1):
+    for k in range(4):
         out_block(k)
-        z_o.outward(k)
-    out_block(0)
     gatt, gqkv = gup, act
 
     def gatt_tile(i):
@@ -1519,15 +1534,20 @@
 
     for one in g_d:
         one.drain()
-    for k in (3, 2, 1):
+    z_u.inward(1, stage)
+    sum_first.add()
+    for k in (3, 2):
         qkv_block(k)
         z_q.outward(k)
+    for k in (3, 2, 1):
+        z_o.outward(k)
+    qkv_block(1)
+    z_q.outward(1)
     qkv_block(0)
 
     reduce.diagonal()
-    z_u.inward(0, stage)
     reduce.sides()
-    z_u.inward(1, stage)
+    z_u.inward(2, stage)
     reduce.arrive()
 
     def block_tile(at, rows):
@@ -1547,15 +1567,16 @@
     partial_sums(
         lambda at, n: nt(gqkv[at, 0 : 3 * head_width], wu[part(n, 512), 0 : 3 * head_width])
     )
-    z_d.finish(stage)
-    deliver(lambda t: gd.at[:, part(t, owned)], o_gd.at[part(share, unit_width), :])
     reduce.diagonal()
-    z_u.inward(2, stage)
+    z_u.finish(stage)
+    deliver(lambda t: gu.at[part(t, owned), 0:unit_width], o_gu.at[:, part(share, unit_width)])
+    z_q.inward(0, stage)
+    reduce.sides()
+    sum_first.show()
+    z_q.inward(1, stage)
+    z_q.inward(2, stage)
     z_o.inward(0, stage)
     z_o.inward(1, stage)
-    reduce.sides()
-    sum_first.add()
-    z_q.inward(0, stage)
     shown.wait()
     shown_far.wait()
     done.append(shown_far)
@@ -1568,8 +1589,7 @@
         gain_buf[0:1, :] = gain_buf[0:1, :] + jnp.sum(gain_terms, axis=0, keepdims=True)
 
     row_tiles(input_tile)
-    outs.append(copies.local(own_out, o_input.at[mine]))
-    input_far = copies.push(own_out, o_input.at[mine], here.across)
+    first_out.forward()
 
     for index in range(2):
         for j in range(8):
@@ -1596,7 +1616,6 @@
         else to_peer(pack, pack_plane.at[share], here.members[d])
         for d in range(SHARE)
     ]
-    z_q.inward(1, stage)
     landed(got)
     for copy in got[1:]:
         copy.wait_send()
@@ -1606,6 +1625,10 @@
         copies.local(pack, pack_side.at[side]),
         to_peer(pack, pack_side.at[side], here.across),
     ]
+    outs.append(copies.local(own_out, o_input.at[mine]))
+    input_far = copies.push(own_out, o_input.at[mine], here.across)
+    z_o.inward(2, stage)
+    first_out.finish()
     landed(got)
     got[1].wait_send()
     done.append(got[1])
@@ -1617,17 +1640,10 @@
         for k in range(4)
     ]
 
-    z_o.inward(2, stage)
-    sum_first.show()
-    z_u.finish(stage)
-    deliver(lambda t: gu.at[part(t, owned), 0:unit_width], o_gu.at[:, part(share, unit_width)])
-    z_q.inward(2, stage)
-    first_out.forward()
     z_o.finish(stage)
     deliver(
         lambda t: go.at[0:head_width, part(t, owned)], o_go.at[part(share, head_width), :]
     )
-    first_out.finish()
     z_q.finish(stage)
     for j in range(3):
         deliver(

time: 435 us -> 408 us (0.938)
  Pallas kernels: 411 us -> 384 us
    pallas_call x1, Pallas kernels: 411 us -> 384 us  [shards(): pl.pallas_call(layer_kernel, out_shape=[shape(b16, rows, width), shape(b1...]
where the time goes in v6:
time: 408 us; the launch traced here: 407 us
  Pallas kernels  384 us (94%)
  other arithmetic  13.6 us (3%)
  local copies, waits for them, and re-layouts  8.61 us (2%)
    pallas_call x1, Pallas kernels, shards(): pl.pallas_call(layer_kernel, out_shape=[shape(b16, rows, width), shape(b1...  384 us

profile of v6, /device:TPU:0, one launch (start us, length us, event | category | flops | bytes accessed | tf_op | source)
XLA Modules:
  0.0 407.0 jit_solution(11328820180020271050)
XLA Ops:
  0.7 0.8 fusion.5
  1.4 0.7 fusion.6
  2.1 0.1 fusion.7
  2.2 0.1 select_reduce_fusion
  2.3 0.7 stack.25
  3.0 0.6 pad.13.row
  3.6 0.8 copy.24
  4.5 0.7 pad.14.second
  5.2 0.3 fusion
  5.5 0.3 fusion.1
  5.8 0.3 fusion.4
  6.1 0.3 fusion.2
  6.4 0.9 copy.25.col
  7.3 384.1 %shard_map.195 = (bf16[256,2048]{1,0:T(8,128)(2,1)}, bf16[256,2048]{1,0:T(8,128)(2,1)}, bf16[3,128,1024]{2,1,0:T(8,128)(2,1)}, bf16[1024,128]{1,0:T(8,128)(2,1)}...) custom-call(bf16[256,2048]{1,0:T(8,128)(2,1)} %tok.1, ...), custom_call_target="tpu_custom_call" | custom-call | tf_op jit(solution)/shard_map/pallas_call | solution.py:1739
  391.4 0.0 copy-start.2
  391.4 0.8 fusion.8
  392.2 0.6 pad_maximum_fusion.1
  392.8 0.7 slice_bitcast_fusion.1
  393.5 0.7 slice.15
  394.2 0.6 reshape.342
  394.8 0.6 pad_maximum_fusion
  395.4 0.0 copy-start.1
  395.4 1.9 convert_element_type.49
  397.3 2.5 convert_bitcast_fusion
  399.8 0.0 copy-done.2
  399.8 0.0 copy-start
  399.8 1.5 convert_element_type.50
  401.3 0.0 copy-done.1
  401.3 1.5 convert_element_type.51
  402.7 0.0 copy-done
  402.8 0.0 copy-start.4
  402.8 0.0 copy-start.3
  402.8 2.3 convert_element_type.52
  405.1 0.0 copy-done.4
  405.1 1.0 copy.32
  406.1 0.0 copy-done.3
  406.1 1.0 copy.33
  (7 shorter events, 0.1 us)
Async XLA Ops:
  391.4 8.3 %copy-start.2 = (bf16[128,4096]{1,0:T(8,128)(2,1)S(1)}, bf16[128,4096]{1,0:T(8,128)(2,1)}, u32[]{:S(2)}) copy-start(bf16[128,4096]{1,0:T(8,128)(2,1)} %get-tuple-element.23) | copy-start | bytes 3145732
  395.4 5.9 %copy-start.1 = (bf16[4096,128]{1,0:T(8,128)(2,1)S(1)}, bf16[4096,128]{1,0:T(8,128)(2,1)}, u32[]{:S(2)}) copy-start(bf16[4096,128]{1,0:T(8,128)(2,1)} %get-tuple-element.24) | copy-start | bytes 3145732
  399.8 3.0 copy-start
  402.8 2.4 copy-start.4
  402.8 3.3 copy-start.3

commit v7 on v6

--- a/solution.py
+++ b/solution.py
@@ -2,6 +2,7 @@
 
 import jax
 import jax.numpy as jnp
+import numpy as np
 from jax import lax
 from jax.experimental import pallas as pl
 from jax.experimental.pallas import tpu as pltpu
@@ -820,6 +821,46 @@
         self.handed.append(copy)
         pl.when(self.here.outer)(copy.start)
 
+    def outward_piece(self, n, size):
+        r, c = self.spot(1)
+        if n == 0:
+            self.out1 = self.copy(1, self.here.near, 0)
+            self.pieces = []
+        lanes = pl.ds(n * size, size)
+        copy = self.copies.remote(
+            self.base.at[pl.ds(r, self.rows), pl.ds(c + n * size, size)],
+            self.landing.at[0, :, lanes],
+            self.here.near,
+        )
+        self.pieces.append(copy)
+        self.handed.append(copy)
+        pl.when(self.here.outer)(copy.start)
+
+    def finish_piece(self, n, size, stage):
+        here = self.here
+
+        @pl.when(here.inner)
+        def _():
+            lanes = pl.ds(n * size, size)
+            if n == 0:
+                self.in3.wait_recv()
+                for load in self.load(3, stage, 1):
+                    load.wait()
+            self.pieces[n].wait_recv()
+            self.copies.local(
+                self.landing.at[0, :, lanes], stage.at[0, pl.ds(0, self.rows), lanes]
+            ).wait()
+            self.add(0, stage, [0, 1], n * size, size)
+
+        if n == 0:
+
+            @pl.when(here.outer)
+            def _():
+                self.out1.wait_recv()
+                for load in self.load(0, stage, 0):
+                    load.wait()
+                self.add(0, stage, [0])
+
     def load(self, index, stage, slot):
         size = min(self.rows, 512)
         return [
@@ -830,19 +871,20 @@
             for n in range(self.rows // size)
         ]
 
-    def add(self, target, stage, slots):
+    def add(self, target, stage, slots, first=0, columns=None):
         size = min(self.rows, 512)
+        columns = self.columns if columns is None else columns
         r, c = self.spot(target)
         for n in range(self.rows // size):
 
             def body(i, n=n):
                 at = pl.ds(pl.multiple_of(i * 64, 64), 64)
                 mine = pl.ds(pl.multiple_of(r + n * size + i * 64, 64), 64)
-                lanes = pl.ds(c, self.columns)
+                lanes = pl.ds(c + first, columns)
                 value = self.base[mine, lanes].astype(wide)
                 for slot in slots:
                     value = value + stage[
-                        slot, at, pl.ds(n * self.columns, self.columns)
+                        slot, at, pl.ds(n * self.columns + first, columns)
                     ].astype(wide)
                 self.base[mine, lanes] = value.astype(low)
 
@@ -915,11 +957,12 @@
 
 
 def layer_kernel(
-    tok, col, row, cot_in, qkvw, outw, upw, downw, first, gains, second,
+    tok, cot_in, qkvw, outw, upw, downw, first, gains, second_in, heads_in, widths_in, turns,
+    lengths,
     o_block, o_input, o_gq, o_go, o_gu, o_gd, o_first, o_pack, s_hid, s_wq, l_q, l_o, l_u, l_d,
     toks, hid, units, cot, early, wo, wu, wd, cols, rows_info, qkvb, probs, att, acc,
     snd, rcv, out_buf, in_buf, proj, mid_buf, go, stage, top, own_tok, own_out,
-    first_buf, slope, gates, dall, r_gate, r_inner, r_slope, r_dpre, r_rows, zpart, zland, gain_buf,
+    first_buf, slope, gates, dall, second, col, row, square, r_gate, r_inner, r_slope, r_dpre, r_rows, zpart, zland, gain_buf,
     pack, pack_plane, pack_side, pack_ring,
     local_sems, send_sems, recv_sems, acks,
 ):
@@ -983,6 +1026,37 @@
             ]
 
     tok_in = Halves(lambda r: tok.at[r, :], lambda at: toks.at[at : at + owned])
+
+    row[...] = jnp.zeros_like(row)
+    for h in range(2):
+        slot = lax.broadcasted_iota(jnp.int32, (1, owned), 1) + h * owned
+        segment = slot * 0 + (lengths.shape[1] + slot)
+        position = slot
+        live = slot * 0
+        begin = 0
+        for n in range(lengths.shape[1]):
+            end = begin + lengths[0, n]
+            member = (slot >= begin) & (slot < end)
+            segment = jnp.where(member, n, segment)
+            position = jnp.where(member, slot - begin, position)
+            live = jnp.where(member, 1, live)
+            begin = end
+        lanes = slice(h * owned, (h + 1) * owned)
+        held = (segment, slot, heads_in[h : h + 1, :], widths_in[h : h + 1, :], live, position)
+        for n, value in enumerate(held):
+            row[n : n + 1, lanes] = value.astype(wide)
+        square[...] = jnp.zeros_like(square)
+        square[0:8, :] = row[:, lanes]
+        turned = jnp.transpose(square[...])
+        angles = turned[:, 5:6] * turns[0:1, :]
+        col[lanes, 0:HD] = jnp.cos(angles)
+        sines = jnp.sin(angles)
+        lane = lax.broadcasted_iota(jnp.int32, (owned, HD), 1)
+        col[lanes, HD : 2 * HD] = jnp.where(lane < HD // 2, -sines, sines)
+        col[lanes, 2 * HD : 3 * HD] = turned
+    second[...] = jnp.zeros_like(second)
+    for index in range(2):
+        second[index, 0:NB, :] = second_in[index]
     col_in = Halves(lambda r: col.at[r, :], lambda at: cols.at[at : at + owned])
     row_in = Halves(
         lambda r: row.at[:, r],
@@ -1047,7 +1121,7 @@
         made = exact(rows_of[0:owned, :].astype(wide), first_buf[...], ((1,), (0,)))
         sig = 1.0 / (1.0 + jnp.exp(-made))
         inner = made * sig
-        logits = exact(inner, second[index], ((1,), (0,)))
+        logits = exact(inner, second[index], ((1,), (1,)))
         lane = lax.broadcasted_iota(jnp.int32, (owned, HD), 1)
         logits = jnp.where(lane < NB, logits, -1e30)
         raised = jnp.where(
@@ -1057,7 +1131,7 @@
         hot = jnp.where(lane.astype(wide) == fact(pl.ds(0, owned), 2 + index), 1.0, 0.0)
         gate = NB * jnp.sum(shares * hot, axis=-1, keepdims=True)
         lean = hot - shares
-        bare = exact(lean, second[index], ((1,), (1,))) * (sig * (1.0 + made * (1.0 - sig)))
+        bare = exact(lean, second[index], ((1,), (0,))) * (sig * (1.0 + made * (1.0 - sig)))
         r_gate[index] = jnp.broadcast_to(gate, (owned, HD))
         r_inner[index] = inner
         r_slope[index] = lean if index else gate * lean
@@ -1536,13 +1610,16 @@
         one.drain()
     z_u.inward(1, stage)
     sum_first.add()
-    for k in (3, 2):
-        qkv_block(k)
-        z_q.outward(k)
-    for k in (3, 2, 1):
-        z_o.outward(k)
+    qkv_block(3)
+    z_q.outward(3)
+    z_o.outward(3)
+    qkv_block(2)
+    z_q.outward(2)
+    z_o.outward(2)
+    z_o.outward(1)
     qkv_block(1)
-    z_q.outward(1)
+    for j in range(3):
+        z_q.outward_piece(j, head_width)
     qkv_block(0)
 
     reduce.diagonal()
@@ -1571,12 +1648,13 @@
     z_u.finish(stage)
     deliver(lambda t: gu.at[part(t, owned), 0:unit_width], o_gu.at[:, part(share, unit_width)])
     z_q.inward(0, stage)
+    z_o.inward(0, stage)
     reduce.sides()
     sum_first.show()
     z_q.inward(1, stage)
     z_q.inward(2, stage)
-    z_o.inward(0, stage)
     z_o.inward(1, stage)
+    z_o.inward(2, stage)
     shown.wait()
     shown_far.wait()
     done.append(shown_far)
@@ -1627,7 +1705,6 @@
     ]
     outs.append(copies.local(own_out, o_input.at[mine]))
     input_far = copies.push(own_out, o_input.at[mine], here.across)
-    z_o.inward(2, stage)
     first_out.finish()
     landed(got)
     got[1].wait_send()
@@ -1644,8 +1721,8 @@
     deliver(
         lambda t: go.at[0:head_width, part(t, owned)], o_go.at[part(share, head_width), :]
     )
-    z_q.finish(stage)
     for j in range(3):
+        z_q.finish_piece(j, head_width, stage)
         deliver(
             lambda t, j=j: gq.at[part(t, owned), j * head_width : (j + 1) * head_width],
             o_gq.at[j, :, part(share, head_width)],
@@ -1669,6 +1746,57 @@
         if not any(copy is one for one in done):
             copy.wait_send()
     copies.check()
+
+
+def finish_kernel(
+    block, inp, gq, go, gu, gd, gf, sums,
+    o_block, o_inp, o_gains, o_gq, o_go, o_gu, o_gd, o_first, o_second, o_usage,
+    b_block, b_inp, b_q, b_o, b_u, b_d, b_f, w_q, w_o, w_u, w_d, w_f, in_sems, out_sems,
+):
+    narrow = [(gu, b_u), (gd, b_d), (gq, b_q), (gf, b_f), (go, b_o)]
+    narrow += [(block, b_block), (inp, b_inp)]
+    loads = [
+        pltpu.make_async_copy(src, dst, in_sems.at[i]) for i, (src, dst) in enumerate(narrow)
+    ]
+    for load in loads:
+        load.start()
+    stores = []
+
+    def store(src, dst):
+        copy = pltpu.make_async_copy(src, dst, out_sems.at[len(stores)])
+        copy.start()
+        stores.append(copy)
+
+    for index in range(2):
+        for j in range(8):
+            o_gains[index : index + 1, j * 256 : (j + 1) * 256] = sums[
+                index * 8 + j : index * 8 + j + 1, :
+            ]
+        o_second[index] = sums[16 + index * 8 : 16 + index * 8 + NB, :]
+        o_usage[index : index + 1, :] = sums[32 + index * 8 : 33 + index * 8, 0:NB]
+    wides = [(b_u, w_u, o_gu), (b_d, w_d, o_gd), (b_q, w_q, o_gq)]
+    wides += [(b_f, w_f, o_first), (b_o, w_o, o_go)]
+    for i, (src, dst, out) in enumerate(wides):
+        loads[i].wait()
+        lead = src.shape[0] if len(src.shape) == 3 else None
+        step = 128
+        rows = src.shape[-2]
+        for n in range(lead or 1):
+
+            def widen(k, src=src, dst=dst, n=n, lead=lead):
+                at = part(k, step)
+                if lead is None:
+                    dst[at, :] = src[at, :].astype(wide)
+                else:
+                    dst[n, at, :] = src[n, at, :].astype(wide)
+
+            tiles(rows // step, widen)
+        store(dst, out)
+    for i, (src, out) in enumerate(((b_block, o_block), (b_inp, o_inp))):
+        loads[5 + i].wait()
+        store(src, out)
+    for copy in stores:
+        copy.wait()
 
 
 def plane(mesh):
@@ -1700,20 +1828,8 @@
         block = width // ring_size
         plane_rows = SHARE * rows
 
-        slot_ids = jnp.arange(rows, dtype=jnp.int32)
-        segment, position, live_rows = (a[0] for a in layout(lengths, slot_ids))
-        frequency = theta_base ** (-2.0 * jnp.arange(HD // 2, dtype=wide) / HD)
-        angles = position.astype(wide)[:, None] * frequency
-        cosine, sine = jnp.cos(angles), jnp.sin(angles)
-        facts = jnp.stack(
-            [segment, slot_ids, head_bucket, ffn_bucket, live_rows.astype(jnp.int32)], axis=1
-        ).astype(wide)
-        col = jnp.concatenate(
-            [cosine, cosine, -sine, sine, jnp.pad(facts, ((0, 0), (0, HD - facts.shape[1])))],
-            axis=1,
-        )
-        row = jnp.pad(facts.T, ((0, 8 - facts.shape[1]), (0, 0)))
-        second = jnp.pad(router_second, ((0, 0), (0, 0), (0, HD - NB)))
+        turns = np.float32(theta_base) ** np.float32(-2.0 * np.arange(HD // 2) / HD)
+        turns = np.tile(np.concatenate([turns, turns])[None, :], (8, 1)).astype(np.float32)
         b16, f32 = low, wide
         hidden = router_first.shape[2]
         small = 48
@@ -1754,7 +1870,7 @@
                 shape(b16, 5, block, units),
                 shape(b16, 5, units, block),
             ],
-            in_specs=[anywhere] * 9 + [vmem] * 2,
+            in_specs=[anywhere] * 7 + [vmem] * 5 + [pl.BlockSpec(memory_space=pltpu.SMEM)],
             out_specs=[anywhere] * 14,
             scratch_shapes=[
                 buffer(b16, plane_rows, width),
@@ -1786,6 +1902,10 @@
                 buffer(f32, half, width),
                 buffer(f32, plane_rows, HD),
                 buffer(b16, plane_rows, hidden),
+                buffer(f32, 2, HD, hidden),
+                buffer(f32, rows, 3 * HD),
+                buffer(f32, 8, rows),
+                buffer(f32, HD, HD),
                 buffer(f32, 2, half, HD),
                 buffer(f32, 2, half, hidden),
                 buffer(f32, 2, half, HD),
@@ -1804,12 +1924,10 @@
                 pltpu.SemaphoreType.REGULAR((3,)),
             ],
             compiler_params=pltpu.CompilerParams(
-                collective_id=0, has_side_effects=True, vmem_limit_bytes=63 * 2**20
+                collective_id=0, has_side_effects=True, vmem_limit_bytes=127 * 2**19
             ),
         )(
             tokens,
-            col,
-            row,
             cotangent,
             jnp.transpose(qkv_weight, (1, 0, 2)),
             out_weight,
@@ -1817,15 +1935,45 @@
             down_weight,
             router_first,
             norm_gains,
-            second,
-        )
-        grad_qkv = jnp.transpose(raw_qkv, (1, 0, 2)).astype(wide)
-        grad_out, grad_up, grad_down, grad_first = (
-            a.astype(wide) for a in (raw_out, raw_up, raw_down, raw_first)
-        )
-        grad_gains = sums[0:16].reshape(2, width)
-        grad_second = jnp.stack([sums[16 : 16 + NB].T, sums[24 : 24 + NB].T])
-        usage = jnp.stack([sums[32, :NB], sums[40, :NB]])
+            jnp.transpose(router_second, (0, 2, 1)),
+            head_bucket.reshape(2, half),
+            ffn_bucket.reshape(2, half),
+            jnp.asarray(turns),
+            lengths,
+        )
+        wides = [
+            (3, owned, local_width),
+            (local_width, owned),
+            (owned, local_units),
+            (local_units, owned),
+            router_first.shape,
+        ]
+        (
+            block_out,
+            input_grad,
+            grad_gains,
+            grad_qkv,
+            grad_out,
+            grad_up,
+            grad_down,
+            grad_first,
+            grad_second,
+            usage,
+        ) = pl.pallas_call(
+            finish_kernel,
+            out_shape=[shape(b16, rows, width), shape(b16, rows, width), shape(f32, 2, width)]
+            + [shape(f32, *dims) for dims in wides]
+            + [shape(f32, 2, NB, hidden), shape(f32, 2, NB)],
+            in_specs=[anywhere] * 7 + [vmem],
+            out_specs=[anywhere] * 2 + [vmem] + [anywhere] * 5 + [vmem] * 2,
+            scratch_shapes=[buffer(b16, rows, width)] * 2
+            + [buffer(b16, *dims) for dims in wides]
+            + [buffer(f32, *dims) for dims in wides]
+            + [pltpu.SemaphoreType.DMA((8,)), pltpu.SemaphoreType.DMA((8,))],
+            compiler_params=pltpu.CompilerParams(vmem_limit_bytes=60 * 2**20),
+        )(block_out, input_grad, raw_qkv, raw_out, raw_up, raw_down, raw_first, sums)
+        grad_qkv = jnp.transpose(grad_qkv, (1, 0, 2))
+        grad_second = jnp.transpose(grad_second, (0, 2, 1))
         return (
             block_out,
             input_grad,

time: 408 us -> 391 us (0.958)
  other arithmetic: 13.6 us -> 0 us
  local copies, waits for them, and re-layouts: 8.61 us -> 0 us
  Pallas kernels: 384 us -> 389 us
    convert_element_type x7 -> x0, other arithmetic: 9.65 us -> none  [the longest x4 7.19 us: shards(): a.astype(wide)]
    pallas_call x0 -> x1, Pallas kernels: none -> 7.81 us  [shards(): pl.pallas_call(finish_kernel, out_shape=[shape(b16, rows, width), shape(b...]
where the time goes in v7:
time: 391 us; the launch traced here: 390 us
  Pallas kernels  389 us (99%)
    pallas_call x1, Pallas kernels, shards(): pl.pallas_call(layer_kernel, out_shape=[shape(b16, rows, width), shape(b1...  381 us

profile of v7, /device:TPU:0, one launch (start us, length us, event | category | flops | bytes accessed | tf_op | source)
XLA Modules:
  0.0 389.7 jit_solution(15912285783628187884)
XLA Ops:
  0.6 381.1 %shard_map.204 = (bf16[256,2048]{1,0:T(8,128)(2,1)}, bf16[256,2048]{1,0:T(8,128)(2,1)}, bf16[3,128,1024]{2,1,0:T(8,128)(2,1)}, bf16[1024,128]{1,0:T(8,128)(2,1)}...) custom-call(bf16[256,2048]{1,0:T(8,128)(2,1)} %tok.1, ...), custom_call_target="tpu_custom_call" | custom-call | tf_op jit(solution)/shard_map/pallas_call | solution.py:1855
  381.7 7.8 %shard_map.205 = (bf16[256,2048]{1,0:T(8,128)(2,1)}, bf16[256,2048]{1,0:T(8,128)(2,1)}, f32[2,2048]{1,0:T(2,128)}, f32[3,128,1024]{2,1,0:T(8,128)}, f32[1024,128...) custom-call(bf16[256,2048]{1,0:T(8,128)(2,1)} %get-tuple-element.28., ...), custom_call_target="tpu_custom_call" | custom-call | tf_op jit(solution)/shard_map/pallas_call | solution.py:1962
